TPU v7x, 256 devices: a whole 4x4x8 slice. The times are simulated.
256 devices in a mesh: tm: 16 (over x, z_hi, core), track: 16 (over z_lo, y).
Axes of the slice: x: 4, y: 4, z: 8 (z_hi: 2, z_lo: 4; z = z_hi * 4 + z_lo), core: 2. Of those that a mesh axis runs over, the one named last changes fastest.
Arguments:
- query_rows: bfloat16 [1024, 2, 16, 1024], P('tm', None, 'track'), may hold values from -10 to 10
- key_rows: bfloat16 [1024, 2, 16, 1024], P('tm', None, 'track'), may hold values from -10 to 10
- value_rows: bfloat16 [1024, 2, 16, 1024], P('tm', None, 'track'), may hold values from -6 to 6
- grad_output: bfloat16 [1024, 2, 16, 1024], P('tm', None, 'track'), may hold values from -6 to 6
- out_weight: bfloat16 [1024, 1024], P(None, 'track'), may hold values from -0.1875 to 0.1875
Outputs:
- grad_query: bfloat16 [1024, 2, 16, 1024], P('tm', None, 'track')
- grad_key: bfloat16 [1024, 2, 16, 1024], P('tm', None, 'track')
- grad_value: bfloat16 [1024, 2, 16, 1024], P('tm', None, 'track')
- grad_weight: float32 [1024, 1024], P(('tm', 'track'))
All inputs are finite; a program needn't handle non-finite values.
Results may differ from a plain program's by a relative error of at most 0.012.
Values may be sent and summed in bfloat16 or wider, within the bound.
No kernel may reach another device: no remote copies, remote signals or barrier semaphores. Data moves between devices by JAX's collectives and lax.ppermute only.
A program may use at most 128 MiB of HBM per device.

v0:
```python
import math

import jax
import jax.numpy as jnp
from jax import lax
from jax.sharding import PartitionSpec as P

HEADS = 8


def normalise(logits, visible):
    logits = jnp.where(visible, logits, -1e30)
    row_peak = jnp.max(logits, axis=-1, keepdims=True)
    weights = jnp.exp(logits - row_peak)
    return weights / jnp.sum(weights, axis=-1, keepdims=True)


def settle(blocks):
    rounded = lax.optimization_barrier(blocks.astype(jnp.bfloat16))
    return jnp.sum(rounded.astype(jnp.float32), axis=0).astype(jnp.bfloat16)


def local(query_rows, key_rows, value_rows, grad_output, out_weight):
    step_rows, score_count, track_local, model_width = query_rows.shape
    seq_count = score_count * track_local
    head_count = HEADS
    head_size = model_width // head_count
    score_scale = head_size ** (-0.5)
    local_shape = (step_rows, score_count, track_local, model_width)
    flat_grad = grad_output.reshape(step_rows * seq_count, model_width)
    attn_grad = lax.dot_general(
        flat_grad,
        lax.all_gather(out_weight, "track", axis=1, tiled=True),
        (((1,), (1,)), ((), ())),
        preferred_element_type=jnp.float32,
    ).astype(jnp.bfloat16)
    attn_grad = attn_grad.reshape(local_shape)
    items_total = seq_count * head_count

    def split_items(array):
        return array.reshape(step_rows, items_total, 1, head_size)

    item_query, item_key, item_value, item_grad = (
        lax.all_to_all(split_items(query_rows), "tm", split_axis=1, concat_axis=0, tiled=True),
        lax.all_to_all(split_items(key_rows), "tm", split_axis=1, concat_axis=0, tiled=True),
        lax.all_to_all(split_items(value_rows), "tm", split_axis=1, concat_axis=0, tiled=True),
        lax.all_to_all(split_items(attn_grad), "tm", split_axis=1, concat_axis=0, tiled=True),
    )
    length = item_query.shape[0]
    item_count = item_query.shape[1]
    query_three = item_query.reshape(length, item_count, head_size)
    key_three = item_key.reshape(length, item_count, head_size)
    value_three = item_value.reshape(length, item_count, head_size)
    grad_three = item_grad.reshape(length, item_count, head_size)
    places = jnp.arange(length)
    visible = places[None, :] <= places[:, None]
    logits = (
        jnp.einsum("qie,kie->iqk", query_three, key_three, preferred_element_type=jnp.float32)
        * score_scale
    )
    probs_full = normalise(logits, visible)
    probs_low = probs_full.astype(jnp.bfloat16)
    attended_items = jnp.einsum(
        "iqk,kie->qie", probs_low, value_three, preferred_element_type=jnp.float32
    ).astype(jnp.bfloat16)
    dprobs = jnp.einsum("qie,kie->iqk", grad_three, value_three, preferred_element_type=jnp.float32)
    row_delta = jnp.sum(probs_full * dprobs, axis=-1, keepdims=True)
    dscores = (probs_full * (dprobs - row_delta) * score_scale).astype(jnp.bfloat16)
    query_grads = jnp.einsum(
        "iqk,kie->qie", dscores, key_three, preferred_element_type=jnp.float32
    ).astype(jnp.bfloat16)
    block_count = length // step_rows
    score_grad_blocks = dscores.reshape(item_count, block_count, step_rows, length)
    probability_blocks = probs_low.reshape(item_count, block_count, step_rows, length)
    query_blocks = query_three.reshape(block_count, step_rows, item_count, head_size)
    grad_blocks = grad_three.reshape(block_count, step_rows, item_count, head_size)
    key_grads = settle(
        jnp.einsum(
            "ibqk,bqie->bkie", score_grad_blocks, query_blocks, preferred_element_type=jnp.float32
        )
    )
    value_grads = settle(
        jnp.einsum(
            "ibqk,bqie->bkie", probability_blocks, grad_blocks, preferred_element_type=jnp.float32
        )
    )

    def back_items(array):
        return array.reshape(length, item_count, 1, head_size)

    returned = (
        lax.all_to_all(back_items(query_grads), "tm", split_axis=0, concat_axis=1, tiled=True),
        lax.all_to_all(back_items(key_grads), "tm", split_axis=0, concat_axis=1, tiled=True),
        lax.all_to_all(back_items(value_grads), "tm", split_axis=0, concat_axis=1, tiled=True),
        lax.all_to_all(back_items(attended_items), "tm", split_axis=0, concat_axis=1, tiled=True),
    )
    grad_query, grad_key, grad_value, attended = [array.reshape(local_shape) for array in returned]
    total_tokens = step_rows * lax.axis_size("tm") * seq_count * lax.axis_size("track")
    norm_factor = 1.0 / math.sqrt(total_tokens)
    attended_flat = attended.reshape(step_rows * seq_count, model_width)
    grad_weight = lax.psum_scatter(
        lax.dot_general(
            attended_flat, flat_grad, (((0,), (0,)), ((), ())), preferred_element_type=jnp.float32
        )
        * norm_factor,
        ("tm", "track"),
        scatter_dimension=0,
        tiled=True,
    )
    return (grad_query, grad_key, grad_value, grad_weight)


def solution(mesh):
    return jax.shard_map(
        local,
        mesh=mesh,
        in_specs=(
            P("tm", None, "track", None),
            P("tm", None, "track", None),
            P("tm", None, "track", None),
            P("tm", None, "track", None),
            P(None, "track"),
        ),
        out_specs=(
            P("tm", None, "track", None),
            P("tm", None, "track", None),
            P("tm", None, "track", None),
            P(("tm", "track"), None),
        ),
        check_vma=False,
    )
```

profile of v0, /device:TPU:48, one launch (start us, length us, event | category | flops | bytes accessed | tf_op | source)
XLA Modules:
  0.0 429.0 jit_solution(2694740185769021518)
XLA Ops:
  7.9 1.1 reshape.139
  9.8 10.1 %all-to-all-start = ((bf16[64,16,1,128]{3,0,2,1:T(8,128)(2,1)}), bf16[64,16,1,128]{3,0,2,1:T(8,128)(2,1)S(1)}, u32[]{:S(2)}, u32[]{:S(2)}) async-start(bf16[64,16,1,128]{3,0,2,1:T(8,128)(2,1)} %copy.51), calls=%async_computation | async-start | bytes 524288 | tf_op jit(solution)/shard_map/all_to_all | solution.py:44
  19.9 1.1 reshape.141
  21.8 12.9 %all-to-all-done = bf16[64,16,1,128]{3,0,2,1:T(8,128)(2,1)S(1)} async-done(((bf16[64,16,1,128]{3,0,2,1:T(8,128)(2,1)}), bf16[64,16,1,128]{3,0,2,1:T(8,128)(2,1)S(1)}, u32[]{:S(2)}, u32[]{:S(2)}) %all-to-all-start) | async-done | bytes 262176 | tf_op jit(solution)/shard_map/all_to_all | solution.py:44
  34.7 3.5 all-to-all-start.1
  38.3 1.1 reshape.145
  40.1 11.0 %all-to-all-done.1 = bf16[64,16,1,128]{3,0,2,1:T(8,128)(2,1)S(1)} async-done(((bf16[64,16,1,128]{3,0,2,1:T(8,128)(2,1)}), bf16[64,16,1,128]{3,0,2,1:T(8,128)(2,1)S(1)}, u32[]{:S(2)}, u32[]{:S(2)}) %all-to-all-start.1) | async-done | bytes 262176 | tf_op jit(solution)/shard_map/all_to_all | solution.py:45
  51.2 3.5 all-to-all-start.3
  54.8 33.0 %all-gather.2.cloned.1.call-done = bf16[1024,1024]{0,1:T(8,128)(2,1)} async-done(((bf16[1024,64]{0,1:T(8,128)(2,1)}), bf16[1024,1024]{0,1:T(8,128)(2,1)}) %all-gather.2.cloned.1.call-update) | async-done | bytes 2097168 | tf_op jit(solution)/shard_map/all_gather | solution.py:33
  87.8 2.0 convolution_convert_fusion.2
  90.8 7.7 %all-to-all-start.2 = ((bf16[64,16,1,128]{3,0,2,1:T(8,128)(2,1)}), bf16[64,16,1,128]{3,0,2,1:T(8,128)(2,1)S(1)}, u32[]{:S(2)}, u32[]{:S(2)}) async-start(bf16[64,16,1,128]{3,0,2,1:T(8,128)(2,1)} %copy.53), calls=%async_computation.2 | async-start | bytes 524288 | tf_op jit(solution)/shard_map/all_to_all | solution.py:47
  99.3 1.9 copy-done.1
  102.0 8.6 %all-to-all-done.2 = bf16[64,16,1,128]{3,0,2,1:T(8,128)(2,1)S(1)} async-done(((bf16[64,16,1,128]{3,0,2,1:T(8,128)(2,1)}), bf16[64,16,1,128]{3,0,2,1:T(8,128)(2,1)S(1)}, u32[]{:S(2)}, u32[]{:S(2)}) %all-to-all-start.2) | async-done | bytes 262176 | tf_op jit(solution)/shard_map/all_to_all | solution.py:47
  110.5 4.1 multiply_reduce_fusion
  114.7 1.9 fusion.7
  116.6 1.4 copy-done
  120.0 15.3 %all_to_all.120 = bf16[16,2,4096]{2,1,0:T(2,128)(2,1)} all-to-all(bf16[16,2,4096]{2,1,0:T(2,128)(2,1)S(1)} %reshape.164), channel_id=1, replica_groups=mesh['tm'=16,'track'=16] {'tm'}, dimensions={0} | all-to-all | bytes 524288 | tf_op jit(solution)/shard_map/all_to_all | solution.py:95
  135.4 2.2 reshape.165
  137.9 2.7 convolution_multiply_fusion
  140.6 4.9 %convert_bitcast_fusion = bf16[16,1024,1,128]{1,3,0,2:T(8,128)(2,1)} fusion(bf16[16,64,1024]{2,1,0:T(8,128)(2,1)} %bitcast.112, bf16[64,16,1,128]{3,0,2,1:T(8,128)(2,1)S(1)} %copy-done.4), kind=kOutput, calls=%fused_computation | convolution fusion | flops 270532608 | bytes 6553600 | tf_op jit(solution)/shard_map/ibqk,bqie->bkie/dot_general | solution.py:83
  145.5 3.1 reduce_sum.45
  150.4 3.7 all-to-all-start.6
  154.1 3.3 convert_bitcast_fusion.1
  157.4 3.1 reduce_sum.44
  162.1 3.9 all-to-all-done.6
  166.0 5.3 %all-to-all-start.5 = ((bf16[16,2,4096]{2,1,0:T(2,128)(2,1)}), bf16[16,2,4096]{2,1,0:T(2,128)(2,1)S(1)}, u32[]{:S(2)}, u32[]{:S(2)}) async-start(bf16[16,2,4096]{2,1,0:T(2,128)(2,1)} %reshape.160), calls=%async_computation.5 | async-start | bytes 524288 | tf_op jit(solution)/shard_map/all_to_all | solution.py:93
  172.0 0.8 reduce.10
  173.6 10.7 %all-to-all-done.5 = bf16[16,2,4096]{2,1,0:T(2,128)(2,1)S(1)} async-done(((bf16[16,2,4096]{2,1,0:T(2,128)(2,1)}), bf16[16,2,4096]{2,1,0:T(2,128)(2,1)S(1)}, u32[]{:S(2)}, u32[]{:S(2)}) %all-to-all-start.5) | async-done | bytes 262176 | tf_op jit(solution)/shard_map/all_to_all | solution.py:93
  184.2 3.5 all-to-all-start.4
  190.3 9.8 %all-to-all-done.4 = bf16[16,2,4096]{2,1,0:T(2,128)(2,1)S(1)} async-done(((bf16[16,2,4096]{2,1,0:T(2,128)(2,1)}), bf16[16,2,4096]{2,1,0:T(2,128)(2,1)S(1)}, u32[]{:S(2)}, u32[]{:S(2)}) %all-to-all-start.4) | async-done | bytes 262176 | tf_op jit(solution)/shard_map/all_to_all | solution.py:92
  201.5 219.3 %all-reduce.3.cloned.1.call-done = f32[1024,1024]{1,0:T(8,128)} async-done(((f32[1024,1024]{1,0:T(8,128)}), f32[1024,1024]{1,0:T(8,128)}) %all-reduce.3.cloned.1.call-update) | async-done | bytes 4194320
  420.8 1.4 constant_dynamic-slice_fusion
  (49 shorter events, 16.6 us)
Async XLA Ops:
  7.2 47.6 %copy-start.5 = (bf16[64,2,1,1024]{3,1,2,0:T(2,128)(2,1)S(1)}, bf16[64,2,1,1024]{3,1,2,0:T(2,128)(2,1)}, u32[]{:S(2)}) copy-start(bf16[64,2,1,1024]{3,1,2,0:T(2,128)(2,1)} %param.8) | copy-start | bytes 786436
  7.2 80.6 %all-gather.2.cloned.1.call-start = ((), (), s32[]{:S(2)}) async-start(), calls=%async_computation.8 | async-start | bytes 2228224 | tf_op jit(solution)/shard_map/all_gather | solution.py:33
  9.8 24.9 %all-to-all-start = ((bf16[64,16,1,128]{3,0,2,1:T(8,128)(2,1)}), bf16[64,16,1,128]{3,0,2,1:T(8,128)(2,1)S(1)}, u32[]{:S(2)}, u32[]{:S(2)}) async-start(bf16[64,16,1,128]{3,0,2,1:T(8,128)(2,1)} %copy.51), calls=%async_computation | async-start | bytes 524288 | tf_op jit(solution)/shard_map/all_to_all | solution.py:44
  34.7 16.5 %all-to-all-start.1 = ((bf16[64,16,1,128]{3,0,2,1:T(8,128)(2,1)}), bf16[64,16,1,128]{3,0,2,1:T(8,128)(2,1)S(1)}, u32[]{:S(2)}, u32[]{:S(2)}) async-start(bf16[64,16,1,128]{3,0,2,1:T(8,128)(2,1)} %copy.52), calls=%async_computation.1 | async-start | bytes 524288 | tf_op jit(solution)/shard_map/all_to_all | solution.py:45
  51.2 39.6 %all-to-all-start.3 = ((bf16[64,16,1,128]{3,0,2,1:T(8,128)(2,1)}), bf16[64,16,1,128]{3,0,2,1:T(8,128)(2,1)S(1)}, u32[]{:S(2)}, u32[]{:S(2)}) async-start(bf16[64,16,1,128]{3,0,2,1:T(8,128)(2,1)} %copy.54), calls=%async_computation.3 | async-start | bytes 524288 | tf_op jit(solution)/shard_map/all_to_all | solution.py:46
  90.8 19.8 %all-to-all-start.2 = ((bf16[64,16,1,128]{3,0,2,1:T(8,128)(2,1)}), bf16[64,16,1,128]{3,0,2,1:T(8,128)(2,1)S(1)}, u32[]{:S(2)}, u32[]{:S(2)}) async-start(bf16[64,16,1,128]{3,0,2,1:T(8,128)(2,1)} %copy.53), calls=%async_computation.2 | async-start | bytes 524288 | tf_op jit(solution)/shard_map/all_to_all | solution.py:47
  98.5 322.3 %all-reduce.3.cloned.1.call-start = ((), (), s32[]{:S(2)}) async-start(), calls=%async_computation.9 | async-start | bytes 8388608
  99.3 1.9 copy-start.1
  110.5 4.2 copy-start.3
  110.5 4.2 copy-start.2
  116.6 1.4 copy-start
  137.9 2.7 copy-start.4
  150.4 15.6 %all-to-all-start.6 = ((bf16[16,2,4096]{2,1,0:T(2,128)(2,1)}), bf16[16,2,4096]{2,1,0:T(2,128)(2,1)S(1)}, u32[]{:S(2)}, u32[]{:S(2)}) async-start(bf16[16,2,4096]{2,1,0:T(2,128)(2,1)} %reshape.162), calls=%async_computation.6 | async-start | bytes 524288 | tf_op jit(solution)/shard_map/all_to_all | solution.py:94
  166.0 18.3 %all-to-all-start.5 = ((bf16[16,2,4096]{2,1,0:T(2,128)(2,1)}), bf16[16,2,4096]{2,1,0:T(2,128)(2,1)S(1)}, u32[]{:S(2)}, u32[]{:S(2)}) async-start(bf16[16,2,4096]{2,1,0:T(2,128)(2,1)} %reshape.160), calls=%async_computation.5 | async-start | bytes 524288 | tf_op jit(solution)/shard_map/all_to_all | solution.py:93
  184.2 16.0 %all-to-all-start.4 = ((bf16[16,2,4096]{2,1,0:T(2,128)(2,1)}), bf16[16,2,4096]{2,1,0:T(2,128)(2,1)S(1)}, u32[]{:S(2)}, u32[]{:S(2)}) async-start(bf16[16,2,4096]{2,1,0:T(2,128)(2,1)} %reshape.158), calls=%async_computation.4 | async-start | bytes 524288 | tf_op jit(solution)/shard_map/all_to_all | solution.py:92
Sparse Core Ops, SparseCore 0:
  9.8 77.9 all-gather.1
  140.7 279.9 all-reduce.2
where the time goes:
time: 433 us; the launch traced here: 429 us
  waiting for transfers between devices  310 us (72%)
  starting transfers between devices  37.5 us (9%)
  local copies, waits for them, and re-layouts  20.6 us (5%)
  matrix products  19.3 us (4%)
  blocking collectives  15.3 us (4%)
  between operations  14.4 us (3%)
  other arithmetic  12 us (3%)
    unnamed x3, waiting for transfers between devices  220 us
    all_gather x1, waiting for transfers between devices, local(): lax.all_gather(out_weight, 'track', axis=1, tiled=True)  33 us
    all_to_all x1, blocking collectives, local(): lax.all_to_all(back_items(attended_items), 'tm', split_axis=0, concat_axi...  15.3 us
    all_to_all x1, waiting for transfers between devices, local(): lax.all_to_all(split_items(query_rows), 'tm', split_axis=1, concat_axis=0...  12.9 us
    all_to_all x1, waiting for transfers between devices, local(): lax.all_to_all(split_items(key_rows), 'tm', split_axis=1, concat_axis=0,...  11 us
    all_to_all x1, waiting for transfers between devices, local(): lax.all_to_all(back_items(key_grads), 'tm', split_axis=0, concat_axis=1,...  10.7 us
    unnamed x26, local copies, waits for them, and re-layouts  10.3 us
    all_to_all x1, starting transfers between devices, local(): lax.all_to_all(split_items(query_rows), 'tm', split_axis=1, concat_axis=0...  10.1 us
  transfers between devices with their start and end apart: 9, of which 8 were waited for; matrix products, arithmetic and copies ran while one was open for 8% of the time, Pallas kernels for 0%

commit v1 on v0

v1 whole, which is shorter than its diff:
```python
import functools
import math

import jax
import jax.numpy as jnp
from jax import lax
from jax.experimental import pallas as pl
from jax.experimental.pallas import tpu as pltpu
from jax.sharding import PartitionSpec as P

HEADS = 8
HEAD = 128
BLOCK = 64
ROWS = 256


def dot(a, b, ca, cb):
    return lax.dot_general(
        a, b, (((ca,), (cb,)), ((), ())), preferred_element_type=jnp.float32
    )


def attention_kernel(
    n_tm, norm_factor, where_ref, qkv_ref, *refs
):
    piece_refs, weight_refs = refs[:8], refs[8:13]
    grads_ref, keep_ref, send_ref = refs[13:16]
    w_ref, do_ref, att_ref, gk_ref, gv_ref, gw_ref = refs[16:]
    length = n_tm * BLOCK
    x, z, core, track = where_ref[0], where_ref[1], where_ref[2], where_ref[3]

    chunk = w_ref.shape[0] // 16
    position = 0
    for ref in weight_refs:
        for j in range(ref.shape[0] // chunk):
            reverse = int(format(position, "04b")[::-1], 2)
            owner = track ^ reverse
            w_ref[pl.ds(pl.multiple_of(owner * chunk, chunk), chunk), :] = ref[
                j * chunk : (j + 1) * chunk, :
            ]
            position += 1

    def block_rows(piece, sub):
        dz, d = piece // 4, piece % 4
        block = 4 * ((x + 4 - d) % 4) + 2 * (z ^ dz) + (core ^ sub)
        return pl.ds(pl.multiple_of(block * BLOCK, BLOCK), BLOCK)

    for piece in range(8):
        part = dot(piece_refs[piece][...], w_ref[...], 1, 0).astype(jnp.bfloat16)
        do_ref[block_rows(piece, 0), :] = part[:BLOCK]
        do_ref[block_rows(piece, 1), :] = part[BLOCK:]

    scale = HEAD ** (-0.5)
    steps = ROWS // BLOCK
    for i in range(length // ROWS):
        width = (i + 1) * ROWS
        rows = slice(i * ROWS, (i + 1) * ROWS)
        blocks = slice(i * steps, (i + 1) * steps)
        q = qkv_ref[blocks, 0].reshape(ROWS, HEAD)
        k = qkv_ref[: (i + 1) * steps, 1].reshape(width, HEAD)
        v = qkv_ref[: (i + 1) * steps, 2].reshape(width, HEAD)
        do = do_ref[rows, :]
        s = dot(q, k, 1, 1) * scale
        row_at = lax.broadcasted_iota(jnp.int32, s.shape, 0) + i * ROWS
        col_at = lax.broadcasted_iota(jnp.int32, s.shape, 1)
        s = jnp.where(col_at <= row_at, s, -1e30)
        peak = jnp.max(s, axis=1, keepdims=True)
        e = jnp.exp(s - peak)
        p = e / jnp.sum(e, axis=1, keepdims=True)
        p_low = p.astype(jnp.bfloat16)
        att_ref[rows, :] = dot(p_low, v, 1, 0).astype(jnp.bfloat16)
        dp = dot(do, v, 1, 1)
        delta = jnp.sum(p * dp, axis=1, keepdims=True)
        ds = (p * (dp - delta) * scale).astype(jnp.bfloat16)
        gq = dot(ds, k, 1, 0).astype(jnp.bfloat16)
        grads_ref[blocks, 0] = gq.reshape(steps, BLOCK, HEAD)
        gk = dot(q, ds, 0, 0)
        gv = dot(do, p_low, 0, 0)
        if i:
            gk_ref[:, : width - ROWS] += gk[:, : width - ROWS]
            gv_ref[:, : width - ROWS] += gv[:, : width - ROWS]
            gk, gv = gk[:, width - ROWS :], gv[:, width - ROWS :]
        gk_ref[:, rows] = gk
        gv_ref[:, rows] = gv
    grads_ref[:, 1] = gk_ref[...].T.astype(jnp.bfloat16).reshape(n_tm, BLOCK, HEAD)
    grads_ref[:, 2] = gv_ref[...].T.astype(jnp.bfloat16).reshape(n_tm, BLOCK, HEAD)

    for piece in range(8):
        att = jnp.concatenate(
            [att_ref[block_rows(piece, 0), :], att_ref[block_rows(piece, 1), :]], axis=0
        )
        term = dot(att, piece_refs[piece][...], 0, 0)
        if piece == 0:
            gw_ref[...] = term
        else:
            gw_ref[...] += term
    half = HEAD // 2
    keep_ref[...] = gw_ref[pl.ds(pl.multiple_of(core * half, half), half), :] * norm_factor
    send_ref[...] = gw_ref[pl.ds(pl.multiple_of((1 - core) * half, half), half), :] * norm_factor


def attention(where, qkv, pieces, weights, n_tm, norm_factor):
    width = pieces[0].shape[1]
    length = n_tm * BLOCK
    vmem = pl.BlockSpec(memory_space=pltpu.VMEM)
    return pl.pallas_call(
        functools.partial(attention_kernel, n_tm, norm_factor),
        out_shape=(
            jax.ShapeDtypeStruct((n_tm, 3, BLOCK, HEAD), jnp.bfloat16),
            jax.ShapeDtypeStruct((HEAD // 2, width), jnp.float32),
            jax.ShapeDtypeStruct((HEAD // 2, width), jnp.float32),
        ),
        in_specs=[pl.BlockSpec(memory_space=pltpu.SMEM)] + [vmem] * (1 + len(pieces) + len(weights)),
        out_specs=(vmem, vmem, vmem),
        scratch_shapes=[
            pltpu.VMEM((width, HEAD), jnp.bfloat16),
            pltpu.VMEM((length, HEAD), jnp.bfloat16),
            pltpu.VMEM((length, HEAD), jnp.bfloat16),
            pltpu.VMEM((HEAD, length), jnp.float32),
            pltpu.VMEM((HEAD, length), jnp.float32),
            pltpu.VMEM((HEAD, width), jnp.float32),
        ],
        compiler_params=pltpu.CompilerParams(vmem_limit_bytes=48 * 1024 * 1024),
        cost_estimate=pl.CostEstimate(
            flops=2 * 6 * length * length * HEAD, bytes_accessed=4 << 20, transcendentals=length * length
        ),
        name="attention_backward",
    )(where, qkv, *pieces, *weights)


def swap(array, axis, mask):
    return lax.ppermute(array, axis, [(i, i ^ mask) for i in range(16)])


def local(query_rows, key_rows, value_rows, grad_output, out_weight):
    step_rows, score_count, track_local, model_width = query_rows.shape
    n_tm = lax.axis_size("tm")
    total_tokens = step_rows * n_tm * score_count * track_local * lax.axis_size("track")
    norm_factor = 1.0 / math.sqrt(total_tokens)
    tm = lax.axis_index("tm")
    track = lax.axis_index("track")
    x, z, core = tm // 4, (tm // 2) % 2, tm % 2
    head = tm // 2

    grads = grad_output.reshape(step_rows, score_count, model_width)
    first, second = grads[:, 0], grads[:, 1]
    mine = jnp.where(core == 0, first, second)
    other = jnp.where(core == 0, second, first)
    chip_piece = jnp.concatenate([mine, swap(other, "tm", 1)], axis=0)
    pieces = []
    for piece in (chip_piece, swap(chip_piece, "tm", 2)):
        pieces.append(piece)
        for d in (1, 2, 3):
            pieces.append(lax.ppermute(piece, "tm", [(i, (i + 4 * d) % 16) for i in range(16)]))

    held = lax.dynamic_slice_in_dim(out_weight.T, head * HEAD, HEAD, axis=1)
    weights = [held]
    for mask in (8, 4, 2, 1):
        got = swap(held, "track", mask)
        weights.append(got)
        held = jnp.concatenate([held, got], axis=0)

    qkv = jnp.stack([query_rows, key_rows, value_rows]).reshape(
        3, step_rows, score_count, HEADS, HEAD
    )
    qkv = qkv.transpose(3, 2, 0, 1, 4).reshape(n_tm, 3, step_rows, HEAD)
    qkv = lax.all_to_all(qkv, "tm", split_axis=0, concat_axis=0, tiled=True)

    where = jnp.stack([x, z, core, track]).astype(jnp.int32)
    item_grads, keep, send = attention(where, qkv, pieces, weights, n_tm, norm_factor)

    total = keep + swap(send, "tm", 1)
    total = total.reshape(2, 2, 2, 2, 4, model_width)
    for axis, mask in ((3, 1), (2, 2), (1, 4), (0, 8)):
        bit = (track & mask) != 0
        low = lax.index_in_dim(total, 0, axis, keepdims=True)
        high = lax.index_in_dim(total, 1, axis, keepdims=True)
        got = swap(jnp.where(bit, low, high), "track", mask)
        total = jnp.where(bit, high, low) + got
    grad_weight = total.reshape(4, model_width)

    returned = lax.all_to_all(item_grads, "tm", split_axis=0, concat_axis=0, tiled=True)
    returned = returned.reshape(HEADS, score_count, 3, step_rows, HEAD).transpose(2, 3, 1, 0, 4)
    returned = returned.reshape(3, step_rows, score_count, track_local, model_width)
    return (returned[0], returned[1], returned[2], grad_weight)


def solution(mesh):
    return jax.shard_map(
        local,
        mesh=mesh,
        in_specs=(
            P("tm", None, "track", None),
            P("tm", None, "track", None),
            P("tm", None, "track", None),
            P("tm", None, "track", None),
            P(None, "track"),
        ),
        out_specs=(
            P("tm", None, "track", None),
            P("tm", None, "track", None),
            P("tm", None, "track", None),
            P(("tm", "track"), None),
        ),
        check_vma=False,
    )
```

time: 433 us -> 120 us (0.28)
  waiting for transfers between devices: 310 us -> 55.9 us
  matrix products: 19.3 us -> 0 us
  blocking collectives: 15.3 us -> 0 us
  local copies, waits for them, and re-layouts: 20.6 us -> 6.47 us
  between operations: 14.4 us -> 0.87 us
  other arithmetic: 12 us -> 1.93 us
  starting transfers between devices: 37.5 us -> 46.8 us
  Pallas kernels: 0 us -> 6.37 us
    unnamed x3 -> x0, waiting for transfers between devices: 220 us -> none
    all_to_all x7 -> x2, waiting for transfers between devices: 56.8 us -> 1.83 us  [the longest x1 1.83 us: local(): lax.all_to_all(item_grads, 'tm', split_axis=0, concat_axis=0, tiled=True)]
    ppermute x0 -> x17, waiting for transfers between devices: none -> 54.1 us  [the longest x11 43.9 us: swap(): return lax.ppermute(array, axis, [(i, i ^ mask) for i in range(16)])]
    all_gather x1 -> x0, waiting for transfers between devices: 33 us -> none  [local(): lax.all_gather(out_weight, 'track', axis=1, tiled=True)]
    ppermute x0 -> x17, starting transfers between devices: none -> 30.9 us  [the longest x11 19 us: swap(): return lax.ppermute(array, axis, [(i, i ^ mask) for i in range(16)])]
    all_to_all x7 -> x2, starting transfers between devices: 37.5 us -> 15.9 us  [the longest x1 10.3 us: local(): qkv = lax.all_to_all(qkv, 'tm', split_axis=0, concat_axis=0, tiled=True)]
    dot_general x8 -> x0, matrix products: 19.3 us -> none  [the longest x1 4.86 us: local(): jnp.einsum('ibqk,bqie->bkie', probability_blocks, grad_blocks, preferred_...]
    all_to_all x1 -> x0, blocking collectives: 15.3 us -> none  [local(): lax.all_to_all(back_items(attended_items), 'tm', split_axis=0, concat_axi...]
  transfers between devices with their start and end apart: 9 -> 19, of which waited for: 8 -> 10; matrix products, arithmetic and copies ran while one was open for 8% -> 1% of each run, Pallas kernels for 0% -> 0%
where the time goes in v1:
time: 120 us; the launch traced here: 118 us
  waiting for transfers between devices  55.9 us (47%)
  starting transfers between devices  46.8 us (39%)
  local copies, waits for them, and re-layouts  6.47 us (5%)
  Pallas kernels  6.37 us (5%)
  other arithmetic  1.93 us (2%)
    ppermute x11, waiting for transfers between devices, swap(): return lax.ppermute(array, axis, [(i, i ^ mask) for i in range(16)])  43.9 us
    ppermute x11, starting transfers between devices, swap(): return lax.ppermute(array, axis, [(i, i ^ mask) for i in range(16)])  19 us
    ppermute x6, starting transfers between devices, local(): lax.ppermute(piece, 'tm', [(i, (i + 4 * d) % 16) for i in range(16)])  11.9 us
    all_to_all x1, starting transfers between devices, local(): qkv = lax.all_to_all(qkv, 'tm', split_axis=0, concat_axis=0, tiled=True)  10.3 us
    ppermute x6, waiting for transfers between devices, local(): lax.ppermute(piece, 'tm', [(i, (i + 4 * d) % 16) for i in range(16)])  10.1 us
    pallas_call x1, Pallas kernels, attention(): pl.pallas_call(functools.partial(attention_kernel, n_tm, norm_factor), ou...  6.37 us
    all_to_all x1, starting transfers between devices, local(): lax.all_to_all(item_grads, 'tm', split_axis=0, concat_axis=0, tiled=True)  5.64 us
  transfers between devices with their start and end apart: 19, of which 10 were waited for; matrix products, arithmetic and copies ran while one was open for 1% of the time, Pallas kernels for 0%

profile of v1, /device:TPU:48, one launch (start us, length us, event | category | flops | bytes accessed | tf_op | source)
XLA Modules:
  0.0 118.3 jit_solution(17714871485348672328)
XLA Ops:
  0.6 1.2 stack.33
  1.9 0.9 copy-done.1
  3.0 0.9 copy-done.2
  4.1 1.0 pad_maximum_fusion
  5.1 10.3 %all-to-all-start = ((bf16[16,3,64,128]{3,2,1,0:T(8,128)(2,1)}), bf16[16,3,64,128]{3,2,1,0:T(8,128)(2,1)S(1)}, u32[]{:S(2)}, u32[]{:S(2)}) async-start(bf16[16,3,64,128]{3,2,1,0:T(8,128)(2,1)} %bitcast.5), calls=%async_computation | async-start | bytes 1572864 | tf_op jit(solution)/shard_map/all_to_all | solution.py:167
  15.4 1.6 %collective-permute-start.8 = (bf16[64,128]{1,0:T(8,128)(2,1)S(1)}, bf16[64,128]{1,0:T(8,128)(2,1)S(1)}, u32[]{:S(2)}, u32[]{:S(2)}) collective-permute-start(bf16[64,128]{1,0:T(8,128)(2,1)S(1)} %dynamic-slice_bitcast_fusion.refs_8_), channel_id=1, source_target_pairs={{0,8},{1,9},{2,10},{3,11},{4,12},{5,13},{6,14},{7,15},{8,0},{9,1},... | collective-permute-start | bytes 49160 | tf_op jit(solution)/shard_map/ppermute | solution.py:132
  17.1 12.3 %collective-permute-done.8.refs_9_ = bf16[64,128]{1,0:T(8,128)(2,1)S(1)} collective-permute-done((bf16[64,128]{1,0:T(8,128)(2,1)S(1)}, bf16[64,128]{1,0:T(8,128)(2,1)S(1)}, u32[]{:S(2)}, u32[]{:S(2)}) %collective-permute-start.8) | collective-permute-done | bytes 16416 | tf_op jit(solution)/shard_map/ppermute | solution.py:132
  29.4 1.7 %collective-permute-start.9 = (bf16[128,128]{1,0:T(8,128)(2,1)S(1)}, bf16[128,128]{1,0:T(8,128)(2,1)S(1)}, u32[]{:S(2)}, u32[]{:S(2)}) collective-permute-start(bf16[128,128]{1,0:T(8,128)(2,1)S(1)} %pad_maximum_fusion.4), channel_id=1, source_target_pairs={{0,4},{1,5},{2,6},{3,7},{4,0},{5,1},{6,2},{7,3},{8,12},{9,13},{10,... | collective-permute-start | bytes 98312 | tf_op jit(solution)/shard_map/ppermute | solution.py:132
  31.2 7.8 %collective-permute-done.9.refs_10_ = bf16[128,128]{1,0:T(8,128)(2,1)S(1)} collective-permute-done((bf16[128,128]{1,0:T(8,128)(2,1)S(1)}, bf16[128,128]{1,0:T(8,128)(2,1)S(1)}, u32[]{:S(2)}, u32[]{:S(2)}) %collective-permute-start.9) | collective-permute-done | bytes 32800 | tf_op jit(solution)/shard_map/ppermute | solution.py:132
  39.4 5.2 %collective-permute-start.4 = (bf16[128,1024]{1,0:T(8,128)(2,1)S(1)}, bf16[128,1024]{1,0:T(8,128)(2,1)S(1)}, u32[]{:S(2)}, u32[]{:S(2)}) collective-permute-start(bf16[128,1024]{1,0:T(8,128)(2,1)S(1)} %pad_maximum_fusion.1.refs_0_), channel_id=1, source_target_pairs={{0,32},{16,48},{32,0},{48,16},{64,96},{80,112},{96,64},{112,80},{1... | collective-permute-start | bytes 786440 | tf_op jit(solution)/shard_map/ppermute | solution.py:132
  44.6 1.2 %collective-permute-start.1 = (bf16[128,1024]{1,0:T(8,128)(2,1)S(1)}, bf16[128,1024]{1,0:T(8,128)(2,1)S(1)}, u32[]{:S(2)}, u32[]{:S(2)}) collective-permute-start(bf16[128,1024]{1,0:T(8,128)(2,1)S(1)} %pad_maximum_fusion.1.refs_0_), channel_id=1, source_target_pairs={{0,64},{16,80},{32,96},{48,112},{64,128},{80,144},{96,160},{112,17... | collective-permute-start | bytes 786440 | tf_op jit(solution)/shard_map/ppermute | solution.py:154
  45.9 2.3 %collective-permute-start.11 = (bf16[512,128]{1,0:T(8,128)(2,1)S(1)}, bf16[512,128]{1,0:T(8,128)(2,1)S(1)}, u32[]{:S(2)}, u32[]{:S(2)}) collective-permute-start(bf16[512,128]{1,0:T(8,128)(2,1)S(1)} %pad_maximum_fusion.2), channel_id=1, source_target_pairs={{0,1},{1,0},{2,3},{3,2},{4,5},{5,4},{6,7},{7,6},{8,9},{9,8},{10,11... | collective-permute-start | bytes 393224 | tf_op jit(solution)/shard_map/ppermute | solution.py:132
  48.1 2.7 %collective-permute-start.2 = (bf16[128,1024]{1,0:T(8,128)(2,1)S(1)}, bf16[128,1024]{1,0:T(8,128)(2,1)S(1)}, u32[]{:S(2)}, u32[]{:S(2)}) collective-permute-start(bf16[128,1024]{1,0:T(8,128)(2,1)S(1)} %pad_maximum_fusion.1.refs_0_), channel_id=1, source_target_pairs={{0,128},{16,144},{32,160},{48,176},{64,192},{80,208},{96,224},{112... | collective-permute-start | bytes 786440 | tf_op jit(solution)/shard_map/ppermute | solution.py:154
  50.8 1.5 %collective-permute-start.3 = (bf16[128,1024]{1,0:T(8,128)(2,1)S(1)}, bf16[128,1024]{1,0:T(8,128)(2,1)S(1)}, u32[]{:S(2)}, u32[]{:S(2)}) collective-permute-start(bf16[128,1024]{1,0:T(8,128)(2,1)S(1)} %pad_maximum_fusion.1.refs_0_), channel_id=1, source_target_pairs={{0,192},{16,208},{32,224},{48,240},{64,0},{80,16},{96,32},{112,48}... | collective-permute-start | bytes 786440 | tf_op jit(solution)/shard_map/ppermute | solution.py:154
  52.3 3.8 %collective-permute-done.4.refs_4_ = bf16[128,1024]{1,0:T(8,128)(2,1)S(1)} collective-permute-done((bf16[128,1024]{1,0:T(8,128)(2,1)S(1)}, bf16[128,1024]{1,0:T(8,128)(2,1)S(1)}, u32[]{:S(2)}, u32[]{:S(2)}) %collective-permute-start.4) | collective-permute-done | bytes 262176 | tf_op jit(solution)/shard_map/ppermute | solution.py:132
  56.0 2.4 %collective-permute-start.5 = (bf16[128,1024]{1,0:T(8,128)(2,1)S(1)}, bf16[128,1024]{1,0:T(8,128)(2,1)S(1)}, u32[]{:S(2)}, u32[]{:S(2)}) collective-permute-start(bf16[128,1024]{1,0:T(8,128)(2,1)S(1)} %collective-permute-done.4.refs_4_), channel_id=1, source_target_pairs={{0,64},{16,80},{32,96},{48,112},{64,128},{80,144},{96,160},{112,17... | collective-permute-start | bytes 786440 | tf_op jit(solution)/shard_map/ppermute | solution.py:154
  58.5 2.7 %collective-permute-start.6 = (bf16[128,1024]{1,0:T(8,128)(2,1)S(1)}, bf16[128,1024]{1,0:T(8,128)(2,1)S(1)}, u32[]{:S(2)}, u32[]{:S(2)}) collective-permute-start(bf16[128,1024]{1,0:T(8,128)(2,1)S(1)} %collective-permute-done.4.refs_4_), channel_id=1, source_target_pairs={{0,128},{16,144},{32,160},{48,176},{64,192},{80,208},{96,224},{112... | collective-permute-start | bytes 786440 | tf_op jit(solution)/shard_map/ppermute | solution.py:154
  61.1 1.5 %collective-permute-start.7 = (bf16[128,1024]{1,0:T(8,128)(2,1)S(1)}, bf16[128,1024]{1,0:T(8,128)(2,1)S(1)}, u32[]{:S(2)}, u32[]{:S(2)}) collective-permute-start(bf16[128,1024]{1,0:T(8,128)(2,1)S(1)} %collective-permute-done.4.refs_4_), channel_id=1, source_target_pairs={{0,192},{16,208},{32,224},{48,240},{64,0},{80,16},{96,32},{112,48}... | collective-permute-start | bytes 786440 | tf_op jit(solution)/shard_map/ppermute | solution.py:154
  62.7 3.3 %collective-permute-done.5.refs_5_ = bf16[128,1024]{1,0:T(8,128)(2,1)S(1)} collective-permute-done((bf16[128,1024]{1,0:T(8,128)(2,1)S(1)}, bf16[128,1024]{1,0:T(8,128)(2,1)S(1)}, u32[]{:S(2)}, u32[]{:S(2)}) %collective-permute-start.5) | collective-permute-done | bytes 262176 | tf_op jit(solution)/shard_map/ppermute | solution.py:154
  66.0 6.8 %collective-permute-done.6.refs_6_ = bf16[128,1024]{1,0:T(8,128)(2,1)S(1)} collective-permute-done((bf16[128,1024]{1,0:T(8,128)(2,1)S(1)}, bf16[128,1024]{1,0:T(8,128)(2,1)S(1)}, u32[]{:S(2)}, u32[]{:S(2)}) %collective-permute-start.6) | collective-permute-done | bytes 262176 | tf_op jit(solution)/shard_map/ppermute | solution.py:154
  72.8 6.4 %attention_backward.1 = (bf16[16,3,64,128]{3,2,1,0:T(8,128)(2,1)}, f32[64,1024]{1,0:T(8,128)S(1)}, f32[64,1024]{1,0:T(8,128)}) custom-call(s32[4]{0:T(128)S(1)} %pad_add_fusion.where_ref, bf16[16,3,64,128]{3,2,1,0:T(8,128)(2,1)S(1)} %all-to-all-done.qkv_ref, bf16[128,1024]{1,0:T(8,128)(2,1)S(1)} %pad_maximum_fusion.1.refs_0_, ...), custom_call_target="tpu_custom_call" | custom-call | flops 1610612736 | bytes 4194304 | tf_op jit(solution)/shard_map/attention_backward/pallas_call | solution.py:106
  79.2 1.7 %collective-permute-done.12 = f32[64,1024]{1,0:T(8,128)S(1)} collective-permute-done((f32[64,1024]{1,0:T(8,128)}, f32[64,1024]{1,0:T(8,128)S(1)}, u32[]{:S(2)}, u32[]{:S(2)}) %collective-permute-start.12) | collective-permute-done | bytes 262176 | tf_op jit(solution)/shard_map/ppermute | solution.py:132
  81.1 2.3 %collective-permute-start.13 = (f32[2,2,2,1,4,1024]{5,4,3,2,1,0:T(4,128)S(1)}, f32[2,2,2,1,4,1024]{5,4,3,2,1,0:T(4,128)S(1)}, u32[]{:S(2)}, u32[]{:S(2)}) collective-permute-start(f32[2,2,2,1,4,1024]{5,4,3,2,1,0:T(4,128)S(1)} %slice_select_fusion), channel_id=1, source_target_pairs={{0,1},{1,0},{2,3},{3,2},{4,5},{5,4},{6,7},{7,6},{8,9},{9,8},{10,11... | collective-permute-start | bytes 393224 | tf_op jit(solution)/shard_map/ppermute | solution.py:132
  83.4 5.6 %all-to-all-start.1 = ((bf16[16,3,64,128]{3,2,1,0:T(8,128)(2,1)}), bf16[16,3,64,128]{3,2,1,0:T(8,128)(2,1)S(1)}, u32[]{:S(2)}, u32[]{:S(2)}) async-start(bf16[16,3,64,128]{3,2,1,0:T(8,128)(2,1)} %get-tuple-element.7), calls=%async_computation.1 | async-start | bytes 1572864 | tf_op jit(solution)/shard_map/all_to_all | solution.py:182
  89.1 1.8 %collective-permute-start.14 = (f32[2,2,1,1,4,1024]{5,4,3,2,1,0:T(4,128)S(1)}, f32[2,2,1,1,4,1024]{5,4,3,2,1,0:T(4,128)S(1)}, u32[]{:S(2)}, u32[]{:S(2)}) collective-permute-start(f32[2,2,1,1,4,1024]{5,4,3,2,1,0:T(4,128)S(1)} %slice_select_fusion.1), channel_id=1, source_target_pairs={{0,2},{1,3},{2,0},{3,1},{4,6},{5,7},{6,4},{7,5},{8,10},{9,11},{10,... | collective-permute-start | bytes 196616 | tf_op jit(solution)/shard_map/ppermute | solution.py:132
  90.9 4.3 %collective-permute-done.14 = f32[2,2,1,1,4,1024]{5,4,3,2,1,0:T(4,128)S(1)} collective-permute-done((f32[2,2,1,1,4,1024]{5,4,3,2,1,0:T(4,128)S(1)}, f32[2,2,1,1,4,1024]{5,4,3,2,1,0:T(4,128)S(1)}, u32[]{:S(2)}, u32[]{:S(2)}) %collective-permute-start.14) | collective-permute-done | bytes 65568 | tf_op jit(solution)/shard_map/ppermute | solution.py:132
  95.9 11.7 %collective-permute-done.15 = f32[2,1,1,1,4,1024]{5,4,3,2,1,0:T(4,128)S(1)} collective-permute-done((f32[2,1,1,1,4,1024]{5,4,3,2,1,0:T(4,128)S(1)}, f32[2,1,1,1,4,1024]{5,4,3,2,1,0:T(4,128)S(1)}, u32[]{:S(2)}, u32[]{:S(2)}) %collective-permute-start.15) | collective-permute-done | bytes 32800 | tf_op jit(solution)/shard_map/ppermute | solution.py:132
  107.6 3.1 %collective-permute-start.16 = (f32[1,1,1,1,4,1024]{5,4,3,2,1,0:T(4,128)S(1)}, f32[1,1,1,1,4,1024]{5,4,3,2,1,0:T(4,128)S(1)}, u32[]{:S(2)}, u32[]{:S(2)}) collective-permute-start(f32[1,1,1,1,4,1024]{5,4,3,2,1,0:T(4,128)S(1)} %slice_select_fusion.3), channel_id=1, source_target_pairs={{0,8},{1,9},{2,10},{3,11},{4,12},{5,13},{6,14},{7,15},{8,0},{9,1},... | collective-permute-start | bytes 49160 | tf_op jit(solution)/shard_map/ppermute | solution.py:132
  110.7 2.2 %collective-permute-done.16 = f32[1,1,1,1,4,1024]{5,4,3,2,1,0:T(4,128)S(1)} collective-permute-done((f32[1,1,1,1,4,1024]{5,4,3,2,1,0:T(4,128)S(1)}, f32[1,1,1,1,4,1024]{5,4,3,2,1,0:T(4,128)S(1)}, u32[]{:S(2)}, u32[]{:S(2)}) %collective-permute-start.16) | collective-permute-done | bytes 16416 | tf_op jit(solution)/shard_map/ppermute | solution.py:132
  113.6 1.8 %all-to-all-done.1 = bf16[16,3,64,128]{3,2,1,0:T(8,128)(2,1)S(1)} async-done(((bf16[16,3,64,128]{3,2,1,0:T(8,128)(2,1)}), bf16[16,3,64,128]{3,2,1,0:T(8,128)(2,1)S(1)}, u32[]{:S(2)}, u32[]{:S(2)}) %all-to-all-start.1) | async-done | bytes 786464 | tf_op jit(solution)/shard_map/all_to_all | solution.py:182
  116.6 0.8 squeeze.12
  117.5 0.8 squeeze.13
  (47 shorter events, 4.1 us)
Async XLA Ops:
  0.6 14.8 %copy-start = (bf16[1024,64]{0,1:T(8,128)(2,1)S(1)}, bf16[1024,64]{0,1:T(8,128)(2,1)}, u32[]{:S(2)}) copy-start(bf16[1024,64]{0,1:T(8,128)(2,1)} %param.9) | copy-start | bytes 393220
  1.8 1.0 copy-start.1
  2.9 1.0 copy-start.2
  5.1 11.9 %copy-start.3 = (bf16[64,2,1,1024]{3,1,2,0:T(2,128)(2,1)S(1)}, bf16[64,2,1,1024]{3,1,2,0:T(2,128)(2,1)}, u32[]{:S(2)}) copy-start(bf16[64,2,1,1024]{3,1,2,0:T(2,128)(2,1)} %param.8) | copy-start | bytes 786436
  5.1 67.7 %all-to-all-start = ((bf16[16,3,64,128]{3,2,1,0:T(8,128)(2,1)}), bf16[16,3,64,128]{3,2,1,0:T(8,128)(2,1)S(1)}, u32[]{:S(2)}, u32[]{:S(2)}) async-start(bf16[16,3,64,128]{3,2,1,0:T(8,128)(2,1)} %bitcast.5), calls=%async_computation | async-start | bytes 1572864 | tf_op jit(solution)/shard_map/all_to_all | solution.py:167
  15.4 14.0 %collective-permute-start.8 = (bf16[64,128]{1,0:T(8,128)(2,1)S(1)}, bf16[64,128]{1,0:T(8,128)(2,1)S(1)}, u32[]{:S(2)}, u32[]{:S(2)}) collective-permute-start(bf16[64,128]{1,0:T(8,128)(2,1)S(1)} %dynamic-slice_bitcast_fusion.refs_8_), channel_id=1, source_target_pairs={{0,8},{1,9},{2,10},{3,11},{4,12},{5,13},{6,14},{7,15},{8,0},{9,1},... | collective-permute-start | bytes 49160 | tf_op jit(solution)/shard_map/ppermute | solution.py:132
  29.4 9.7 %collective-permute-start.9 = (bf16[128,128]{1,0:T(8,128)(2,1)S(1)}, bf16[128,128]{1,0:T(8,128)(2,1)S(1)}, u32[]{:S(2)}, u32[]{:S(2)}) collective-permute-start(bf16[128,128]{1,0:T(8,128)(2,1)S(1)} %pad_maximum_fusion.4), channel_id=1, source_target_pairs={{0,4},{1,5},{2,6},{3,7},{4,0},{5,1},{6,2},{7,3},{8,12},{9,13},{10,... | collective-permute-start | bytes 98312 | tf_op jit(solution)/shard_map/ppermute | solution.py:132
  31.1 8.3 %collective-permute-start = (bf16[64,1024]{1,0:T(8,128)(2,1)S(1)}, bf16[64,1024]{1,0:T(8,128)(2,1)S(1)}, u32[]{:S(2)}, u32[]{:S(2)}) collective-permute-start(bf16[64,1024]{1,0:T(8,128)(2,1)S(1)} %get-tuple-element.14), channel_id=1, source_target_pairs={{0,16},{16,0},{32,48},{48,32},{64,80},{80,64},{96,112},{112,96},{1... | collective-permute-start | bytes 393224 | tf_op jit(solution)/shard_map/ppermute | solution.py:132
  39.1 6.8 %collective-permute-start.10 = (bf16[256,128]{1,0:T(8,128)(2,1)S(1)}, bf16[256,128]{1,0:T(8,128)(2,1)S(1)}, u32[]{:S(2)}, u32[]{:S(2)}) collective-permute-start(bf16[256,128]{1,0:T(8,128)(2,1)S(1)} %pad_maximum_fusion.3), channel_id=1, source_target_pairs={{0,2},{1,3},{2,0},{3,1},{4,6},{5,7},{6,4},{7,5},{8,10},{9,11},{10,... | collective-permute-start | bytes 196616 | tf_op jit(solution)/shard_map/ppermute | solution.py:132
  39.4 16.6 %collective-permute-start.4 = (bf16[128,1024]{1,0:T(8,128)(2,1)S(1)}, bf16[128,1024]{1,0:T(8,128)(2,1)S(1)}, u32[]{:S(2)}, u32[]{:S(2)}) collective-permute-start(bf16[128,1024]{1,0:T(8,128)(2,1)S(1)} %pad_maximum_fusion.1.refs_0_), channel_id=1, source_target_pairs={{0,32},{16,48},{32,0},{48,16},{64,96},{80,112},{96,64},{112,80},{1... | collective-permute-start | bytes 786440 | tf_op jit(solution)/shard_map/ppermute | solution.py:132
  44.6 16.5 %collective-permute-start.1 = (bf16[128,1024]{1,0:T(8,128)(2,1)S(1)}, bf16[128,1024]{1,0:T(8,128)(2,1)S(1)}, u32[]{:S(2)}, u32[]{:S(2)}) collective-permute-start(bf16[128,1024]{1,0:T(8,128)(2,1)S(1)} %pad_maximum_fusion.1.refs_0_), channel_id=1, source_target_pairs={{0,64},{16,80},{32,96},{48,112},{64,128},{80,144},{96,160},{112,17... | collective-permute-start | bytes 786440 | tf_op jit(solution)/shard_map/ppermute | solution.py:154
  45.9 12.6 %collective-permute-start.11 = (bf16[512,128]{1,0:T(8,128)(2,1)S(1)}, bf16[512,128]{1,0:T(8,128)(2,1)S(1)}, u32[]{:S(2)}, u32[]{:S(2)}) collective-permute-start(bf16[512,128]{1,0:T(8,128)(2,1)S(1)} %pad_maximum_fusion.2), channel_id=1, source_target_pairs={{0,1},{1,0},{2,3},{3,2},{4,5},{5,4},{6,7},{7,6},{8,9},{9,8},{10,11... | collective-permute-start | bytes 393224 | tf_op jit(solution)/shard_map/ppermute | solution.py:132
  48.1 14.5 %collective-permute-start.2 = (bf16[128,1024]{1,0:T(8,128)(2,1)S(1)}, bf16[128,1024]{1,0:T(8,128)(2,1)S(1)}, u32[]{:S(2)}, u32[]{:S(2)}) collective-permute-start(bf16[128,1024]{1,0:T(8,128)(2,1)S(1)} %pad_maximum_fusion.1.refs_0_), channel_id=1, source_target_pairs={{0,128},{16,144},{32,160},{48,176},{64,192},{80,208},{96,224},{112... | collective-permute-start | bytes 786440 | tf_op jit(solution)/shard_map/ppermute | solution.py:154
  50.8 11.9 %collective-permute-start.3 = (bf16[128,1024]{1,0:T(8,128)(2,1)S(1)}, bf16[128,1024]{1,0:T(8,128)(2,1)S(1)}, u32[]{:S(2)}, u32[]{:S(2)}) collective-permute-start(bf16[128,1024]{1,0:T(8,128)(2,1)S(1)} %pad_maximum_fusion.1.refs_0_), channel_id=1, source_target_pairs={{0,192},{16,208},{32,224},{48,240},{64,0},{80,16},{96,32},{112,48}... | collective-permute-start | bytes 786440 | tf_op jit(solution)/shard_map/ppermute | solution.py:154
  56.0 10.0 %collective-permute-start.5 = (bf16[128,1024]{1,0:T(8,128)(2,1)S(1)}, bf16[128,1024]{1,0:T(8,128)(2,1)S(1)}, u32[]{:S(2)}, u32[]{:S(2)}) collective-permute-start(bf16[128,1024]{1,0:T(8,128)(2,1)S(1)} %collective-permute-done.4.refs_4_), channel_id=1, source_target_pairs={{0,64},{16,80},{32,96},{48,112},{64,128},{80,144},{96,160},{112,17... | collective-permute-start | bytes 786440 | tf_op jit(solution)/shard_map/ppermute | solution.py:154
  58.5 14.3 %collective-permute-start.6 = (bf16[128,1024]{1,0:T(8,128)(2,1)S(1)}, bf16[128,1024]{1,0:T(8,128)(2,1)S(1)}, u32[]{:S(2)}, u32[]{:S(2)}) collective-permute-start(bf16[128,1024]{1,0:T(8,128)(2,1)S(1)} %collective-permute-done.4.refs_4_), channel_id=1, source_target_pairs={{0,128},{16,144},{32,160},{48,176},{64,192},{80,208},{96,224},{112... | collective-permute-start | bytes 786440 | tf_op jit(solution)/shard_map/ppermute | solution.py:154
  61.1 11.7 %collective-permute-start.7 = (bf16[128,1024]{1,0:T(8,128)(2,1)S(1)}, bf16[128,1024]{1,0:T(8,128)(2,1)S(1)}, u32[]{:S(2)}, u32[]{:S(2)}) collective-permute-start(bf16[128,1024]{1,0:T(8,128)(2,1)S(1)} %collective-permute-done.4.refs_4_), channel_id=1, source_target_pairs={{0,192},{16,208},{32,224},{48,240},{64,0},{80,16},{96,32},{112,48}... | collective-permute-start | bytes 786440 | tf_op jit(solution)/shard_map/ppermute | solution.py:154
  79.2 1.7 %collective-permute-start.12 = (f32[64,1024]{1,0:T(8,128)}, f32[64,1024]{1,0:T(8,128)S(1)}, u32[]{:S(2)}, u32[]{:S(2)}) collective-permute-start(f32[64,1024]{1,0:T(8,128)} %get-tuple-element.9), channel_id=1, source_target_pairs={{0,16},{16,0},{32,48},{48,32},{64,80},{80,64},{96,112},{112,96},{1... | collective-permute-start | bytes 786440 | tf_op jit(solution)/shard_map/ppermute | solution.py:132
  81.1 7.9 %collective-permute-start.13 = (f32[2,2,2,1,4,1024]{5,4,3,2,1,0:T(4,128)S(1)}, f32[2,2,2,1,4,1024]{5,4,3,2,1,0:T(4,128)S(1)}, u32[]{:S(2)}, u32[]{:S(2)}) collective-permute-start(f32[2,2,2,1,4,1024]{5,4,3,2,1,0:T(4,128)S(1)} %slice_select_fusion), channel_id=1, source_target_pairs={{0,1},{1,0},{2,3},{3,2},{4,5},{5,4},{6,7},{7,6},{8,9},{9,8},{10,11... | collective-permute-start | bytes 393224 | tf_op jit(solution)/shard_map/ppermute | solution.py:132
  83.4 32.0 %all-to-all-start.1 = ((bf16[16,3,64,128]{3,2,1,0:T(8,128)(2,1)}), bf16[16,3,64,128]{3,2,1,0:T(8,128)(2,1)S(1)}, u32[]{:S(2)}, u32[]{:S(2)}) async-start(bf16[16,3,64,128]{3,2,1,0:T(8,128)(2,1)} %get-tuple-element.7), calls=%async_computation.1 | async-start | bytes 1572864 | tf_op jit(solution)/shard_map/all_to_all | solution.py:182
  89.1 6.0 %collective-permute-start.14 = (f32[2,2,1,1,4,1024]{5,4,3,2,1,0:T(4,128)S(1)}, f32[2,2,1,1,4,1024]{5,4,3,2,1,0:T(4,128)S(1)}, u32[]{:S(2)}, u32[]{:S(2)}) collective-permute-start(f32[2,2,1,1,4,1024]{5,4,3,2,1,0:T(4,128)S(1)} %slice_select_fusion.1), channel_id=1, source_target_pairs={{0,2},{1,3},{2,0},{3,1},{4,6},{5,7},{6,4},{7,5},{8,10},{9,11},{10,... | collective-permute-start | bytes 196616 | tf_op jit(solution)/shard_map/ppermute | solution.py:132
  95.2 12.4 %collective-permute-start.15 = (f32[2,1,1,1,4,1024]{5,4,3,2,1,0:T(4,128)S(1)}, f32[2,1,1,1,4,1024]{5,4,3,2,1,0:T(4,128)S(1)}, u32[]{:S(2)}, u32[]{:S(2)}) collective-permute-start(f32[2,1,1,1,4,1024]{5,4,3,2,1,0:T(4,128)S(1)} %slice_select_fusion.2), channel_id=1, source_target_pairs={{0,4},{1,5},{2,6},{3,7},{4,0},{5,1},{6,2},{7,3},{8,12},{9,13},{10,... | collective-permute-start | bytes 98312 | tf_op jit(solution)/shard_map/ppermute | solution.py:132
  107.6 5.3 %collective-permute-start.16 = (f32[1,1,1,1,4,1024]{5,4,3,2,1,0:T(4,128)S(1)}, f32[1,1,1,1,4,1024]{5,4,3,2,1,0:T(4,128)S(1)}, u32[]{:S(2)}, u32[]{:S(2)}) collective-permute-start(f32[1,1,1,1,4,1024]{5,4,3,2,1,0:T(4,128)S(1)} %slice_select_fusion.3), channel_id=1, source_target_pairs={{0,8},{1,9},{2,10},{3,11},{4,12},{5,13},{6,14},{7,15},{8,0},{9,1},... | collective-permute-start | bytes 49160 | tf_op jit(solution)/shard_map/ppermute | solution.py:132

commit v2 on v1

v2 whole, which is shorter than its diff:
```python
import functools
import math

import jax
import jax.numpy as jnp
from jax import lax
from jax.experimental import pallas as pl
from jax.experimental.pallas import tpu as pltpu
from jax.sharding import PartitionSpec as P

HEADS = 8
HEAD = 128
BLOCK = 64
ROWS = 256


def dot(a, b, ca, cb):
    return lax.dot_general(
        a, b, (((ca,), (cb,)), ((), ())), preferred_element_type=jnp.float32
    )


def logits_of(qkv_ref, i):
    steps = ROWS // BLOCK
    width = (i + 1) * ROWS
    q = qkv_ref[i * steps : (i + 1) * steps, 0].reshape(ROWS, HEAD)
    k = qkv_ref[: (i + 1) * steps, 1].reshape(width, HEAD)
    v = qkv_ref[: (i + 1) * steps, 2].reshape(width, HEAD)
    s = dot(q, k, 1, 1) * (HEAD ** (-0.5) * math.log2(math.e))
    row_at = lax.broadcasted_iota(jnp.int32, s.shape, 0) + i * ROWS
    col_at = lax.broadcasted_iota(jnp.int32, s.shape, 1)
    return jnp.where(col_at <= row_at, s, -1e30), q, k, v


def forward_kernel(qkv_ref, att_ref, lse_ref):
    for i in range(att_ref.shape[0] // ROWS):
        rows = slice(i * ROWS, (i + 1) * ROWS)
        s, _, _, v = logits_of(qkv_ref, i)
        peak = jnp.max(s, axis=1, keepdims=True)
        e = jnp.exp2(s - peak)
        total = jnp.sum(e, axis=1, keepdims=True)
        p_low = (e * (1.0 / total)).astype(jnp.bfloat16)
        att_ref[rows, :] = dot(p_low, v, 1, 0).astype(jnp.bfloat16)
        lse_ref[rows, :] = peak + jnp.log2(total)


def chunks(places, piece_refs):
    tm = lax.axis_index("tm")
    x, z, core = tm // 4, (tm // 2) % 2, tm % 2
    for (far, back), ref in zip(places, piece_refs):
        for at in range(ref.shape[0] // (2 * BLOCK)):
            chip_x = at if back is None else (x + 4 - back) % 4
            first = 4 * chip_x + 2 * (z ^ far)
            rows = [
                pl.ds(pl.multiple_of((first + (core ^ sub)) * BLOCK, BLOCK), BLOCK) for sub in range(2)
            ]
            yield ref[at * 2 * BLOCK : (at + 1) * 2 * BLOCK, :], rows


def weight_kernel(norm_factor, places, att_ref, *refs):
    keep_ref, send_ref, gw_ref = refs[len(places) :]
    core = lax.axis_index("tm") % 2
    for n, (chunk, rows) in enumerate(chunks(places, refs)):
        att = jnp.concatenate([att_ref[r, :] for r in rows], axis=0)
        term = dot(att, chunk, 0, 0)
        if n == 0:
            gw_ref[...] = term
        else:
            gw_ref[...] += term
    half = HEAD // 2
    keep_ref[...] = gw_ref[pl.ds(pl.multiple_of(core * half, half), half), :] * norm_factor
    send_ref[...] = gw_ref[pl.ds(pl.multiple_of((1 - core) * half, half), half), :] * norm_factor


def backward_kernel(places, qkv_ref, lse_ref, *refs):
    weight_refs = refs[len(places) : len(places) + 4]
    grads_ref, w_ref, do_ref, gk_ref, gv_ref = refs[len(places) + 4 :]
    n_tm = qkv_ref.shape[0]
    length = n_tm * BLOCK

    track = lax.axis_index("track")
    size = w_ref.shape[0] // 16
    for p in range(16):
        owner = track ^ ((p % 4) * 4 + p // 4)
        w_ref[pl.ds(pl.multiple_of(owner * size, size), size), :] = weight_refs[p // 4][
            (p % 4) * size : (p % 4 + 1) * size, :
        ]
    for chunk, rows in chunks(places, refs):
        part = dot(chunk, w_ref[...], 1, 0).astype(jnp.bfloat16)
        do_ref[rows[0], :] = part[:BLOCK]
        do_ref[rows[1], :] = part[BLOCK:]

    scale = HEAD ** (-0.5)
    steps = ROWS // BLOCK
    for i in range(length // ROWS):
        width = (i + 1) * ROWS
        rows = slice(i * ROWS, (i + 1) * ROWS)
        do = do_ref[rows, :]
        s, q, k, v = logits_of(qkv_ref, i)
        p = jnp.exp2(s - lse_ref[rows, :])
        dp = dot(do, v, 1, 1)
        delta = jnp.sum(p * dp, axis=1, keepdims=True)
        ds = (p * (dp - delta) * scale).astype(jnp.bfloat16)
        gq = dot(ds, k, 1, 0).astype(jnp.bfloat16)
        grads_ref[i * steps : (i + 1) * steps, 0] = gq.reshape(steps, BLOCK, HEAD)
        gk = dot(q, ds, 0, 0)
        gv = dot(do, p.astype(jnp.bfloat16), 0, 0)
        if i:
            gk_ref[:, : width - ROWS] += gk[:, : width - ROWS]
            gv_ref[:, : width - ROWS] += gv[:, : width - ROWS]
            gk, gv = gk[:, width - ROWS :], gv[:, width - ROWS :]
        gk_ref[:, rows] = gk
        gv_ref[:, rows] = gv
    grads_ref[:, 1] = gk_ref[...].T.astype(jnp.bfloat16).reshape(n_tm, BLOCK, HEAD)
    grads_ref[:, 2] = gv_ref[...].T.astype(jnp.bfloat16).reshape(n_tm, BLOCK, HEAD)


VMEM = pl.BlockSpec(memory_space=pltpu.VMEM)
PARAMS = pltpu.CompilerParams(vmem_limit_bytes=48 * 1024 * 1024)


def cost(products, length, bytes_accessed):
    return pl.CostEstimate(
        flops=2 * products * length * length * HEAD,
        bytes_accessed=bytes_accessed,
        transcendentals=length * length,
    )


def forward(qkv):
    length = qkv.shape[0] * BLOCK
    return pl.pallas_call(
        forward_kernel,
        out_shape=(
            jax.ShapeDtypeStruct((length, HEAD), jnp.bfloat16),
            jax.ShapeDtypeStruct((length, 1), jnp.float32),
        ),
        in_specs=[VMEM],
        out_specs=(VMEM, VMEM),
        compiler_params=PARAMS,
        cost_estimate=cost(2, length, 2 << 20),
        name="forward",
    )(qkv)


def weight_term(att, places, pieces, norm_factor):
    length, width = att.shape[0], pieces[0].shape[1]
    half = jax.ShapeDtypeStruct((HEAD // 2, width), jnp.float32)
    return pl.pallas_call(
        functools.partial(weight_kernel, norm_factor, places),
        out_shape=(half, half),
        in_specs=[VMEM] * (1 + len(pieces)),
        out_specs=(VMEM, VMEM),
        scratch_shapes=[pltpu.VMEM((HEAD, width), jnp.float32)],
        compiler_params=PARAMS,
        cost_estimate=cost(1, length, 3 << 20),
        name="weight_term",
    )(att, *pieces)


def backward(qkv, lse, places, pieces, weight):
    length = lse.shape[0]
    return pl.pallas_call(
        functools.partial(backward_kernel, places),
        out_shape=jax.ShapeDtypeStruct(qkv.shape, jnp.bfloat16),
        in_specs=[VMEM] * (2 + len(pieces) + len(weight)),
        out_specs=VMEM,
        scratch_shapes=[
            pltpu.VMEM((pieces[0].shape[1], HEAD), jnp.bfloat16),
            pltpu.VMEM((length, HEAD), jnp.bfloat16),
            pltpu.VMEM((HEAD, length), jnp.float32),
            pltpu.VMEM((HEAD, length), jnp.float32),
        ],
        compiler_params=PARAMS,
        cost_estimate=cost(6, length, 4 << 20),
        name="backward",
    )(qkv, lse, *pieces, *weight)


def shuffle(inverse, flip):
    near = lax.broadcasted_iota(jnp.int32, (2 * BLOCK, 2 * BLOCK), 1 if inverse else 0)
    far = lax.broadcasted_iota(jnp.int32, (2 * BLOCK, 2 * BLOCK), 0 if inverse else 1)
    score = (near // BLOCK) ^ flip
    return jnp.where(far == 2 * (near % BLOCK) + score, 1.0, 0.0).astype(jnp.bfloat16)


def prepare_kernel(query_ref, key_ref, value_ref, grad_ref, out_ref, mine_ref, other_ref):
    parts = dot(shuffle(False, lax.axis_index("tm") % 2), grad_ref[...].reshape(2 * BLOCK, -1), 1, 0)
    mine_ref[...] = parts[:BLOCK].astype(jnp.bfloat16)
    other_ref[...] = parts[BLOCK:].astype(jnp.bfloat16)
    move = shuffle(False, 0)
    for a, ref in enumerate((query_ref, key_ref, value_ref)):
        rows = ref[...].reshape(2 * BLOCK, ref.shape[2])
        parts = dot(move, rows, 1, 0).astype(jnp.bfloat16)
        for score in range(2):
            for head in range(HEADS):
                out_ref[2 * head + score, a] = parts[
                    score * BLOCK : (score + 1) * BLOCK, head * HEAD : (head + 1) * HEAD
                ]


def unpack_kernel(in_ref, query_ref, key_ref, value_ref):
    move = shuffle(True, 0)
    for a, ref in enumerate((query_ref, key_ref, value_ref)):
        parts = jnp.concatenate(
            [
                jnp.concatenate([in_ref[2 * head + score, a] for head in range(HEADS)], axis=1)
                for score in range(2)
            ],
            axis=0,
        )
        rows = dot(move, parts, 1, 0).astype(jnp.bfloat16)
        ref[...] = rows.reshape(ref.shape)


def prepare(query, key, value, grad):
    half = jax.ShapeDtypeStruct((grad.shape[0], grad.shape[2]), grad.dtype)
    return pl.pallas_call(
        prepare_kernel,
        out_shape=(jax.ShapeDtypeStruct((2 * HEADS, 3, BLOCK, HEAD), query.dtype), half, half),
        in_specs=[VMEM] * 4,
        out_specs=(VMEM,) * 3,
        name="prepare",
    )(query, key, value, grad)


def unpack(items):
    rows = jax.ShapeDtypeStruct((BLOCK, 2, HEADS * HEAD), items.dtype)
    return pl.pallas_call(
        unpack_kernel, out_shape=(rows,) * 3, in_specs=[VMEM], out_specs=(VMEM,) * 3, name="unpack"
    )(items)


def swap(array, axis, mask):
    return lax.ppermute(array, axis, [(i, i ^ mask) for i in range(16)])


def shift(array, by):
    return lax.ppermute(array, "tm", [(i, (i + 4 * by) % 16) for i in range(16)])


def local(query_rows, key_rows, value_rows, grad_output, out_weight):
    step_rows, score_count, track_local, model_width = query_rows.shape
    n_tm = lax.axis_size("tm")
    total_tokens = step_rows * n_tm * score_count * track_local * lax.axis_size("track")
    norm_factor = 1.0 / math.sqrt(total_tokens)
    tm = lax.axis_index("tm")
    track = lax.axis_index("track")
    head = tm // 2

    flat = (step_rows, score_count, model_width)

    qkv, mine, other = prepare(*(a.reshape(flat) for a in (query_rows, key_rows, value_rows, grad_output)))
    chip_piece = jnp.concatenate([mine, swap(other, "tm", 1)], axis=0)
    far_piece = swap(chip_piece, "tm", 2)
    places, pieces = [], []
    for d in range(4):
        places.append((0, d))
        pieces.append(shift(chip_piece, d) if d else chip_piece)
    for d in range(4):
        places.append((1, d))
        pieces.append(shift(far_piece, d) if d else far_piece)

    held = lax.dynamic_slice_in_dim(out_weight.T, head * HEAD, HEAD, axis=1)
    held = jnp.concatenate([held] + [swap(held, "track", 4 * j) for j in (1, 2, 3)], axis=0)
    held_z = held
    held, _ = lax.optimization_barrier((held, far_piece))
    weight = [held] + [swap(held, "track", j) for j in (1, 2, 3)]

    qkv, _ = lax.optimization_barrier((qkv, (far_piece, held_z, pieces[1], pieces[2], pieces[3])))
    qkv = lax.all_to_all(qkv, "tm", split_axis=0, concat_axis=0, tiled=True)

    att, lse = forward(qkv)
    keep, send = weight_term(att, places, pieces, norm_factor)
    lse, _ = lax.optimization_barrier((lse, (keep, send)))

    total = keep + swap(send, "tm", 1)
    after_core = total
    total = total.reshape(4, 4, 4, model_width)
    for axis, step, place in ((1, 1, track % 4), (0, 4, track // 4)):
        parts = [lax.dynamic_index_in_dim(total, place ^ j, axis, keepdims=False) for j in range(4)]
        total = parts[0]
        for j in (1, 2, 3):
            total = total + swap(parts[j], "track", step * j)
        if step == 1:
            after_y = total
    grad_weight = total

    item_grads = backward(qkv, lse, places, pieces, weight)
    returned = lax.all_to_all(item_grads, "tm", split_axis=0, concat_axis=0, tiled=True)
    shape = query_rows.shape
    grad_query, grad_key, grad_value = (g.reshape(shape) for g in unpack(returned))
    return (grad_query, grad_key, grad_value, grad_weight)


def solution(mesh):
    return jax.shard_map(
        local,
        mesh=mesh,
        in_specs=(
            P("tm", None, "track", None),
            P("tm", None, "track", None),
            P("tm", None, "track", None),
            P("tm", None, "track", None),
            P(None, "track"),
        ),
        out_specs=(
            P("tm", None, "track", None),
            P("tm", None, "track", None),
            P("tm", None, "track", None),
            P(("tm", "track"), None),
        ),
        check_vma=False,
    )
```

time: 120 us -> 105 us (0.88)
  waiting for transfers between devices: 55.9 us -> 42.7 us
  Pallas kernels: 6.37 us -> 11.9 us
  local copies, waits for them, and re-layouts: 6.47 us -> 2.66 us
  starting transfers between devices: 46.8 us -> 45.1 us
  other arithmetic: 1.93 us -> 0.68 us
    ppermute x11 -> x15, waiting for transfers between devices: 43.9 us -> 26.3 us  [swap(): return lax.ppermute(array, axis, [(i, i ^ mask) for i in range(16)])]
    pallas_call x1 -> x5, Pallas kernels: 6.37 us -> 11.9 us  [the longest x1 4.11 us: backward(): pl.pallas_call(functools.partial(backward_kernel, places), out_shape=jax....]
    all_to_all x1, starting transfers between devices: 10.3 us -> 4.8 us  [local(): qkv = lax.all_to_all(qkv, 'tm', split_axis=0, concat_axis=0, tiled=True)]
    all_to_all x1, waiting for transfers between devices: 0.01 us -> 3.45 us  [local(): qkv = lax.all_to_all(qkv, 'tm', split_axis=0, concat_axis=0, tiled=True)]
    ppermute x11 -> x15, starting transfers between devices: 19 us -> 21.7 us  [swap(): return lax.ppermute(array, axis, [(i, i ^ mask) for i in range(16)])]
    squeeze x3 -> x2, local copies, waits for them, and re-layouts: 2.3 us -> 0.04 us  [local(): lax.dynamic_index_in_dim(total, place ^ j, axis, keepdims=False)]
    all_to_all x1, starting transfers between devices: 5.64 us -> 7.47 us  [local(): lax.all_to_all(item_grads, 'tm', split_axis=0, concat_axis=0, tiled=True)]
    another operation x6 -> x0, local copies, waits for them, and re-layouts: 1.7 us -> none  [local(): jnp.stack([query_rows, key_rows, value_rows])]
  transfers between devices with their start and end apart: 19 -> 23, of which waited for: 10 -> 15; matrix products, arithmetic and copies ran while one was open for 1% -> 2% of each run, Pallas kernels for 0% -> 3%
where the time goes in v2:
time: 105 us; the launch traced here: 104 us
  starting transfers between devices  45.1 us (43%)
  waiting for transfers between devices  42.7 us (41%)
  Pallas kernels  11.9 us (11%)
  local copies, waits for them, and re-layouts  2.66 us (3%)
    ppermute x15, waiting for transfers between devices, swap(): return lax.ppermute(array, axis, [(i, i ^ mask) for i in range(16)])  26.3 us
    ppermute x15, starting transfers between devices, swap(): return lax.ppermute(array, axis, [(i, i ^ mask) for i in range(16)])  21.7 us
    ppermute x6, starting transfers between devices, shift(): lax.ppermute(array, 'tm', [(i, (i + 4 * by) % 16) for i in range(16)])  11.1 us
    ppermute x6, waiting for transfers between devices, shift(): lax.ppermute(array, 'tm', [(i, (i + 4 * by) % 16) for i in range(16)])  10.8 us
    all_to_all x1, starting transfers between devices, local(): lax.all_to_all(item_grads, 'tm', split_axis=0, concat_axis=0, tiled=True)  7.47 us
    all_to_all x1, starting transfers between devices, local(): qkv = lax.all_to_all(qkv, 'tm', split_axis=0, concat_axis=0, tiled=True)  4.8 us
    pallas_call x1, Pallas kernels, backward(): pl.pallas_call(functools.partial(backward_kernel, places), out_shape=jax....  4.11 us
    all_to_all x1, waiting for transfers between devices, local(): qkv = lax.all_to_all(qkv, 'tm', split_axis=0, concat_axis=0, tiled=True)  3.45 us
  transfers between devices with their start and end apart: 23, of which 15 were waited for; matrix products, arithmetic and copies ran while one was open for 2% of the time, Pallas kernels for 3%

profile of v2, /device:TPU:48, one launch (start us, length us, event | category | flops | bytes accessed | tf_op | source)
XLA Modules:
  0.0 103.8 jit_solution(14806101098210351834)
XLA Ops:
  0.6 2.6 %prepare.1 = (bf16[16,3,64,128]{3,2,1,0:T(8,128)(2,1)}, bf16[64,1024]{1,0:T(8,128)(2,1)}, bf16[64,1024]{1,0:T(8,128)(2,1)}) custom-call(bf16[64,2,1024]{2,1,0:T(2,128)(2,1)} %bitcast.39, bf16[64,2,1024]{2,1,0:T(2,128)(2,1)} %bitcast.40, bf16[64,2,1024]{2,1,0:T(2,128)(2,1)} %bitcast.41, bf16[64,2,1024]{2,1,0:T(2,128)(2,1)} %bitcast.42), custom_call_target="tpu_custom_call" | custom-call | tf_op jit(solution)/shard_map/prepare/pallas_call | solution.py:218
  3.2 0.9 constant_dynamic-update-slice_fusion.1
  4.8 6.4 %collective-permute-start.1 = (bf16[128,1024]{1,0:T(8,128)(2,1)S(1)}, bf16[128,1024]{1,0:T(8,128)(2,1)S(1)}, u32[]{:S(2)}, u32[]{:S(2)}) collective-permute-start(bf16[128,1024]{1,0:T(8,128)(2,1)S(1)} %constant_dynamic-update-slice_fusion.refs_0_), channel_id=1, source_target_pairs={{0,32},{16,48},{32,0},{48,16},{64,96},{80,112},{96,64},{112,80},{1... | collective-permute-start | bytes 786440 | tf_op jit(solution)/shard_map/ppermute | solution.py:235
  11.2 1.5 %collective-permute-start.5 = (bf16[128,1024]{1,0:T(8,128)(2,1)S(1)}, bf16[128,1024]{1,0:T(8,128)(2,1)S(1)}, u32[]{:S(2)}, u32[]{:S(2)}) collective-permute-start(bf16[128,1024]{1,0:T(8,128)(2,1)S(1)} %constant_dynamic-update-slice_fusion.refs_0_), channel_id=1, source_target_pairs={{0,64},{16,80},{32,96},{48,112},{64,128},{80,144},{96,160},{112,17... | collective-permute-start | bytes 786440 | tf_op jit(solution)/shard_map/ppermute | solution.py:239
  12.7 2.7 %collective-permute-start.6 = (bf16[128,1024]{1,0:T(8,128)(2,1)S(1)}, bf16[128,1024]{1,0:T(8,128)(2,1)S(1)}, u32[]{:S(2)}, u32[]{:S(2)}) collective-permute-start(bf16[128,1024]{1,0:T(8,128)(2,1)S(1)} %constant_dynamic-update-slice_fusion.refs_0_), channel_id=1, source_target_pairs={{0,128},{16,144},{32,160},{48,176},{64,192},{80,208},{96,224},{112... | collective-permute-start | bytes 786440 | tf_op jit(solution)/shard_map/ppermute | solution.py:239
  15.4 1.4 %collective-permute-start.7 = (bf16[128,1024]{1,0:T(8,128)(2,1)S(1)}, bf16[128,1024]{1,0:T(8,128)(2,1)S(1)}, u32[]{:S(2)}, u32[]{:S(2)}) collective-permute-start(bf16[128,1024]{1,0:T(8,128)(2,1)S(1)} %constant_dynamic-update-slice_fusion.refs_0_), channel_id=1, source_target_pairs={{0,192},{16,208},{32,224},{48,240},{64,0},{80,16},{96,32},{112,48}... | collective-permute-start | bytes 786440 | tf_op jit(solution)/shard_map/ppermute | solution.py:239
  16.8 1.1 %collective-permute-start.2 = (bf16[64,128]{1,0:T(8,128)(2,1)S(1)}, bf16[64,128]{1,0:T(8,128)(2,1)S(1)}, u32[]{:S(2)}, u32[]{:S(2)}) collective-permute-start(bf16[64,128]{1,0:T(8,128)(2,1)S(1)} %dynamic-slice_bitcast_fusion.6), channel_id=1, source_target_pairs={{0,4},{1,5},{2,6},{3,7},{4,0},{5,1},{6,2},{7,3},{8,12},{9,13},{10,... | collective-permute-start | bytes 49160 | tf_op jit(solution)/shard_map/ppermute | solution.py:235
  17.9 5.8 %collective-permute-done.2 = bf16[64,128]{1,0:T(8,128)(2,1)S(1)} collective-permute-done((bf16[64,128]{1,0:T(8,128)(2,1)S(1)}, bf16[64,128]{1,0:T(8,128)(2,1)S(1)}, u32[]{:S(2)}, u32[]{:S(2)}) %collective-permute-start.2) | collective-permute-done | bytes 16416 | tf_op jit(solution)/shard_map/ppermute | solution.py:235
  23.7 2.0 %collective-permute-start.3 = (bf16[64,128]{1,0:T(8,128)(2,1)S(1)}, bf16[64,128]{1,0:T(8,128)(2,1)S(1)}, u32[]{:S(2)}, u32[]{:S(2)}) collective-permute-start(bf16[64,128]{1,0:T(8,128)(2,1)S(1)} %dynamic-slice_bitcast_fusion.6), channel_id=1, source_target_pairs={{0,8},{1,9},{2,10},{3,11},{4,12},{5,13},{6,14},{7,15},{8,0},{9,1},... | collective-permute-start | bytes 49160 | tf_op jit(solution)/shard_map/ppermute | solution.py:235
  25.8 2.6 %collective-permute-done.3 = bf16[64,128]{1,0:T(8,128)(2,1)S(1)} collective-permute-done((bf16[64,128]{1,0:T(8,128)(2,1)S(1)}, bf16[64,128]{1,0:T(8,128)(2,1)S(1)}, u32[]{:S(2)}, u32[]{:S(2)}) %collective-permute-start.3) | collective-permute-done | bytes 16416 | tf_op jit(solution)/shard_map/ppermute | solution.py:235
  29.0 3.2 %collective-permute-done.4 = bf16[64,128]{1,0:T(8,128)(2,1)S(1)} collective-permute-done((bf16[64,128]{1,0:T(8,128)(2,1)S(1)}, bf16[64,128]{1,0:T(8,128)(2,1)S(1)}, u32[]{:S(2)}, u32[]{:S(2)}) %collective-permute-start.4) | collective-permute-done | bytes 16416 | tf_op jit(solution)/shard_map/ppermute | solution.py:235
  32.2 4.8 %all-to-all-start = ((bf16[16,3,64,128]{3,2,1,0:T(8,128)(2,1)}), bf16[16,3,64,128]{3,2,1,0:T(8,128)(2,1)S(1)}, u32[]{:S(2)}, u32[]{:S(2)}) async-start(bf16[16,3,64,128]{3,2,1,0:T(8,128)(2,1)} %get-tuple-element.20), calls=%async_computation | async-start | bytes 1572864 | tf_op jit(solution)/shard_map/all_to_all | solution.py:271
  37.0 3.1 %collective-permute-start.10 = (bf16[128,1024]{1,0:T(8,128)(2,1)S(1)}, bf16[128,1024]{1,0:T(8,128)(2,1)S(1)}, u32[]{:S(2)}, u32[]{:S(2)}) collective-permute-start(bf16[128,1024]{1,0:T(8,128)(2,1)S(1)} %collective-permute-done.1.refs_4_), channel_id=1, source_target_pairs={{0,192},{16,208},{32,224},{48,240},{64,0},{80,16},{96,32},{112,48}... | collective-permute-start | bytes 786440 | tf_op jit(solution)/shard_map/ppermute | solution.py:239
  40.1 2.3 %collective-permute-start.9 = (bf16[128,1024]{1,0:T(8,128)(2,1)S(1)}, bf16[128,1024]{1,0:T(8,128)(2,1)S(1)}, u32[]{:S(2)}, u32[]{:S(2)}) collective-permute-start(bf16[128,1024]{1,0:T(8,128)(2,1)S(1)} %collective-permute-done.1.refs_4_), channel_id=1, source_target_pairs={{0,128},{16,144},{32,160},{48,176},{64,192},{80,208},{96,224},{112... | collective-permute-start | bytes 786440 | tf_op jit(solution)/shard_map/ppermute | solution.py:239
  42.4 1.3 %collective-permute-start.11 = (bf16[256,128]{1,0:T(8,128)(2,1)S(1)}, bf16[256,128]{1,0:T(8,128)(2,1)S(1)}, u32[]{:S(2)}, u32[]{:S(2)}) collective-permute-start(bf16[256,128]{1,0:T(8,128)(2,1)S(1)} %pad_maximum_fusion.refs_8_), channel_id=1, source_target_pairs={{0,1},{1,0},{2,3},{3,2},{4,5},{5,4},{6,7},{7,6},{8,9},{9,8},{10,11... | collective-permute-start | bytes 196616 | tf_op jit(solution)/shard_map/ppermute | solution.py:235
  44.3 10.3 %collective-permute-done.10.refs_7_ = bf16[128,1024]{1,0:T(8,128)(2,1)S(1)} collective-permute-done((bf16[128,1024]{1,0:T(8,128)(2,1)S(1)}, bf16[128,1024]{1,0:T(8,128)(2,1)S(1)}, u32[]{:S(2)}, u32[]{:S(2)}) %collective-permute-start.10) | collective-permute-done | bytes 262176 | tf_op jit(solution)/shard_map/ppermute | solution.py:239
  55.1 3.4 %all-to-all-done.qkv_ref = bf16[16,3,64,128]{3,2,1,0:T(8,128)(2,1)S(1)} async-done(((bf16[16,3,64,128]{3,2,1,0:T(8,128)(2,1)}), bf16[16,3,64,128]{3,2,1,0:T(8,128)(2,1)S(1)}, u32[]{:S(2)}, u32[]{:S(2)}) %all-to-all-start) | async-done | bytes 786464 | tf_op jit(solution)/shard_map/all_to_all | solution.py:271
  58.5 2.2 %forward.1 = (bf16[1024,128]{1,0:T(8,128)(2,1)S(1)}, f32[1024,1]{1,0:T(8,128)S(1)}) custom-call(bf16[16,3,64,128]{3,2,1,0:T(8,128)(2,1)S(1)} %all-to-all-done.qkv_ref), custom_call_target="tpu_custom_call" | custom-call | flops 536870912 | bytes 2097152 | tf_op jit(solution)/shard_map/forward/pallas_call | solution.py:132
  61.3 0.8 weight_term.1
  62.8 4.1 %backward.1 = bf16[16,3,64,128]{3,2,1,0:T(8,128)(2,1)} custom-call(bf16[16,3,64,128]{3,2,1,0:T(8,128)(2,1)S(1)} %all-to-all-done.qkv_ref, f32[1024,1]{1,0:T(8,128)S(1)} %get-tuple-element.25.lse_ref, bf16[128,1024]{1,0:T(8,128)(2,1)S(1)} %constant_dynamic-update-slice_fusion.refs_0_, bf16[128,1024]{1,0:T(8,128)(2,1)S(1)} %collective-permute-done.5.refs_1_, ...), custom_call_target="tpu_custom_call" | custom-call | flops 1610612736 | bytes 4194304 | tf_op jit(solution)/shard_map/backward/pallas_call | solution.py:163
  66.9 7.5 %all-to-all-start.1 = ((bf16[16,3,64,128]{3,2,1,0:T(8,128)(2,1)}), bf16[16,3,64,128]{3,2,1,0:T(8,128)(2,1)S(1)}, u32[]{:S(2)}, u32[]{:S(2)}) async-start(bf16[16,3,64,128]{3,2,1,0:T(8,128)(2,1)} %backward.1), calls=%async_computation.1 | async-start | bytes 1572864 | tf_op jit(solution)/shard_map/all_to_all | solution.py:290
  74.9 1.2 %collective-permute-done.14 = f32[64,1024]{1,0:T(8,128)S(1)} collective-permute-done((f32[64,1024]{1,0:T(8,128)S(1)}, f32[64,1024]{1,0:T(8,128)S(1)}, u32[]{:S(2)}, u32[]{:S(2)}) %collective-permute-start.14) | collective-permute-done | bytes 262176 | tf_op jit(solution)/shard_map/ppermute | solution.py:235
  76.2 1.4 %collective-permute-start.15 = (f32[4,4,1024]{2,1,0:T(4,128)S(1)}, f32[4,4,1024]{2,1,0:T(4,128)S(1)}, u32[]{:S(2)}, u32[]{:S(2)}) collective-permute-start(f32[4,4,1024]{2,1,0:T(4,128)S(1)} %get-tuple-element.34), channel_id=1, source_target_pairs={{0,1},{1,0},{2,3},{3,2},{4,5},{5,4},{6,7},{7,6},{8,9},{9,8},{10,11... | collective-permute-start | bytes 196616 | tf_op jit(solution)/shard_map/ppermute | solution.py:235
  78.2 1.6 %collective-permute-start.17 = (f32[4,4,1024]{2,1,0:T(4,128)S(1)}, f32[4,4,1024]{2,1,0:T(4,128)S(1)}, u32[]{:S(2)}, u32[]{:S(2)}) collective-permute-start(f32[4,4,1024]{2,1,0:T(4,128)S(1)} %get-tuple-element.35), channel_id=1, source_target_pairs={{0,3},{1,2},{2,1},{3,0},{4,7},{5,6},{6,5},{7,4},{8,11},{9,10},{10,... | collective-permute-start | bytes 196616 | tf_op jit(solution)/shard_map/ppermute | solution.py:235
  79.8 1.4 %collective-permute-done.15 = f32[4,4,1024]{2,1,0:T(4,128)S(1)} collective-permute-done((f32[4,4,1024]{2,1,0:T(4,128)S(1)}, f32[4,4,1024]{2,1,0:T(4,128)S(1)}, u32[]{:S(2)}, u32[]{:S(2)}) %collective-permute-start.15) | collective-permute-done | bytes 65568 | tf_op jit(solution)/shard_map/ppermute | solution.py:235
  81.2 2.2 %collective-permute-done.16 = f32[4,4,1024]{2,1,0:T(4,128)S(1)} collective-permute-done((f32[4,4,1024]{2,1,0:T(4,128)S(1)}, f32[4,4,1024]{2,1,0:T(4,128)S(1)}, u32[]{:S(2)}, u32[]{:S(2)}) %collective-permute-start.16) | collective-permute-done | bytes 65568 | tf_op jit(solution)/shard_map/ppermute | solution.py:235
  83.9 3.6 %collective-permute-start.18 = (f32[4,1024]{1,0:T(4,128)S(1)}, f32[4,1024]{1,0:T(4,128)S(1)}, u32[]{:S(2)}, u32[]{:S(2)}) collective-permute-start(f32[4,1024]{1,0:T(4,128)S(1)} %get-tuple-element.37), channel_id=1, source_target_pairs={{0,4},{1,5},{2,6},{3,7},{4,0},{5,1},{6,2},{7,3},{8,12},{9,13},{10,... | collective-permute-start | bytes 49160 | tf_op jit(solution)/shard_map/ppermute | solution.py:235
  88.0 1.0 %collective-permute-start.20 = (f32[4,1024]{1,0:T(4,128)S(1)}, f32[4,1024]{1,0:T(4,128)S(1)}, u32[]{:S(2)}, u32[]{:S(2)}) collective-permute-start(f32[4,1024]{1,0:T(4,128)S(1)} %get-tuple-element.38), channel_id=1, source_target_pairs={{0,12},{1,13},{2,14},{3,15},{4,8},{5,9},{6,10},{7,11},{8,4},{9,5},... | collective-permute-start | bytes 49160 | tf_op jit(solution)/shard_map/ppermute | solution.py:235
  89.1 7.7 %collective-permute-done.18 = f32[4,1024]{1,0:T(4,128)S(1)} collective-permute-done((f32[4,1024]{1,0:T(4,128)S(1)}, f32[4,1024]{1,0:T(4,128)S(1)}, u32[]{:S(2)}, u32[]{:S(2)}) %collective-permute-start.18) | collective-permute-done | bytes 16416 | tf_op jit(solution)/shard_map/ppermute | solution.py:235
  98.6 2.1 %all-to-all-done.1.in_ref = bf16[16,3,64,128]{3,2,1,0:T(8,128)(2,1)S(1)} async-done(((bf16[16,3,64,128]{3,2,1,0:T(8,128)(2,1)}), bf16[16,3,64,128]{3,2,1,0:T(8,128)(2,1)S(1)}, u32[]{:S(2)}, u32[]{:S(2)}) %all-to-all-start.1) | async-done | bytes 786464 | tf_op jit(solution)/shard_map/all_to_all | solution.py:290
  100.7 0.9 copy-done.3
  101.6 2.2 %unpack.1 = (bf16[64,2,1024]{2,1,0:T(2,128)(2,1)}, bf16[64,2,1024]{2,1,0:T(2,128)(2,1)}, bf16[64,2,1024]{2,1,0:T(2,128)(2,1)}) custom-call(bf16[16,3,64,128]{3,2,1,0:T(8,128)(2,1)} %copy-done.3), custom_call_target="tpu_custom_call" | custom-call | tf_op jit(solution)/shard_map/unpack/pallas_call | solution.py:229
  (37 shorter events, 7.7 us)
Async XLA Ops:
  0.6 16.2 %copy-start = (bf16[1024,64]{0,1:T(8,128)(2,1)S(1)}, bf16[1024,64]{0,1:T(8,128)(2,1)}, u32[]{:S(2)}) copy-start(bf16[1024,64]{0,1:T(8,128)(2,1)} %param.9) | copy-start | bytes 393220
  3.2 1.6 %collective-permute-start = (bf16[64,1024]{1,0:T(8,128)(2,1)}, bf16[64,1024]{1,0:T(8,128)(2,1)S(1)}, u32[]{:S(2)}, u32[]{:S(2)}) collective-permute-start(bf16[64,1024]{1,0:T(8,128)(2,1)} %get-tuple-element.19), channel_id=1, source_target_pairs={{0,16},{16,0},{32,48},{48,32},{64,80},{80,64},{96,112},{112,96},{1... | collective-permute-start | bytes 393224 | tf_op jit(solution)/shard_map/ppermute | solution.py:235
  4.8 27.3 %collective-permute-start.1 = (bf16[128,1024]{1,0:T(8,128)(2,1)S(1)}, bf16[128,1024]{1,0:T(8,128)(2,1)S(1)}, u32[]{:S(2)}, u32[]{:S(2)}) collective-permute-start(bf16[128,1024]{1,0:T(8,128)(2,1)S(1)} %constant_dynamic-update-slice_fusion.refs_0_), channel_id=1, source_target_pairs={{0,32},{16,48},{32,0},{48,16},{64,96},{80,112},{96,64},{112,80},{1... | collective-permute-start | bytes 786440 | tf_op jit(solution)/shard_map/ppermute | solution.py:235
  11.2 21.0 %collective-permute-start.5 = (bf16[128,1024]{1,0:T(8,128)(2,1)S(1)}, bf16[128,1024]{1,0:T(8,128)(2,1)S(1)}, u32[]{:S(2)}, u32[]{:S(2)}) collective-permute-start(bf16[128,1024]{1,0:T(8,128)(2,1)S(1)} %constant_dynamic-update-slice_fusion.refs_0_), channel_id=1, source_target_pairs={{0,64},{16,80},{32,96},{48,112},{64,128},{80,144},{96,160},{112,17... | collective-permute-start | bytes 786440 | tf_op jit(solution)/shard_map/ppermute | solution.py:239
  12.7 19.5 %collective-permute-start.6 = (bf16[128,1024]{1,0:T(8,128)(2,1)S(1)}, bf16[128,1024]{1,0:T(8,128)(2,1)S(1)}, u32[]{:S(2)}, u32[]{:S(2)}) collective-permute-start(bf16[128,1024]{1,0:T(8,128)(2,1)S(1)} %constant_dynamic-update-slice_fusion.refs_0_), channel_id=1, source_target_pairs={{0,128},{16,144},{32,160},{48,176},{64,192},{80,208},{96,224},{112... | collective-permute-start | bytes 786440 | tf_op jit(solution)/shard_map/ppermute | solution.py:239
  15.4 16.8 %collective-permute-start.7 = (bf16[128,1024]{1,0:T(8,128)(2,1)S(1)}, bf16[128,1024]{1,0:T(8,128)(2,1)S(1)}, u32[]{:S(2)}, u32[]{:S(2)}) collective-permute-start(bf16[128,1024]{1,0:T(8,128)(2,1)S(1)} %constant_dynamic-update-slice_fusion.refs_0_), channel_id=1, source_target_pairs={{0,192},{16,208},{32,224},{48,240},{64,0},{80,16},{96,32},{112,48}... | collective-permute-start | bytes 786440 | tf_op jit(solution)/shard_map/ppermute | solution.py:239
  16.8 6.9 %collective-permute-start.2 = (bf16[64,128]{1,0:T(8,128)(2,1)S(1)}, bf16[64,128]{1,0:T(8,128)(2,1)S(1)}, u32[]{:S(2)}, u32[]{:S(2)}) collective-permute-start(bf16[64,128]{1,0:T(8,128)(2,1)S(1)} %dynamic-slice_bitcast_fusion.6), channel_id=1, source_target_pairs={{0,4},{1,5},{2,6},{3,7},{4,0},{5,1},{6,2},{7,3},{8,12},{9,13},{10,... | collective-permute-start | bytes 49160 | tf_op jit(solution)/shard_map/ppermute | solution.py:235
  23.7 4.6 %collective-permute-start.3 = (bf16[64,128]{1,0:T(8,128)(2,1)S(1)}, bf16[64,128]{1,0:T(8,128)(2,1)S(1)}, u32[]{:S(2)}, u32[]{:S(2)}) collective-permute-start(bf16[64,128]{1,0:T(8,128)(2,1)S(1)} %dynamic-slice_bitcast_fusion.6), channel_id=1, source_target_pairs={{0,8},{1,9},{2,10},{3,11},{4,12},{5,13},{6,14},{7,15},{8,0},{9,1},... | collective-permute-start | bytes 49160 | tf_op jit(solution)/shard_map/ppermute | solution.py:235
  28.4 3.7 %collective-permute-start.4 = (bf16[64,128]{1,0:T(8,128)(2,1)S(1)}, bf16[64,128]{1,0:T(8,128)(2,1)S(1)}, u32[]{:S(2)}, u32[]{:S(2)}) collective-permute-start(bf16[64,128]{1,0:T(8,128)(2,1)S(1)} %dynamic-slice_bitcast_fusion.6), channel_id=1, source_target_pairs={{0,12},{1,13},{2,14},{3,15},{4,8},{5,9},{6,10},{7,11},{8,4},{9,5},... | collective-permute-start | bytes 49160 | tf_op jit(solution)/shard_map/ppermute | solution.py:235
  32.2 26.3 %all-to-all-start = ((bf16[16,3,64,128]{3,2,1,0:T(8,128)(2,1)}), bf16[16,3,64,128]{3,2,1,0:T(8,128)(2,1)S(1)}, u32[]{:S(2)}, u32[]{:S(2)}) async-start(bf16[16,3,64,128]{3,2,1,0:T(8,128)(2,1)} %get-tuple-element.20), calls=%async_computation | async-start | bytes 1572864 | tf_op jit(solution)/shard_map/all_to_all | solution.py:271
  37.0 17.6 %collective-permute-start.10 = (bf16[128,1024]{1,0:T(8,128)(2,1)S(1)}, bf16[128,1024]{1,0:T(8,128)(2,1)S(1)}, u32[]{:S(2)}, u32[]{:S(2)}) collective-permute-start(bf16[128,1024]{1,0:T(8,128)(2,1)S(1)} %collective-permute-done.1.refs_4_), channel_id=1, source_target_pairs={{0,192},{16,208},{32,224},{48,240},{64,0},{80,16},{96,32},{112,48}... | collective-permute-start | bytes 786440 | tf_op jit(solution)/shard_map/ppermute | solution.py:239
  40.1 20.6 %collective-permute-start.8 = (bf16[128,1024]{1,0:T(8,128)(2,1)S(1)}, bf16[128,1024]{1,0:T(8,128)(2,1)S(1)}, u32[]{:S(2)}, u32[]{:S(2)}) collective-permute-start(bf16[128,1024]{1,0:T(8,128)(2,1)S(1)} %collective-permute-done.1.refs_4_), channel_id=1, source_target_pairs={{0,64},{16,80},{32,96},{48,112},{64,128},{80,144},{96,160},{112,17... | collective-permute-start | bytes 786440 | tf_op jit(solution)/shard_map/ppermute | solution.py:239
  40.1 21.2 %collective-permute-start.9 = (bf16[128,1024]{1,0:T(8,128)(2,1)S(1)}, bf16[128,1024]{1,0:T(8,128)(2,1)S(1)}, u32[]{:S(2)}, u32[]{:S(2)}) collective-permute-start(bf16[128,1024]{1,0:T(8,128)(2,1)S(1)} %collective-permute-done.1.refs_4_), channel_id=1, source_target_pairs={{0,128},{16,144},{32,160},{48,176},{64,192},{80,208},{96,224},{112... | collective-permute-start | bytes 786440 | tf_op jit(solution)/shard_map/ppermute | solution.py:239
  42.4 20.4 %collective-permute-start.11 = (bf16[256,128]{1,0:T(8,128)(2,1)S(1)}, bf16[256,128]{1,0:T(8,128)(2,1)S(1)}, u32[]{:S(2)}, u32[]{:S(2)}) collective-permute-start(bf16[256,128]{1,0:T(8,128)(2,1)S(1)} %pad_maximum_fusion.refs_8_), channel_id=1, source_target_pairs={{0,1},{1,0},{2,3},{3,2},{4,5},{5,4},{6,7},{7,6},{8,9},{9,8},{10,11... | collective-permute-start | bytes 196616 | tf_op jit(solution)/shard_map/ppermute | solution.py:235
  43.7 19.1 %collective-permute-start.12 = (bf16[256,128]{1,0:T(8,128)(2,1)S(1)}, bf16[256,128]{1,0:T(8,128)(2,1)S(1)}, u32[]{:S(2)}, u32[]{:S(2)}) collective-permute-start(bf16[256,128]{1,0:T(8,128)(2,1)S(1)} %pad_maximum_fusion.refs_8_), channel_id=1, source_target_pairs={{0,2},{1,3},{2,0},{3,1},{4,6},{5,7},{6,4},{7,5},{8,10},{9,11},{10,... | collective-permute-start | bytes 196616 | tf_op jit(solution)/shard_map/ppermute | solution.py:235
  54.6 8.2 %collective-permute-start.13 = (bf16[256,128]{1,0:T(8,128)(2,1)S(1)}, bf16[256,128]{1,0:T(8,128)(2,1)S(1)}, u32[]{:S(2)}, u32[]{:S(2)}) collective-permute-start(bf16[256,128]{1,0:T(8,128)(2,1)S(1)} %pad_maximum_fusion.refs_8_), channel_id=1, source_target_pairs={{0,3},{1,2},{2,1},{3,0},{4,7},{5,6},{6,5},{7,4},{8,11},{9,10},{10,... | collective-permute-start | bytes 196616 | tf_op jit(solution)/shard_map/ppermute | solution.py:235
  62.1 0.7 copy-start.1
  66.9 7.5 %copy-start.2 = (f32[64,1024]{1,0:T(8,128)S(1)}, f32[64,1024]{1,0:T(8,128)}, u32[]{:S(2)}) copy-start(f32[64,1024]{1,0:T(8,128)} %copy-done.1) | copy-start | bytes 786436
  66.9 33.8 %all-to-all-start.1 = ((bf16[16,3,64,128]{3,2,1,0:T(8,128)(2,1)}), bf16[16,3,64,128]{3,2,1,0:T(8,128)(2,1)S(1)}, u32[]{:S(2)}, u32[]{:S(2)}) async-start(bf16[16,3,64,128]{3,2,1,0:T(8,128)(2,1)} %backward.1), calls=%async_computation.1 | async-start | bytes 1572864 | tf_op jit(solution)/shard_map/all_to_all | solution.py:290
  74.4 1.7 %collective-permute-start.14 = (f32[64,1024]{1,0:T(8,128)S(1)}, f32[64,1024]{1,0:T(8,128)S(1)}, u32[]{:S(2)}, u32[]{:S(2)}) collective-permute-start(f32[64,1024]{1,0:T(8,128)S(1)} %copy-done.2), channel_id=1, source_target_pairs={{0,16},{16,0},{32,48},{48,32},{64,80},{80,64},{96,112},{112,96},{1... | collective-permute-start | bytes 786440 | tf_op jit(solution)/shard_map/ppermute | solution.py:235
  76.2 5.0 %collective-permute-start.15 = (f32[4,4,1024]{2,1,0:T(4,128)S(1)}, f32[4,4,1024]{2,1,0:T(4,128)S(1)}, u32[]{:S(2)}, u32[]{:S(2)}) collective-permute-start(f32[4,4,1024]{2,1,0:T(4,128)S(1)} %get-tuple-element.34), channel_id=1, source_target_pairs={{0,1},{1,0},{2,3},{3,2},{4,5},{5,4},{6,7},{7,6},{8,9},{9,8},{10,11... | collective-permute-start | bytes 196616 | tf_op jit(solution)/shard_map/ppermute | solution.py:235
  77.6 5.8 %collective-permute-start.16 = (f32[4,4,1024]{2,1,0:T(4,128)S(1)}, f32[4,4,1024]{2,1,0:T(4,128)S(1)}, u32[]{:S(2)}, u32[]{:S(2)}) collective-permute-start(f32[4,4,1024]{2,1,0:T(4,128)S(1)} %get-tuple-element.36), channel_id=1, source_target_pairs={{0,2},{1,3},{2,0},{3,1},{4,6},{5,7},{6,4},{7,5},{8,10},{9,11},{10,... | collective-permute-start | bytes 196616 | tf_op jit(solution)/shard_map/ppermute | solution.py:235
  78.2 5.7 %collective-permute-start.17 = (f32[4,4,1024]{2,1,0:T(4,128)S(1)}, f32[4,4,1024]{2,1,0:T(4,128)S(1)}, u32[]{:S(2)}, u32[]{:S(2)}) collective-permute-start(f32[4,4,1024]{2,1,0:T(4,128)S(1)} %get-tuple-element.35), channel_id=1, source_target_pairs={{0,3},{1,2},{2,1},{3,0},{4,7},{5,6},{6,5},{7,4},{8,11},{9,10},{10,... | collective-permute-start | bytes 196616 | tf_op jit(solution)/shard_map/ppermute | solution.py:235
  83.9 12.8 %collective-permute-start.18 = (f32[4,1024]{1,0:T(4,128)S(1)}, f32[4,1024]{1,0:T(4,128)S(1)}, u32[]{:S(2)}, u32[]{:S(2)}) collective-permute-start(f32[4,1024]{1,0:T(4,128)S(1)} %get-tuple-element.37), channel_id=1, source_target_pairs={{0,4},{1,5},{2,6},{3,7},{4,0},{5,1},{6,2},{7,3},{8,12},{9,13},{10,... | collective-permute-start | bytes 49160 | tf_op jit(solution)/shard_map/ppermute | solution.py:235
  87.5 10.0 %collective-permute-start.19 = (f32[4,1024]{1,0:T(4,128)S(1)}, f32[4,1024]{1,0:T(4,128)S(1)}, u32[]{:S(2)}, u32[]{:S(2)}) collective-permute-start(f32[4,1024]{1,0:T(4,128)S(1)} %get-tuple-element.39), channel_id=1, source_target_pairs={{0,8},{1,9},{2,10},{3,11},{4,12},{5,13},{6,14},{7,15},{8,0},{9,1},... | collective-permute-start | bytes 49160 | tf_op jit(solution)/shard_map/ppermute | solution.py:235
  88.0 9.9 %collective-permute-start.20 = (f32[4,1024]{1,0:T(4,128)S(1)}, f32[4,1024]{1,0:T(4,128)S(1)}, u32[]{:S(2)}, u32[]{:S(2)}) collective-permute-start(f32[4,1024]{1,0:T(4,128)S(1)} %get-tuple-element.38), channel_id=1, source_target_pairs={{0,12},{1,13},{2,14},{3,15},{4,8},{5,9},{6,10},{7,11},{8,4},{9,5},... | collective-permute-start | bytes 49160 | tf_op jit(solution)/shard_map/ppermute | solution.py:235
  100.7 0.9 copy-start.3

commit v3 on v2

--- a/solution.py
+++ b/solution.py
@@ -199,6 +199,12 @@
                 ]
 
 
+def split_scores_kernel(rows_ref, mine_ref, other_ref):
+    parts = dot(shuffle(False, lax.axis_index("tm") % 2), rows_ref[...].reshape(2 * BLOCK, -1), 1, 0)
+    mine_ref[...] = parts[:BLOCK].astype(jnp.bfloat16)
+    other_ref[...] = parts[BLOCK:].astype(jnp.bfloat16)
+
+
 def unpack_kernel(in_ref, query_ref, key_ref, value_ref):
     move = shuffle(True, 0)
     for a, ref in enumerate((query_ref, key_ref, value_ref)):
@@ -224,6 +230,13 @@
     )(query, key, value, grad)
 
 
+def split_scores(rows):
+    half = jax.ShapeDtypeStruct((rows.shape[0], rows.shape[2]), rows.dtype)
+    return pl.pallas_call(
+        split_scores_kernel, out_shape=(half, half), in_specs=[VMEM], out_specs=(VMEM, VMEM), name="split_scores"
+    )(rows)
+
+
 def unpack(items):
     rows = jax.ShapeDtypeStruct((BLOCK, 2, HEADS * HEAD), items.dtype)
     return pl.pallas_call(
@@ -252,30 +265,37 @@
 
     qkv, mine, other = prepare(*(a.reshape(flat) for a in (query_rows, key_rows, value_rows, grad_output)))
     chip_piece = jnp.concatenate([mine, swap(other, "tm", 1)], axis=0)
-    far_piece = swap(chip_piece, "tm", 2)
-    places, pieces = [], []
-    for d in range(4):
-        places.append((0, d))
-        pieces.append(shift(chip_piece, d) if d else chip_piece)
-    for d in range(4):
-        places.append((1, d))
-        pieces.append(shift(far_piece, d) if d else far_piece)
+    far_rows = swap(grad_output.reshape(flat), "tm", 2)
+    places = [(far, back) for far in range(2) for back in range(4)]
+    shifted = {2: shift(chip_piece, 2), 1: shift(chip_piece, 1), 3: shift(chip_piece, 3)}
+    pieces = [chip_piece] + [shifted[d] for d in (1, 2, 3)]
+    far_mine, far_other = split_scores(far_rows)
+    far_piece = jnp.concatenate([far_mine, swap(far_other, "tm", 1)], axis=0)
+    shifted = {2: shift(far_piece, 2), 1: shift(far_piece, 1), 3: shift(far_piece, 3)}
+    pieces += [far_piece] + [shifted[d] for d in (1, 2, 3)]
 
     held = lax.dynamic_slice_in_dim(out_weight.T, head * HEAD, HEAD, axis=1)
-    held = jnp.concatenate([held] + [swap(held, "track", 4 * j) for j in (1, 2, 3)], axis=0)
+    held, _ = lax.optimization_barrier((held, chip_piece))
+    for mask in (4, 8):
+        held = jnp.concatenate([held, swap(held, "track", mask)], axis=0)
+
     held_z = held
-    held, _ = lax.optimization_barrier((held, far_piece))
+    held, _ = lax.optimization_barrier((held, far_rows))
     weight = [held] + [swap(held, "track", j) for j in (1, 2, 3)]
 
-    qkv, _ = lax.optimization_barrier((qkv, (far_piece, held_z, pieces[1], pieces[2], pieces[3])))
+    qkv, _ = lax.optimization_barrier((qkv, (far_rows, held_z, pieces[1], pieces[2], pieces[3])))
     qkv = lax.all_to_all(qkv, "tm", split_axis=0, concat_axis=0, tiled=True)
 
+    qkv, _ = lax.optimization_barrier((qkv, weight))
     att, lse = forward(qkv)
     keep, send = weight_term(att, places, pieces, norm_factor)
     lse, _ = lax.optimization_barrier((lse, (keep, send)))
 
-    total = keep + swap(send, "tm", 1)
-    after_core = total
+    item_grads = backward(qkv, lse, places, pieces, weight)
+
+    from_core = swap(send, "tm", 1)
+    item_grads, from_core = lax.optimization_barrier((item_grads, from_core))
+    total = keep + from_core
     total = total.reshape(4, 4, 4, model_width)
     for axis, step, place in ((1, 1, track % 4), (0, 4, track // 4)):
         parts = [lax.dynamic_index_in_dim(total, place ^ j, axis, keepdims=False) for j in range(4)]
@@ -286,7 +306,7 @@
             after_y = total
     grad_weight = total
 
-    item_grads = backward(qkv, lse, places, pieces, weight)
+
     returned = lax.all_to_all(item_grads, "tm", split_axis=0, concat_axis=0, tiled=True)
     shape = query_rows.shape
     grad_query, grad_key, grad_value = (g.reshape(shape) for g in unpack(returned))

time: 105 us -> 100 us (0.952)
  starting transfers between devices: 45.1 us -> 40.3 us
  waiting for transfers between devices: 42.7 us -> 40.1 us
  Pallas kernels: 11.9 us -> 13.8 us
    ppermute x6, waiting for transfers between devices: 10.8 us -> 3.78 us  [shift(): lax.ppermute(array, 'tm', [(i, (i + 4 * by) % 16) for i in range(16)])]
    all_to_all x1, waiting for transfers between devices: 3.45 us -> 7.94 us  [local(): qkv = lax.all_to_all(qkv, 'tm', split_axis=0, concat_axis=0, tiled=True)]
    all_to_all x1, starting transfers between devices: 7.47 us -> 4.13 us  [local(): lax.all_to_all(item_grads, 'tm', split_axis=0, concat_axis=0, tiled=True)]
    pallas_call x0 -> x1, Pallas kernels: none -> 1.86 us  [split_scores(): pl.pallas_call(split_scores_kernel, out_shape=(half, half), in_specs=[VME...]
    ppermute x15, starting transfers between devices: 21.7 us -> 20.4 us  [swap(): return lax.ppermute(array, axis, [(i, i ^ mask) for i in range(16)])]
    unnamed x9 -> x10, local copies, waits for them, and re-layouts: 2.53 us -> 2.76 us
  transfers between devices with their start and end apart: 23 -> 23, of which waited for: 15 -> 15; matrix products, arithmetic and copies ran while one was open for 2% -> 4% of each run, Pallas kernels for 3% -> 11%
where the time goes in v3:
time: 100 us; the launch traced here: 99.6 us
  starting transfers between devices  40.3 us (40%)
  waiting for transfers between devices  40.1 us (40%)
  Pallas kernels  13.8 us (14%)
  local copies, waits for them, and re-layouts  2.91 us (3%)
  other arithmetic  1.63 us (2%)
    ppermute x15, waiting for transfers between devices, swap(): return lax.ppermute(array, axis, [(i, i ^ mask) for i in range(16)])  26.2 us
    ppermute x15, starting transfers between devices, swap(): return lax.ppermute(array, axis, [(i, i ^ mask) for i in range(16)])  20.4 us
    ppermute x6, starting transfers between devices, shift(): lax.ppermute(array, 'tm', [(i, (i + 4 * by) % 16) for i in range(16)])  11.7 us
    all_to_all x1, waiting for transfers between devices, local(): qkv = lax.all_to_all(qkv, 'tm', split_axis=0, concat_axis=0, tiled=True)  7.94 us
    all_to_all x1, starting transfers between devices, local(): lax.all_to_all(item_grads, 'tm', split_axis=0, concat_axis=0, tiled=True)  4.13 us
    pallas_call x1, Pallas kernels, backward(): pl.pallas_call(functools.partial(backward_kernel, places), out_shape=jax....  4.11 us
    all_to_all x1, starting transfers between devices, local(): qkv = lax.all_to_all(qkv, 'tm', split_axis=0, concat_axis=0, tiled=True)  4.04 us
    ppermute x6, waiting for transfers between devices, shift(): lax.ppermute(array, 'tm', [(i, (i + 4 * by) % 16) for i in range(16)])  3.78 us
  transfers between devices with their start and end apart: 23, of which 15 were waited for; matrix products, arithmetic and copies ran while one was open for 4% of the time, Pallas kernels for 11%

profile of v3, /device:TPU:48, one launch (start us, length us, event | category | flops | bytes accessed | tf_op | source)
XLA Modules:
  0.0 99.6 jit_solution(17736303711238426970)
XLA Ops:
  0.6 6.4 %collective-permute-start = (bf16[64,2,1024]{2,1,0:T(2,128)(2,1)}, bf16[64,2,1024]{2,1,0:T(2,128)(2,1)S(1)}, u32[]{:S(2)}, u32[]{:S(2)}) collective-permute-start(bf16[64,2,1024]{2,1,0:T(2,128)(2,1)} %bitcast.42), channel_id=1, source_target_pairs={{0,32},{16,48},{32,0},{48,16},{64,96},{80,112},{96,64},{112,80},{1... | collective-permute-start | bytes 786440 | tf_op jit(solution)/shard_map/ppermute | solution.py:248
  7.0 2.5 %prepare.1 = (bf16[16,3,64,128]{3,2,1,0:T(8,128)(2,1)}, bf16[64,1024]{1,0:T(8,128)(2,1)}, bf16[64,1024]{1,0:T(8,128)(2,1)}) custom-call(bf16[64,2,1024]{2,1,0:T(2,128)(2,1)} %bitcast.39, bf16[64,2,1024]{2,1,0:T(2,128)(2,1)} %bitcast.40, bf16[64,2,1024]{2,1,0:T(2,128)(2,1)} %bitcast.41, bf16[64,2,1024]{2,1,0:T(2,128)(2,1)} %bitcast.43), custom_call_target="tpu_custom_call" | custom-call | tf_op jit(solution)/shard_map/prepare/pallas_call | solution.py:224
  11.1 1.1 %collective-permute-start.2 = (bf16[64,128]{1,0:T(8,128)(2,1)S(1)}, bf16[64,128]{1,0:T(8,128)(2,1)S(1)}, u32[]{:S(2)}, u32[]{:S(2)}) collective-permute-start(bf16[64,128]{1,0:T(8,128)(2,1)S(1)} %dynamic-slice_bitcast_fusion.6), channel_id=1, source_target_pairs={{0,4},{1,5},{2,6},{3,7},{4,0},{5,1},{6,2},{7,3},{8,12},{9,13},{10,... | collective-permute-start | bytes 49160 | tf_op jit(solution)/shard_map/ppermute | solution.py:248
  12.2 1.5 %collective-permute-start.4 = (bf16[128,1024]{1,0:T(8,128)(2,1)S(1)}, bf16[128,1024]{1,0:T(8,128)(2,1)S(1)}, u32[]{:S(2)}, u32[]{:S(2)}) collective-permute-start(bf16[128,1024]{1,0:T(8,128)(2,1)S(1)} %constant_dynamic-update-slice_fusion.refs_0_), channel_id=1, source_target_pairs={{0,64},{16,80},{32,96},{48,112},{64,128},{80,144},{96,160},{112,17... | collective-permute-start | bytes 786440 | tf_op jit(solution)/shard_map/ppermute | solution.py:252
  13.7 2.7 %collective-permute-start.5 = (bf16[128,1024]{1,0:T(8,128)(2,1)S(1)}, bf16[128,1024]{1,0:T(8,128)(2,1)S(1)}, u32[]{:S(2)}, u32[]{:S(2)}) collective-permute-start(bf16[128,1024]{1,0:T(8,128)(2,1)S(1)} %constant_dynamic-update-slice_fusion.refs_0_), channel_id=1, source_target_pairs={{0,128},{16,144},{32,160},{48,176},{64,192},{80,208},{96,224},{112... | collective-permute-start | bytes 786440 | tf_op jit(solution)/shard_map/ppermute | solution.py:252
  16.4 1.4 %collective-permute-start.6 = (bf16[128,1024]{1,0:T(8,128)(2,1)S(1)}, bf16[128,1024]{1,0:T(8,128)(2,1)S(1)}, u32[]{:S(2)}, u32[]{:S(2)}) collective-permute-start(bf16[128,1024]{1,0:T(8,128)(2,1)S(1)} %constant_dynamic-update-slice_fusion.refs_0_), channel_id=1, source_target_pairs={{0,192},{16,208},{32,224},{48,240},{64,0},{80,16},{96,32},{112,48}... | collective-permute-start | bytes 786440 | tf_op jit(solution)/shard_map/ppermute | solution.py:252
  17.9 1.6 %collective-permute-done.2 = bf16[64,128]{1,0:T(8,128)(2,1)S(1)} collective-permute-done((bf16[64,128]{1,0:T(8,128)(2,1)S(1)}, bf16[64,128]{1,0:T(8,128)(2,1)S(1)}, u32[]{:S(2)}, u32[]{:S(2)}) %collective-permute-start.2) | collective-permute-done | bytes 16416 | tf_op jit(solution)/shard_map/ppermute | solution.py:248
  19.5 2.0 %collective-permute-start.3 = (bf16[128,128]{1,0:T(8,128)(2,1)S(1)}, bf16[128,128]{1,0:T(8,128)(2,1)S(1)}, u32[]{:S(2)}, u32[]{:S(2)}) collective-permute-start(bf16[128,128]{1,0:T(8,128)(2,1)S(1)} %pad_maximum_fusion), channel_id=1, source_target_pairs={{0,8},{1,9},{2,10},{3,11},{4,12},{5,13},{6,14},{7,15},{8,0},{9,1},... | collective-permute-start | bytes 98312 | tf_op jit(solution)/shard_map/ppermute | solution.py:248
  21.6 2.8 %collective-permute-done.3 = bf16[128,128]{1,0:T(8,128)(2,1)S(1)} collective-permute-done((bf16[128,128]{1,0:T(8,128)(2,1)S(1)}, bf16[128,128]{1,0:T(8,128)(2,1)S(1)}, u32[]{:S(2)}, u32[]{:S(2)}) %collective-permute-start.3) | collective-permute-done | bytes 32800 | tf_op jit(solution)/shard_map/ppermute | solution.py:248
  24.3 3.8 %collective-permute-done.5.refs_2_ = bf16[128,1024]{1,0:T(8,128)(2,1)S(1)} collective-permute-done((bf16[128,1024]{1,0:T(8,128)(2,1)S(1)}, bf16[128,1024]{1,0:T(8,128)(2,1)S(1)}, u32[]{:S(2)}, u32[]{:S(2)}) %collective-permute-start.5) | collective-permute-done | bytes 262176 | tf_op jit(solution)/shard_map/ppermute | solution.py:252
  28.1 4.0 %all-to-all-start = ((bf16[16,3,64,128]{3,2,1,0:T(8,128)(2,1)}), bf16[16,3,64,128]{3,2,1,0:T(8,128)(2,1)S(1)}, u32[]{:S(2)}, u32[]{:S(2)}) async-start(bf16[16,3,64,128]{3,2,1,0:T(8,128)(2,1)} %get-tuple-element.27), calls=%async_computation | async-start | bytes 1572864 | tf_op jit(solution)/shard_map/all_to_all | solution.py:287
  32.2 1.9 %split_scores.1 = (bf16[64,1024]{1,0:T(8,128)(2,1)}, bf16[64,1024]{1,0:T(8,128)(2,1)}) custom-call(bf16[64,2,1024]{2,1,0:T(2,128)(2,1)} %copy-done.2), custom_call_target="tpu_custom_call" | custom-call | tf_op jit(solution)/shard_map/split_scores/pallas_call | solution.py:235
  35.6 2.0 %collective-permute-start.11 = (bf16[128,1024]{1,0:T(8,128)(2,1)S(1)}, bf16[128,1024]{1,0:T(8,128)(2,1)S(1)}, u32[]{:S(2)}, u32[]{:S(2)}) collective-permute-start(bf16[128,1024]{1,0:T(8,128)(2,1)S(1)} %constant_dynamic-update-slice_fusion.5.refs_4_), channel_id=1, source_target_pairs={{0,64},{16,80},{32,96},{48,112},{64,128},{80,144},{96,160},{112,17... | collective-permute-start | bytes 786440 | tf_op jit(solution)/shard_map/ppermute | solution.py:252
  37.6 2.7 %collective-permute-start.12 = (bf16[128,1024]{1,0:T(8,128)(2,1)S(1)}, bf16[128,1024]{1,0:T(8,128)(2,1)S(1)}, u32[]{:S(2)}, u32[]{:S(2)}) collective-permute-start(bf16[128,1024]{1,0:T(8,128)(2,1)S(1)} %constant_dynamic-update-slice_fusion.5.refs_4_), channel_id=1, source_target_pairs={{0,128},{16,144},{32,160},{48,176},{64,192},{80,208},{96,224},{112... | collective-permute-start | bytes 786440 | tf_op jit(solution)/shard_map/ppermute | solution.py:252
  40.3 1.5 %collective-permute-start.13 = (bf16[128,1024]{1,0:T(8,128)(2,1)S(1)}, bf16[128,1024]{1,0:T(8,128)(2,1)S(1)}, u32[]{:S(2)}, u32[]{:S(2)}) collective-permute-start(bf16[128,1024]{1,0:T(8,128)(2,1)S(1)} %constant_dynamic-update-slice_fusion.5.refs_4_), channel_id=1, source_target_pairs={{0,192},{16,208},{32,224},{48,240},{64,0},{80,16},{96,32},{112,48}... | collective-permute-start | bytes 786440 | tf_op jit(solution)/shard_map/ppermute | solution.py:252
  41.7 1.3 %collective-permute-start.7 = (bf16[256,128]{1,0:T(8,128)(2,1)S(1)}, bf16[256,128]{1,0:T(8,128)(2,1)S(1)}, u32[]{:S(2)}, u32[]{:S(2)}) collective-permute-start(bf16[256,128]{1,0:T(8,128)(2,1)S(1)} %constant_dynamic-update-slice_fusion.2.refs_8_), channel_id=1, source_target_pairs={{0,1},{1,0},{2,3},{3,2},{4,5},{5,4},{6,7},{7,6},{8,9},{9,8},{10,11... | collective-permute-start | bytes 196616 | tf_op jit(solution)/shard_map/ppermute | solution.py:248
  43.7 2.4 %collective-permute-done.7.refs_9_ = bf16[256,128]{1,0:T(8,128)(2,1)S(1)} collective-permute-done((bf16[256,128]{1,0:T(8,128)(2,1)S(1)}, bf16[256,128]{1,0:T(8,128)(2,1)S(1)}, u32[]{:S(2)}, u32[]{:S(2)}) %collective-permute-start.7) | collective-permute-done | bytes 65568 | tf_op jit(solution)/shard_map/ppermute | solution.py:248
  46.5 2.3 %collective-permute-done.8.refs_10_ = bf16[256,128]{1,0:T(8,128)(2,1)S(1)} collective-permute-done((bf16[256,128]{1,0:T(8,128)(2,1)S(1)}, bf16[256,128]{1,0:T(8,128)(2,1)S(1)}, u32[]{:S(2)}, u32[]{:S(2)}) %collective-permute-start.8) | collective-permute-done | bytes 65568 | tf_op jit(solution)/shard_map/ppermute | solution.py:248
  48.8 1.5 %collective-permute-done.9.refs_11_ = bf16[256,128]{1,0:T(8,128)(2,1)S(1)} collective-permute-done((bf16[256,128]{1,0:T(8,128)(2,1)S(1)}, bf16[256,128]{1,0:T(8,128)(2,1)S(1)}, u32[]{:S(2)}, u32[]{:S(2)}) %collective-permute-start.9) | collective-permute-done | bytes 65568 | tf_op jit(solution)/shard_map/ppermute | solution.py:248
  50.3 7.9 %all-to-all-done.qkv_ref = bf16[16,3,64,128]{3,2,1,0:T(8,128)(2,1)S(1)} async-done(((bf16[16,3,64,128]{3,2,1,0:T(8,128)(2,1)}), bf16[16,3,64,128]{3,2,1,0:T(8,128)(2,1)S(1)}, u32[]{:S(2)}, u32[]{:S(2)}) %all-to-all-start) | async-done | bytes 786464 | tf_op jit(solution)/shard_map/all_to_all | solution.py:287
  58.2 2.2 %forward.1 = (bf16[1024,128]{1,0:T(8,128)(2,1)S(1)}, f32[1024,1]{1,0:T(8,128)S(1)}) custom-call(bf16[16,3,64,128]{3,2,1,0:T(8,128)(2,1)S(1)} %all-to-all-done.qkv_ref), custom_call_target="tpu_custom_call" | custom-call | flops 536870912 | bytes 2097152 | tf_op jit(solution)/shard_map/forward/pallas_call | solution.py:132
  61.6 4.1 %backward.1 = bf16[16,3,64,128]{3,2,1,0:T(8,128)(2,1)} custom-call(bf16[16,3,64,128]{3,2,1,0:T(8,128)(2,1)S(1)} %all-to-all-done.qkv_ref, f32[1024,1]{1,0:T(8,128)S(1)} %get-tuple-element.36.lse_ref, bf16[128,1024]{1,0:T(8,128)(2,1)S(1)} %constant_dynamic-update-slice_fusion.refs_0_, bf16[128,1024]{1,0:T(8,128)(2,1)S(1)} %collective-permute-done.4.refs_1_, ...), custom_call_target="tpu_custom_call" | custom-call | flops 1610612736 | bytes 4194304 | tf_op jit(solution)/shard_map/backward/pallas_call | solution.py:163
  65.7 4.1 %all-to-all-start.1 = ((bf16[16,3,64,128]{3,2,1,0:T(8,128)(2,1)}), bf16[16,3,64,128]{3,2,1,0:T(8,128)(2,1)S(1)}, u32[]{:S(2)}, u32[]{:S(2)}) async-start(bf16[16,3,64,128]{3,2,1,0:T(8,128)(2,1)} %backward.1), calls=%async_computation.1 | async-start | bytes 1572864 | tf_op jit(solution)/shard_map/all_to_all | solution.py:310
  71.0 1.4 %collective-permute-start.15 = (f32[4,4,1024]{2,1,0:T(4,128)S(1)}, f32[4,4,1024]{2,1,0:T(4,128)S(1)}, u32[]{:S(2)}, u32[]{:S(2)}) collective-permute-start(f32[4,4,1024]{2,1,0:T(4,128)S(1)} %get-tuple-element.46), channel_id=1, source_target_pairs={{0,1},{1,0},{2,3},{3,2},{4,5},{5,4},{6,7},{7,6},{8,9},{9,8},{10,11... | collective-permute-start | bytes 196616 | tf_op jit(solution)/shard_map/ppermute | solution.py:248
  73.0 1.6 %collective-permute-start.17 = (f32[4,4,1024]{2,1,0:T(4,128)S(1)}, f32[4,4,1024]{2,1,0:T(4,128)S(1)}, u32[]{:S(2)}, u32[]{:S(2)}) collective-permute-start(f32[4,4,1024]{2,1,0:T(4,128)S(1)} %get-tuple-element.47), channel_id=1, source_target_pairs={{0,3},{1,2},{2,1},{3,0},{4,7},{5,6},{6,5},{7,4},{8,11},{9,10},{10,... | collective-permute-start | bytes 196616 | tf_op jit(solution)/shard_map/ppermute | solution.py:248
  74.5 1.4 %collective-permute-done.15 = f32[4,4,1024]{2,1,0:T(4,128)S(1)} collective-permute-done((f32[4,4,1024]{2,1,0:T(4,128)S(1)}, f32[4,4,1024]{2,1,0:T(4,128)S(1)}, u32[]{:S(2)}, u32[]{:S(2)}) %collective-permute-start.15) | collective-permute-done | bytes 65568 | tf_op jit(solution)/shard_map/ppermute | solution.py:248
  76.0 2.2 %collective-permute-done.16 = f32[4,4,1024]{2,1,0:T(4,128)S(1)} collective-permute-done((f32[4,4,1024]{2,1,0:T(4,128)S(1)}, f32[4,4,1024]{2,1,0:T(4,128)S(1)}, u32[]{:S(2)}, u32[]{:S(2)}) %collective-permute-start.16) | collective-permute-done | bytes 65568 | tf_op jit(solution)/shard_map/ppermute | solution.py:248
  79.1 3.8 %collective-permute-start.19 = (f32[4,1024]{1,0:T(4,128)S(1)}, f32[4,1024]{1,0:T(4,128)S(1)}, u32[]{:S(2)}, u32[]{:S(2)}) collective-permute-start(f32[4,1024]{1,0:T(4,128)S(1)} %get-tuple-element.51), channel_id=1, source_target_pairs={{0,8},{1,9},{2,10},{3,11},{4,12},{5,13},{6,14},{7,15},{8,0},{9,1},... | collective-permute-start | bytes 49160 | tf_op jit(solution)/shard_map/ppermute | solution.py:248
  83.0 5.7 %collective-permute-done.18 = f32[4,1024]{1,0:T(4,128)S(1)} collective-permute-done((f32[4,1024]{1,0:T(4,128)S(1)}, f32[4,1024]{1,0:T(4,128)S(1)}, u32[]{:S(2)}, u32[]{:S(2)}) %collective-permute-start.18) | collective-permute-done | bytes 16416 | tf_op jit(solution)/shard_map/ppermute | solution.py:248
  88.7 5.0 %collective-permute-done.20 = f32[4,1024]{1,0:T(4,128)S(1)} collective-permute-done((f32[4,1024]{1,0:T(4,128)S(1)}, f32[4,1024]{1,0:T(4,128)S(1)}, u32[]{:S(2)}, u32[]{:S(2)}) %collective-permute-start.20) | collective-permute-done | bytes 16416 | tf_op jit(solution)/shard_map/ppermute | solution.py:248
  94.3 2.2 %all-to-all-done.1.in_ref = bf16[16,3,64,128]{3,2,1,0:T(8,128)(2,1)S(1)} async-done(((bf16[16,3,64,128]{3,2,1,0:T(8,128)(2,1)}), bf16[16,3,64,128]{3,2,1,0:T(8,128)(2,1)S(1)}, u32[]{:S(2)}, u32[]{:S(2)}) %all-to-all-start.1) | async-done | bytes 786464 | tf_op jit(solution)/shard_map/all_to_all | solution.py:310
  97.4 2.2 %unpack.1 = (bf16[64,2,1024]{2,1,0:T(2,128)(2,1)}, bf16[64,2,1024]{2,1,0:T(2,128)(2,1)}, bf16[64,2,1024]{2,1,0:T(2,128)(2,1)}) custom-call(bf16[16,3,64,128]{3,2,1,0:T(8,128)(2,1)} %copy-done.1), custom_call_target="tpu_custom_call" | custom-call | tf_op jit(solution)/shard_map/unpack/pallas_call | solution.py:242
  (41 shorter events, 9.5 us)
Async XLA Ops:
  0.6 8.9 %copy-start = (bf16[1024,64]{0,1:T(8,128)(2,1)S(1)}, bf16[1024,64]{0,1:T(8,128)(2,1)}, u32[]{:S(2)}) copy-start(bf16[1024,64]{0,1:T(8,128)(2,1)} %param.9) | copy-start | bytes 393220
  0.6 23.7 %collective-permute-start = (bf16[64,2,1024]{2,1,0:T(2,128)(2,1)}, bf16[64,2,1024]{2,1,0:T(2,128)(2,1)S(1)}, u32[]{:S(2)}, u32[]{:S(2)}) collective-permute-start(bf16[64,2,1024]{2,1,0:T(2,128)(2,1)} %bitcast.42), channel_id=1, source_target_pairs={{0,32},{16,48},{32,0},{48,16},{64,96},{80,112},{96,64},{112,80},{1... | collective-permute-start | bytes 786440 | tf_op jit(solution)/shard_map/ppermute | solution.py:248
  9.6 1.6 %collective-permute-start.1 = (bf16[64,1024]{1,0:T(8,128)(2,1)}, bf16[64,1024]{1,0:T(8,128)(2,1)S(1)}, u32[]{:S(2)}, u32[]{:S(2)}) collective-permute-start(bf16[64,1024]{1,0:T(8,128)(2,1)} %get-tuple-element.25), channel_id=1, source_target_pairs={{0,16},{16,0},{32,48},{48,32},{64,80},{80,64},{96,112},{112,96},{1... | collective-permute-start | bytes 393224 | tf_op jit(solution)/shard_map/ppermute | solution.py:248
  11.1 8.4 %collective-permute-start.2 = (bf16[64,128]{1,0:T(8,128)(2,1)S(1)}, bf16[64,128]{1,0:T(8,128)(2,1)S(1)}, u32[]{:S(2)}, u32[]{:S(2)}) collective-permute-start(bf16[64,128]{1,0:T(8,128)(2,1)S(1)} %dynamic-slice_bitcast_fusion.6), channel_id=1, source_target_pairs={{0,4},{1,5},{2,6},{3,7},{4,0},{5,1},{6,2},{7,3},{8,12},{9,13},{10,... | collective-permute-start | bytes 49160 | tf_op jit(solution)/shard_map/ppermute | solution.py:248
  12.2 12.1 %collective-permute-start.4 = (bf16[128,1024]{1,0:T(8,128)(2,1)S(1)}, bf16[128,1024]{1,0:T(8,128)(2,1)S(1)}, u32[]{:S(2)}, u32[]{:S(2)}) collective-permute-start(bf16[128,1024]{1,0:T(8,128)(2,1)S(1)} %constant_dynamic-update-slice_fusion.refs_0_), channel_id=1, source_target_pairs={{0,64},{16,80},{32,96},{48,112},{64,128},{80,144},{96,160},{112,17... | collective-permute-start | bytes 786440 | tf_op jit(solution)/shard_map/ppermute | solution.py:252
  13.7 14.4 %collective-permute-start.5 = (bf16[128,1024]{1,0:T(8,128)(2,1)S(1)}, bf16[128,1024]{1,0:T(8,128)(2,1)S(1)}, u32[]{:S(2)}, u32[]{:S(2)}) collective-permute-start(bf16[128,1024]{1,0:T(8,128)(2,1)S(1)} %constant_dynamic-update-slice_fusion.refs_0_), channel_id=1, source_target_pairs={{0,128},{16,144},{32,160},{48,176},{64,192},{80,208},{96,224},{112... | collective-permute-start | bytes 786440 | tf_op jit(solution)/shard_map/ppermute | solution.py:252
  16.4 11.7 %collective-permute-start.6 = (bf16[128,1024]{1,0:T(8,128)(2,1)S(1)}, bf16[128,1024]{1,0:T(8,128)(2,1)S(1)}, u32[]{:S(2)}, u32[]{:S(2)}) collective-permute-start(bf16[128,1024]{1,0:T(8,128)(2,1)S(1)} %constant_dynamic-update-slice_fusion.refs_0_), channel_id=1, source_target_pairs={{0,192},{16,208},{32,224},{48,240},{64,0},{80,16},{96,32},{112,48}... | collective-permute-start | bytes 786440 | tf_op jit(solution)/shard_map/ppermute | solution.py:252
  19.5 4.8 %collective-permute-start.3 = (bf16[128,128]{1,0:T(8,128)(2,1)S(1)}, bf16[128,128]{1,0:T(8,128)(2,1)S(1)}, u32[]{:S(2)}, u32[]{:S(2)}) collective-permute-start(bf16[128,128]{1,0:T(8,128)(2,1)S(1)} %pad_maximum_fusion), channel_id=1, source_target_pairs={{0,8},{1,9},{2,10},{3,11},{4,12},{5,13},{6,14},{7,15},{8,0},{9,1},... | collective-permute-start | bytes 98312 | tf_op jit(solution)/shard_map/ppermute | solution.py:248
  24.3 3.8 %copy-start.2 = (bf16[64,2,1024]{2,1,0:T(2,128)(2,1)}, bf16[64,2,1024]{2,1,0:T(2,128)(2,1)S(1)}, u32[]{:S(2)}) copy-start(bf16[64,2,1024]{2,1,0:T(2,128)(2,1)S(1)} %collective-permute-done.rows_ref) | copy-start | bytes 786436
  28.1 30.1 %all-to-all-start = ((bf16[16,3,64,128]{3,2,1,0:T(8,128)(2,1)}), bf16[16,3,64,128]{3,2,1,0:T(8,128)(2,1)S(1)}, u32[]{:S(2)}, u32[]{:S(2)}) async-start(bf16[16,3,64,128]{3,2,1,0:T(8,128)(2,1)} %get-tuple-element.27), calls=%async_computation | async-start | bytes 1572864 | tf_op jit(solution)/shard_map/all_to_all | solution.py:287
  34.0 1.6 %collective-permute-start.10 = (bf16[64,1024]{1,0:T(8,128)(2,1)}, bf16[64,1024]{1,0:T(8,128)(2,1)S(1)}, u32[]{:S(2)}, u32[]{:S(2)}) collective-permute-start(bf16[64,1024]{1,0:T(8,128)(2,1)} %get-tuple-element.33), channel_id=1, source_target_pairs={{0,16},{16,0},{32,48},{48,32},{64,80},{80,64},{96,112},{112,96},{1... | collective-permute-start | bytes 393224 | tf_op jit(solution)/shard_map/ppermute | solution.py:248
  35.6 24.8 %collective-permute-start.11 = (bf16[128,1024]{1,0:T(8,128)(2,1)S(1)}, bf16[128,1024]{1,0:T(8,128)(2,1)S(1)}, u32[]{:S(2)}, u32[]{:S(2)}) collective-permute-start(bf16[128,1024]{1,0:T(8,128)(2,1)S(1)} %constant_dynamic-update-slice_fusion.5.refs_4_), channel_id=1, source_target_pairs={{0,64},{16,80},{32,96},{48,112},{64,128},{80,144},{96,160},{112,17... | collective-permute-start | bytes 786440 | tf_op jit(solution)/shard_map/ppermute | solution.py:252
  37.6 22.8 %collective-permute-start.12 = (bf16[128,1024]{1,0:T(8,128)(2,1)S(1)}, bf16[128,1024]{1,0:T(8,128)(2,1)S(1)}, u32[]{:S(2)}, u32[]{:S(2)}) collective-permute-start(bf16[128,1024]{1,0:T(8,128)(2,1)S(1)} %constant_dynamic-update-slice_fusion.5.refs_4_), channel_id=1, source_target_pairs={{0,128},{16,144},{32,160},{48,176},{64,192},{80,208},{96,224},{112... | collective-permute-start | bytes 786440 | tf_op jit(solution)/shard_map/ppermute | solution.py:252
  40.3 20.2 %collective-permute-start.13 = (bf16[128,1024]{1,0:T(8,128)(2,1)S(1)}, bf16[128,1024]{1,0:T(8,128)(2,1)S(1)}, u32[]{:S(2)}, u32[]{:S(2)}) collective-permute-start(bf16[128,1024]{1,0:T(8,128)(2,1)S(1)} %constant_dynamic-update-slice_fusion.5.refs_4_), channel_id=1, source_target_pairs={{0,192},{16,208},{32,224},{48,240},{64,0},{80,16},{96,32},{112,48}... | collective-permute-start | bytes 786440 | tf_op jit(solution)/shard_map/ppermute | solution.py:252
  41.7 4.3 %collective-permute-start.7 = (bf16[256,128]{1,0:T(8,128)(2,1)S(1)}, bf16[256,128]{1,0:T(8,128)(2,1)S(1)}, u32[]{:S(2)}, u32[]{:S(2)}) collective-permute-start(bf16[256,128]{1,0:T(8,128)(2,1)S(1)} %constant_dynamic-update-slice_fusion.2.refs_8_), channel_id=1, source_target_pairs={{0,1},{1,0},{2,3},{3,2},{4,5},{5,4},{6,7},{7,6},{8,9},{9,8},{10,11... | collective-permute-start | bytes 196616 | tf_op jit(solution)/shard_map/ppermute | solution.py:248
  43.0 5.8 %collective-permute-start.8 = (bf16[256,128]{1,0:T(8,128)(2,1)S(1)}, bf16[256,128]{1,0:T(8,128)(2,1)S(1)}, u32[]{:S(2)}, u32[]{:S(2)}) collective-permute-start(bf16[256,128]{1,0:T(8,128)(2,1)S(1)} %constant_dynamic-update-slice_fusion.2.refs_8_), channel_id=1, source_target_pairs={{0,2},{1,3},{2,0},{3,1},{4,6},{5,7},{6,4},{7,5},{8,10},{9,11},{10,... | collective-permute-start | bytes 196616 | tf_op jit(solution)/shard_map/ppermute | solution.py:248
  46.0 4.3 %collective-permute-start.9 = (bf16[256,128]{1,0:T(8,128)(2,1)S(1)}, bf16[256,128]{1,0:T(8,128)(2,1)S(1)}, u32[]{:S(2)}, u32[]{:S(2)}) collective-permute-start(bf16[256,128]{1,0:T(8,128)(2,1)S(1)} %constant_dynamic-update-slice_fusion.2.refs_8_), channel_id=1, source_target_pairs={{0,3},{1,2},{2,1},{3,0},{4,7},{5,6},{6,5},{7,4},{8,11},{9,10},{10,... | collective-permute-start | bytes 196616 | tf_op jit(solution)/shard_map/ppermute | solution.py:248
  61.3 4.4 %collective-permute-start.14 = (f32[64,1024]{1,0:T(8,128)S(1)}, f32[64,1024]{1,0:T(8,128)}, u32[]{:S(2)}, u32[]{:S(2)}) collective-permute-start(f32[64,1024]{1,0:T(8,128)S(1)} %get-tuple-element.35), channel_id=1, source_target_pairs={{0,16},{16,0},{32,48},{48,32},{64,80},{80,64},{96,112},{112,96},{1... | collective-permute-start | bytes 786440 | tf_op jit(solution)/shard_map/ppermute | solution.py:248
  65.7 30.8 %all-to-all-start.1 = ((bf16[16,3,64,128]{3,2,1,0:T(8,128)(2,1)}), bf16[16,3,64,128]{3,2,1,0:T(8,128)(2,1)S(1)}, u32[]{:S(2)}, u32[]{:S(2)}) async-start(bf16[16,3,64,128]{3,2,1,0:T(8,128)(2,1)} %backward.1), calls=%async_computation.1 | async-start | bytes 1572864 | tf_op jit(solution)/shard_map/all_to_all | solution.py:310
  71.0 5.0 %collective-permute-start.15 = (f32[4,4,1024]{2,1,0:T(4,128)S(1)}, f32[4,4,1024]{2,1,0:T(4,128)S(1)}, u32[]{:S(2)}, u32[]{:S(2)}) collective-permute-start(f32[4,4,1024]{2,1,0:T(4,128)S(1)} %get-tuple-element.46), channel_id=1, source_target_pairs={{0,1},{1,0},{2,3},{3,2},{4,5},{5,4},{6,7},{7,6},{8,9},{9,8},{10,11... | collective-permute-start | bytes 196616 | tf_op jit(solution)/shard_map/ppermute | solution.py:248
  72.3 5.8 %collective-permute-start.16 = (f32[4,4,1024]{2,1,0:T(4,128)S(1)}, f32[4,4,1024]{2,1,0:T(4,128)S(1)}, u32[]{:S(2)}, u32[]{:S(2)}) collective-permute-start(f32[4,4,1024]{2,1,0:T(4,128)S(1)} %get-tuple-element.48), channel_id=1, source_target_pairs={{0,2},{1,3},{2,0},{3,1},{4,6},{5,7},{6,4},{7,5},{8,10},{9,11},{10,... | collective-permute-start | bytes 196616 | tf_op jit(solution)/shard_map/ppermute | solution.py:248
  73.0 5.7 %collective-permute-start.17 = (f32[4,4,1024]{2,1,0:T(4,128)S(1)}, f32[4,4,1024]{2,1,0:T(4,128)S(1)}, u32[]{:S(2)}, u32[]{:S(2)}) collective-permute-start(f32[4,4,1024]{2,1,0:T(4,128)S(1)} %get-tuple-element.47), channel_id=1, source_target_pairs={{0,3},{1,2},{2,1},{3,0},{4,7},{5,6},{6,5},{7,4},{8,11},{9,10},{10,... | collective-permute-start | bytes 196616 | tf_op jit(solution)/shard_map/ppermute | solution.py:248
  78.7 10.0 %collective-permute-start.18 = (f32[4,1024]{1,0:T(4,128)S(1)}, f32[4,1024]{1,0:T(4,128)S(1)}, u32[]{:S(2)}, u32[]{:S(2)}) collective-permute-start(f32[4,1024]{1,0:T(4,128)S(1)} %get-tuple-element.49), channel_id=1, source_target_pairs={{0,4},{1,5},{2,6},{3,7},{4,0},{5,1},{6,2},{7,3},{8,12},{9,13},{10,... | collective-permute-start | bytes 49160 | tf_op jit(solution)/shard_map/ppermute | solution.py:248
  79.1 9.6 %collective-permute-start.19 = (f32[4,1024]{1,0:T(4,128)S(1)}, f32[4,1024]{1,0:T(4,128)S(1)}, u32[]{:S(2)}, u32[]{:S(2)}) collective-permute-start(f32[4,1024]{1,0:T(4,128)S(1)} %get-tuple-element.51), channel_id=1, source_target_pairs={{0,8},{1,9},{2,10},{3,11},{4,12},{5,13},{6,14},{7,15},{8,0},{9,1},... | collective-permute-start | bytes 49160 | tf_op jit(solution)/shard_map/ppermute | solution.py:248
  83.0 10.7 %collective-permute-start.20 = (f32[4,1024]{1,0:T(4,128)S(1)}, f32[4,1024]{1,0:T(4,128)S(1)}, u32[]{:S(2)}, u32[]{:S(2)}) collective-permute-start(f32[4,1024]{1,0:T(4,128)S(1)} %get-tuple-element.50), channel_id=1, source_target_pairs={{0,12},{1,13},{2,14},{3,15},{4,8},{5,9},{6,10},{7,11},{8,4},{9,5},... | collective-permute-start | bytes 49160 | tf_op jit(solution)/shard_map/ppermute | solution.py:248
  96.5 0.9 copy-start.1

commit v4 on v3

--- a/solution.py
+++ b/solution.py
@@ -116,7 +116,8 @@
 
 
 VMEM = pl.BlockSpec(memory_space=pltpu.VMEM)
-PARAMS = pltpu.CompilerParams(vmem_limit_bytes=48 * 1024 * 1024)
+PARAMS = pltpu.CompilerParams(vmem_limit_bytes=32 * 1024 * 1024)
+SMALL = pltpu.CompilerParams(vmem_limit_bytes=16 * 1024 * 1024)
 
 
 def cost(products, length, bytes_accessed):
@@ -233,14 +234,14 @@
 def split_scores(rows):
     half = jax.ShapeDtypeStruct((rows.shape[0], rows.shape[2]), rows.dtype)
     return pl.pallas_call(
-        split_scores_kernel, out_shape=(half, half), in_specs=[VMEM], out_specs=(VMEM, VMEM), name="split_scores"
+        split_scores_kernel, out_shape=(half, half), in_specs=[VMEM], out_specs=(VMEM, VMEM), compiler_params=SMALL, name="split_scores"
     )(rows)
 
 
 def unpack(items):
     rows = jax.ShapeDtypeStruct((BLOCK, 2, HEADS * HEAD), items.dtype)
     return pl.pallas_call(
-        unpack_kernel, out_shape=(rows,) * 3, in_specs=[VMEM], out_specs=(VMEM,) * 3, name="unpack"
+        unpack_kernel, out_shape=(rows,) * 3, in_specs=[VMEM], out_specs=(VMEM,) * 3, compiler_params=SMALL, name="unpack"
     )(items)
 
 
@@ -283,7 +284,7 @@
     held, _ = lax.optimization_barrier((held, far_rows))
     weight = [held] + [swap(held, "track", j) for j in (1, 2, 3)]
 
-    qkv, _ = lax.optimization_barrier((qkv, (far_rows, held_z, pieces[1], pieces[2], pieces[3])))
+    qkv, _ = lax.optimization_barrier((qkv, (far_mine, held_z, pieces[1], pieces[2], pieces[3])))
     qkv = lax.all_to_all(qkv, "tm", split_axis=0, concat_axis=0, tiled=True)
 
     qkv, _ = lax.optimization_barrier((qkv, weight))

time: 100 us -> 97.4 us (0.974)
  waiting for transfers between devices: 40.1 us -> 43.4 us
  Pallas kernels: 13.8 us -> 11 us
  local copies, waits for them, and re-layouts: 2.91 us -> 1.1 us
  starting transfers between devices: 40.3 us -> 39.1 us
    all_to_all x1, waiting for transfers between devices: 2.15 us -> 7.2 us  [local(): lax.all_to_all(item_grads, 'tm', split_axis=0, concat_axis=0, tiled=True)]
    ppermute x15, waiting for transfers between devices: 26.2 us -> 22.6 us  [swap(): return lax.ppermute(array, axis, [(i, i ^ mask) for i in range(16)])]
    all_to_all x1, waiting for transfers between devices: 7.94 us -> 10 us  [local(): qkv = lax.all_to_all(qkv, 'tm', split_axis=0, concat_axis=0, tiled=True)]
    unnamed x10 -> x6, local copies, waits for them, and re-layouts: 2.76 us -> 0.94 us
    pallas_call x1, Pallas kernels: 1.86 us -> 0.21 us  [split_scores(): pl.pallas_call(split_scores_kernel, out_shape=(half, half), in_specs=[VME...]
    pallas_call x1, Pallas kernels: 2.23 us -> 1.1 us  [unpack(): pl.pallas_call(unpack_kernel, out_shape=(rows,) * 3, in_specs=[VMEM], out...]
  transfers between devices with their start and end apart: 23 -> 23, of which waited for: 15 -> 14; matrix products, arithmetic and copies ran while one was open for 4% -> 3% of each run, Pallas kernels for 11% -> 9%
where the time goes in v4:
time: 97.4 us; the launch traced here: 97 us
  waiting for transfers between devices  43.4 us (45%)
  starting transfers between devices  39.1 us (40%)
  Pallas kernels  11 us (11%)
  other arithmetic  1.63 us (2%)
  local copies, waits for them, and re-layouts  1.1 us (1%)
    ppermute x15, waiting for transfers between devices, swap(): return lax.ppermute(array, axis, [(i, i ^ mask) for i in range(16)])  22.6 us
    ppermute x15, starting transfers between devices, swap(): return lax.ppermute(array, axis, [(i, i ^ mask) for i in range(16)])  19.7 us
    ppermute x6, starting transfers between devices, shift(): lax.ppermute(array, 'tm', [(i, (i + 4 * by) % 16) for i in range(16)])  11.7 us
    all_to_all x1, waiting for transfers between devices, local(): qkv = lax.all_to_all(qkv, 'tm', split_axis=0, concat_axis=0, tiled=True)  10 us
    all_to_all x1, waiting for transfers between devices, local(): lax.all_to_all(item_grads, 'tm', split_axis=0, concat_axis=0, tiled=True)  7.2 us
    pallas_call x1, Pallas kernels, backward(): pl.pallas_call(functools.partial(backward_kernel, places), out_shape=jax....  4.1 us
    all_to_all x1, starting transfers between devices, local(): qkv = lax.all_to_all(qkv, 'tm', split_axis=0, concat_axis=0, tiled=True)  4.04 us
    all_to_all x1, starting transfers between devices, local(): lax.all_to_all(item_grads, 'tm', split_axis=0, concat_axis=0, tiled=True)  3.61 us
  transfers between devices with their start and end apart: 23, of which 14 were waited for; matrix products, arithmetic and copies ran while one was open for 3% of the time, Pallas kernels for 9%

profile of v4, /device:TPU:48, one launch (start us, length us, event | category | flops | bytes accessed | tf_op | source)
XLA Modules:
  0.0 97.0 jit_solution(9868065508505373450)
XLA Ops:
  0.6 6.4 %collective-permute-start = (bf16[64,2,1024]{2,1,0:T(2,128)(2,1)}, bf16[64,2,1024]{2,1,0:T(2,128)(2,1)S(1)}, u32[]{:S(2)}, u32[]{:S(2)}) collective-permute-start(bf16[64,2,1024]{2,1,0:T(2,128)(2,1)} %bitcast.42), channel_id=1, source_target_pairs={{0,32},{16,48},{32,0},{48,16},{64,96},{80,112},{96,64},{112,80},{1... | collective-permute-start | bytes 786440 | tf_op jit(solution)/shard_map/ppermute | solution.py:249
  7.0 2.5 %prepare.1 = (bf16[16,3,64,128]{3,2,1,0:T(8,128)(2,1)}, bf16[64,1024]{1,0:T(8,128)(2,1)}, bf16[64,1024]{1,0:T(8,128)(2,1)}) custom-call(bf16[64,2,1024]{2,1,0:T(2,128)(2,1)} %bitcast.39, bf16[64,2,1024]{2,1,0:T(2,128)(2,1)} %bitcast.40, bf16[64,2,1024]{2,1,0:T(2,128)(2,1)} %bitcast.41, bf16[64,2,1024]{2,1,0:T(2,128)(2,1)} %bitcast.43), custom_call_target="tpu_custom_call" | custom-call | tf_op jit(solution)/shard_map/prepare/pallas_call | solution.py:225
  11.1 1.1 %collective-permute-start.2 = (bf16[64,128]{1,0:T(8,128)(2,1)S(1)}, bf16[64,128]{1,0:T(8,128)(2,1)S(1)}, u32[]{:S(2)}, u32[]{:S(2)}) collective-permute-start(bf16[64,128]{1,0:T(8,128)(2,1)S(1)} %dynamic-slice_bitcast_fusion.6), channel_id=1, source_target_pairs={{0,4},{1,5},{2,6},{3,7},{4,0},{5,1},{6,2},{7,3},{8,12},{9,13},{10,... | collective-permute-start | bytes 49160 | tf_op jit(solution)/shard_map/ppermute | solution.py:249
  12.2 1.5 %collective-permute-start.4 = (bf16[128,1024]{1,0:T(8,128)(2,1)S(1)}, bf16[128,1024]{1,0:T(8,128)(2,1)S(1)}, u32[]{:S(2)}, u32[]{:S(2)}) collective-permute-start(bf16[128,1024]{1,0:T(8,128)(2,1)S(1)} %constant_dynamic-update-slice_fusion.refs_0_), channel_id=1, source_target_pairs={{0,64},{16,80},{32,96},{48,112},{64,128},{80,144},{96,160},{112,17... | collective-permute-start | bytes 786440 | tf_op jit(solution)/shard_map/ppermute | solution.py:253
  13.7 2.7 %collective-permute-start.5 = (bf16[128,1024]{1,0:T(8,128)(2,1)S(1)}, bf16[128,1024]{1,0:T(8,128)(2,1)S(1)}, u32[]{:S(2)}, u32[]{:S(2)}) collective-permute-start(bf16[128,1024]{1,0:T(8,128)(2,1)S(1)} %constant_dynamic-update-slice_fusion.refs_0_), channel_id=1, source_target_pairs={{0,128},{16,144},{32,160},{48,176},{64,192},{80,208},{96,224},{112... | collective-permute-start | bytes 786440 | tf_op jit(solution)/shard_map/ppermute | solution.py:253
  16.4 1.4 %collective-permute-start.6 = (bf16[128,1024]{1,0:T(8,128)(2,1)S(1)}, bf16[128,1024]{1,0:T(8,128)(2,1)S(1)}, u32[]{:S(2)}, u32[]{:S(2)}) collective-permute-start(bf16[128,1024]{1,0:T(8,128)(2,1)S(1)} %constant_dynamic-update-slice_fusion.refs_0_), channel_id=1, source_target_pairs={{0,192},{16,208},{32,224},{48,240},{64,0},{80,16},{96,32},{112,48}... | collective-permute-start | bytes 786440 | tf_op jit(solution)/shard_map/ppermute | solution.py:253
  17.9 1.6 %collective-permute-done.2 = bf16[64,128]{1,0:T(8,128)(2,1)S(1)} collective-permute-done((bf16[64,128]{1,0:T(8,128)(2,1)S(1)}, bf16[64,128]{1,0:T(8,128)(2,1)S(1)}, u32[]{:S(2)}, u32[]{:S(2)}) %collective-permute-start.2) | collective-permute-done | bytes 16416 | tf_op jit(solution)/shard_map/ppermute | solution.py:249
  19.5 2.0 %collective-permute-start.3 = (bf16[128,128]{1,0:T(8,128)(2,1)S(1)}, bf16[128,128]{1,0:T(8,128)(2,1)S(1)}, u32[]{:S(2)}, u32[]{:S(2)}) collective-permute-start(bf16[128,128]{1,0:T(8,128)(2,1)S(1)} %pad_maximum_fusion), channel_id=1, source_target_pairs={{0,8},{1,9},{2,10},{3,11},{4,12},{5,13},{6,14},{7,15},{8,0},{9,1},... | collective-permute-start | bytes 98312 | tf_op jit(solution)/shard_map/ppermute | solution.py:249
  21.6 2.8 %collective-permute-done.3 = bf16[128,128]{1,0:T(8,128)(2,1)S(1)} collective-permute-done((bf16[128,128]{1,0:T(8,128)(2,1)S(1)}, bf16[128,128]{1,0:T(8,128)(2,1)S(1)}, u32[]{:S(2)}, u32[]{:S(2)}) %collective-permute-start.3) | collective-permute-done | bytes 32800 | tf_op jit(solution)/shard_map/ppermute | solution.py:249
  24.6 3.5 %collective-permute-done.5.refs_2_ = bf16[128,1024]{1,0:T(8,128)(2,1)S(1)} collective-permute-done((bf16[128,1024]{1,0:T(8,128)(2,1)S(1)}, bf16[128,1024]{1,0:T(8,128)(2,1)S(1)}, u32[]{:S(2)}, u32[]{:S(2)}) %collective-permute-start.5) | collective-permute-done | bytes 262176 | tf_op jit(solution)/shard_map/ppermute | solution.py:253
  28.1 4.0 %all-to-all-start = ((bf16[16,3,64,128]{3,2,1,0:T(8,128)(2,1)}), bf16[16,3,64,128]{3,2,1,0:T(8,128)(2,1)S(1)}, u32[]{:S(2)}, u32[]{:S(2)}) async-start(bf16[16,3,64,128]{3,2,1,0:T(8,128)(2,1)} %get-tuple-element.28), calls=%async_computation | async-start | bytes 1572864 | tf_op jit(solution)/shard_map/all_to_all | solution.py:288
  32.6 1.0 %collective-permute-done.10 = bf16[64,1024]{1,0:T(8,128)(2,1)S(1)} collective-permute-done((bf16[64,1024]{1,0:T(8,128)(2,1)S(1)}, bf16[64,1024]{1,0:T(8,128)(2,1)S(1)}, u32[]{:S(2)}, u32[]{:S(2)}) %collective-permute-start.10) | collective-permute-done | bytes 131104 | tf_op jit(solution)/shard_map/ppermute | solution.py:249
  33.6 1.9 %collective-permute-start.11 = (bf16[128,1024]{1,0:T(8,128)(2,1)S(1)}, bf16[128,1024]{1,0:T(8,128)(2,1)S(1)}, u32[]{:S(2)}, u32[]{:S(2)}) collective-permute-start(bf16[128,1024]{1,0:T(8,128)(2,1)S(1)} %constant_dynamic-update-slice_fusion.5.refs_4_), channel_id=1, source_target_pairs={{0,64},{16,80},{32,96},{48,112},{64,128},{80,144},{96,160},{112,17... | collective-permute-start | bytes 786440 | tf_op jit(solution)/shard_map/ppermute | solution.py:253
  35.5 2.7 %collective-permute-start.12 = (bf16[128,1024]{1,0:T(8,128)(2,1)S(1)}, bf16[128,1024]{1,0:T(8,128)(2,1)S(1)}, u32[]{:S(2)}, u32[]{:S(2)}) collective-permute-start(bf16[128,1024]{1,0:T(8,128)(2,1)S(1)} %constant_dynamic-update-slice_fusion.5.refs_4_), channel_id=1, source_target_pairs={{0,128},{16,144},{32,160},{48,176},{64,192},{80,208},{96,224},{112... | collective-permute-start | bytes 786440 | tf_op jit(solution)/shard_map/ppermute | solution.py:253
  38.2 1.5 %collective-permute-start.13 = (bf16[128,1024]{1,0:T(8,128)(2,1)S(1)}, bf16[128,1024]{1,0:T(8,128)(2,1)S(1)}, u32[]{:S(2)}, u32[]{:S(2)}) collective-permute-start(bf16[128,1024]{1,0:T(8,128)(2,1)S(1)} %constant_dynamic-update-slice_fusion.5.refs_4_), channel_id=1, source_target_pairs={{0,192},{16,208},{32,224},{48,240},{64,0},{80,16},{96,32},{112,48}... | collective-permute-start | bytes 786440 | tf_op jit(solution)/shard_map/ppermute | solution.py:253
  39.7 1.3 %collective-permute-start.7 = (bf16[256,128]{1,0:T(8,128)(2,1)S(1)}, bf16[256,128]{1,0:T(8,128)(2,1)S(1)}, u32[]{:S(2)}, u32[]{:S(2)}) collective-permute-start(bf16[256,128]{1,0:T(8,128)(2,1)S(1)} %constant_dynamic-update-slice_fusion.2.refs_8_), channel_id=1, source_target_pairs={{0,1},{1,0},{2,3},{3,2},{4,5},{5,4},{6,7},{7,6},{8,9},{9,8},{10,11... | collective-permute-start | bytes 196616 | tf_op jit(solution)/shard_map/ppermute | solution.py:249
  41.6 2.4 %collective-permute-done.7.refs_9_ = bf16[256,128]{1,0:T(8,128)(2,1)S(1)} collective-permute-done((bf16[256,128]{1,0:T(8,128)(2,1)S(1)}, bf16[256,128]{1,0:T(8,128)(2,1)S(1)}, u32[]{:S(2)}, u32[]{:S(2)}) %collective-permute-start.7) | collective-permute-done | bytes 65568 | tf_op jit(solution)/shard_map/ppermute | solution.py:249
  44.4 2.3 %collective-permute-done.8.refs_10_ = bf16[256,128]{1,0:T(8,128)(2,1)S(1)} collective-permute-done((bf16[256,128]{1,0:T(8,128)(2,1)S(1)}, bf16[256,128]{1,0:T(8,128)(2,1)S(1)}, u32[]{:S(2)}, u32[]{:S(2)}) %collective-permute-start.8) | collective-permute-done | bytes 65568 | tf_op jit(solution)/shard_map/ppermute | solution.py:249
  46.7 1.5 %collective-permute-done.9.refs_11_ = bf16[256,128]{1,0:T(8,128)(2,1)S(1)} collective-permute-done((bf16[256,128]{1,0:T(8,128)(2,1)S(1)}, bf16[256,128]{1,0:T(8,128)(2,1)S(1)}, u32[]{:S(2)}, u32[]{:S(2)}) %collective-permute-start.9) | collective-permute-done | bytes 65568 | tf_op jit(solution)/shard_map/ppermute | solution.py:249
  48.2 10.0 %all-to-all-done.qkv_ref = bf16[16,3,64,128]{3,2,1,0:T(8,128)(2,1)S(1)} async-done(((bf16[16,3,64,128]{3,2,1,0:T(8,128)(2,1)}), bf16[16,3,64,128]{3,2,1,0:T(8,128)(2,1)S(1)}, u32[]{:S(2)}, u32[]{:S(2)}) %all-to-all-start) | async-done | bytes 786464 | tf_op jit(solution)/shard_map/all_to_all | solution.py:288
  58.2 2.2 %forward.1 = (bf16[1024,128]{1,0:T(8,128)(2,1)S(1)}, f32[1024,1]{1,0:T(8,128)S(1)}) custom-call(bf16[16,3,64,128]{3,2,1,0:T(8,128)(2,1)S(1)} %all-to-all-done.qkv_ref), custom_call_target="tpu_custom_call" | custom-call | flops 536870912 | bytes 2097152 | tf_op jit(solution)/shard_map/forward/pallas_call | solution.py:133
  61.6 4.1 %backward.1 = bf16[16,3,64,128]{3,2,1,0:T(8,128)(2,1)} custom-call(bf16[16,3,64,128]{3,2,1,0:T(8,128)(2,1)S(1)} %all-to-all-done.qkv_ref, f32[1024,1]{1,0:T(8,128)S(1)} %get-tuple-element.36.lse_ref, bf16[128,1024]{1,0:T(8,128)(2,1)S(1)} %constant_dynamic-update-slice_fusion.refs_0_, bf16[128,1024]{1,0:T(8,128)(2,1)S(1)} %collective-permute-done.4.refs_1_, ...), custom_call_target="tpu_custom_call" | custom-call | flops 1610612736 | bytes 4194304 | tf_op jit(solution)/shard_map/backward/pallas_call | solution.py:164
  65.7 3.6 %all-to-all-start.1 = ((bf16[16,3,64,128]{3,2,1,0:T(8,128)(2,1)}), bf16[16,3,64,128]{3,2,1,0:T(8,128)(2,1)S(1)}, u32[]{:S(2)}, u32[]{:S(2)}) async-start(bf16[16,3,64,128]{3,2,1,0:T(8,128)(2,1)} %backward.1), calls=%async_computation.1 | async-start | bytes 1572864 | tf_op jit(solution)/shard_map/all_to_all | solution.py:311
  69.3 1.0 %add.57 = f32[64,1024]{1,0:T(8,128)S(1)} add(f32[64,1024]{1,0:T(8,128)S(1)} %get-tuple-element.34, f32[64,1024]{1,0:T(8,128)} %collective-permute-done.14) | non-fusion elementwise | flops 65536 | bytes 786432 | tf_op jit(solution)/shard_map/add | solution.py:299
  70.4 1.4 %collective-permute-start.15 = (f32[4,4,1024]{2,1,0:T(4,128)S(1)}, f32[4,4,1024]{2,1,0:T(4,128)S(1)}, u32[]{:S(2)}, u32[]{:S(2)}) collective-permute-start(f32[4,4,1024]{2,1,0:T(4,128)S(1)} %get-tuple-element.46), channel_id=1, source_target_pairs={{0,1},{1,0},{2,3},{3,2},{4,5},{5,4},{6,7},{7,6},{8,9},{9,8},{10,11... | collective-permute-start | bytes 196616 | tf_op jit(solution)/shard_map/ppermute | solution.py:249
  72.4 1.6 %collective-permute-start.17 = (f32[4,4,1024]{2,1,0:T(4,128)S(1)}, f32[4,4,1024]{2,1,0:T(4,128)S(1)}, u32[]{:S(2)}, u32[]{:S(2)}) collective-permute-start(f32[4,4,1024]{2,1,0:T(4,128)S(1)} %get-tuple-element.47), channel_id=1, source_target_pairs={{0,3},{1,2},{2,1},{3,0},{4,7},{5,6},{6,5},{7,4},{8,11},{9,10},{10,... | collective-permute-start | bytes 196616 | tf_op jit(solution)/shard_map/ppermute | solution.py:249
  74.0 1.4 %collective-permute-done.15 = f32[4,4,1024]{2,1,0:T(4,128)S(1)} collective-permute-done((f32[4,4,1024]{2,1,0:T(4,128)S(1)}, f32[4,4,1024]{2,1,0:T(4,128)S(1)}, u32[]{:S(2)}, u32[]{:S(2)}) %collective-permute-start.15) | collective-permute-done | bytes 65568 | tf_op jit(solution)/shard_map/ppermute | solution.py:249
  75.4 2.2 %collective-permute-done.16 = f32[4,4,1024]{2,1,0:T(4,128)S(1)} collective-permute-done((f32[4,4,1024]{2,1,0:T(4,128)S(1)}, f32[4,4,1024]{2,1,0:T(4,128)S(1)}, u32[]{:S(2)}, u32[]{:S(2)}) %collective-permute-start.16) | collective-permute-done | bytes 65568 | tf_op jit(solution)/shard_map/ppermute | solution.py:249
  79.1 2.5 %collective-permute-start.19 = (f32[4,1024]{1,0:T(4,128)S(1)}, f32[4,1024]{1,0:T(4,128)S(1)}, u32[]{:S(2)}, u32[]{:S(2)}) collective-permute-start(f32[4,1024]{1,0:T(4,128)S(1)} %get-tuple-element.51), channel_id=1, source_target_pairs={{0,8},{1,9},{2,10},{3,11},{4,12},{5,13},{6,14},{7,15},{8,0},{9,1},... | collective-permute-start | bytes 49160 | tf_op jit(solution)/shard_map/ppermute | solution.py:249
  81.7 6.3 %collective-permute-done.18 = f32[4,1024]{1,0:T(4,128)S(1)} collective-permute-done((f32[4,1024]{1,0:T(4,128)S(1)}, f32[4,1024]{1,0:T(4,128)S(1)}, u32[]{:S(2)}, u32[]{:S(2)}) %collective-permute-start.18) | collective-permute-done | bytes 16416 | tf_op jit(solution)/shard_map/ppermute | solution.py:249
  88.7 7.2 %all-to-all-done.1.in_ref = bf16[16,3,64,128]{3,2,1,0:T(8,128)(2,1)S(1)} async-done(((bf16[16,3,64,128]{3,2,1,0:T(8,128)(2,1)}), bf16[16,3,64,128]{3,2,1,0:T(8,128)(2,1)S(1)}, u32[]{:S(2)}, u32[]{:S(2)}) %all-to-all-start.1) | async-done | bytes 786464 | tf_op jit(solution)/shard_map/all_to_all | solution.py:311
  95.9 1.1 %unpack.1 = (bf16[64,2,1024]{2,1,0:T(2,128)(2,1)}, bf16[64,2,1024]{2,1,0:T(2,128)(2,1)}, bf16[64,2,1024]{2,1,0:T(2,128)(2,1)}) custom-call(bf16[16,3,64,128]{3,2,1,0:T(8,128)(2,1)S(1)} %all-to-all-done.1.in_ref), custom_call_target="tpu_custom_call" | custom-call | tf_op jit(solution)/shard_map/unpack/pallas_call | solution.py:243
  (37 shorter events, 7.3 us)
Async XLA Ops:
  0.6 8.9 %copy-start = (bf16[1024,64]{0,1:T(8,128)(2,1)S(1)}, bf16[1024,64]{0,1:T(8,128)(2,1)}, u32[]{:S(2)}) copy-start(bf16[1024,64]{0,1:T(8,128)(2,1)} %param.9) | copy-start | bytes 393220
  0.6 23.7 %collective-permute-start = (bf16[64,2,1024]{2,1,0:T(2,128)(2,1)}, bf16[64,2,1024]{2,1,0:T(2,128)(2,1)S(1)}, u32[]{:S(2)}, u32[]{:S(2)}) collective-permute-start(bf16[64,2,1024]{2,1,0:T(2,128)(2,1)} %bitcast.42), channel_id=1, source_target_pairs={{0,32},{16,48},{32,0},{48,16},{64,96},{80,112},{96,64},{112,80},{1... | collective-permute-start | bytes 786440 | tf_op jit(solution)/shard_map/ppermute | solution.py:249
  9.5 1.6 %collective-permute-start.1 = (bf16[64,1024]{1,0:T(8,128)(2,1)}, bf16[64,1024]{1,0:T(8,128)(2,1)S(1)}, u32[]{:S(2)}, u32[]{:S(2)}) collective-permute-start(bf16[64,1024]{1,0:T(8,128)(2,1)} %get-tuple-element.26), channel_id=1, source_target_pairs={{0,16},{16,0},{32,48},{48,32},{64,80},{80,64},{96,112},{112,96},{1... | collective-permute-start | bytes 393224 | tf_op jit(solution)/shard_map/ppermute | solution.py:249
  11.1 8.4 %collective-permute-start.2 = (bf16[64,128]{1,0:T(8,128)(2,1)S(1)}, bf16[64,128]{1,0:T(8,128)(2,1)S(1)}, u32[]{:S(2)}, u32[]{:S(2)}) collective-permute-start(bf16[64,128]{1,0:T(8,128)(2,1)S(1)} %dynamic-slice_bitcast_fusion.6), channel_id=1, source_target_pairs={{0,4},{1,5},{2,6},{3,7},{4,0},{5,1},{6,2},{7,3},{8,12},{9,13},{10,... | collective-permute-start | bytes 49160 | tf_op jit(solution)/shard_map/ppermute | solution.py:249
  12.2 12.3 %collective-permute-start.4 = (bf16[128,1024]{1,0:T(8,128)(2,1)S(1)}, bf16[128,1024]{1,0:T(8,128)(2,1)S(1)}, u32[]{:S(2)}, u32[]{:S(2)}) collective-permute-start(bf16[128,1024]{1,0:T(8,128)(2,1)S(1)} %constant_dynamic-update-slice_fusion.refs_0_), channel_id=1, source_target_pairs={{0,64},{16,80},{32,96},{48,112},{64,128},{80,144},{96,160},{112,17... | collective-permute-start | bytes 786440 | tf_op jit(solution)/shard_map/ppermute | solution.py:253
  13.7 14.4 %collective-permute-start.5 = (bf16[128,1024]{1,0:T(8,128)(2,1)S(1)}, bf16[128,1024]{1,0:T(8,128)(2,1)S(1)}, u32[]{:S(2)}, u32[]{:S(2)}) collective-permute-start(bf16[128,1024]{1,0:T(8,128)(2,1)S(1)} %constant_dynamic-update-slice_fusion.refs_0_), channel_id=1, source_target_pairs={{0,128},{16,144},{32,160},{48,176},{64,192},{80,208},{96,224},{112... | collective-permute-start | bytes 786440 | tf_op jit(solution)/shard_map/ppermute | solution.py:253
  16.4 11.7 %collective-permute-start.6 = (bf16[128,1024]{1,0:T(8,128)(2,1)S(1)}, bf16[128,1024]{1,0:T(8,128)(2,1)S(1)}, u32[]{:S(2)}, u32[]{:S(2)}) collective-permute-start(bf16[128,1024]{1,0:T(8,128)(2,1)S(1)} %constant_dynamic-update-slice_fusion.refs_0_), channel_id=1, source_target_pairs={{0,192},{16,208},{32,224},{48,240},{64,0},{80,16},{96,32},{112,48}... | collective-permute-start | bytes 786440 | tf_op jit(solution)/shard_map/ppermute | solution.py:253
  19.5 4.8 %collective-permute-start.3 = (bf16[128,128]{1,0:T(8,128)(2,1)S(1)}, bf16[128,128]{1,0:T(8,128)(2,1)S(1)}, u32[]{:S(2)}, u32[]{:S(2)}) collective-permute-start(bf16[128,128]{1,0:T(8,128)(2,1)S(1)} %pad_maximum_fusion), channel_id=1, source_target_pairs={{0,8},{1,9},{2,10},{3,11},{4,12},{5,13},{6,14},{7,15},{8,0},{9,1},... | collective-permute-start | bytes 98312 | tf_op jit(solution)/shard_map/ppermute | solution.py:249
  28.1 30.1 %all-to-all-start = ((bf16[16,3,64,128]{3,2,1,0:T(8,128)(2,1)}), bf16[16,3,64,128]{3,2,1,0:T(8,128)(2,1)S(1)}, u32[]{:S(2)}, u32[]{:S(2)}) async-start(bf16[16,3,64,128]{3,2,1,0:T(8,128)(2,1)} %get-tuple-element.28), calls=%async_computation | async-start | bytes 1572864 | tf_op jit(solution)/shard_map/all_to_all | solution.py:288
  32.2 1.4 %collective-permute-start.10 = (bf16[64,1024]{1,0:T(8,128)(2,1)S(1)}, bf16[64,1024]{1,0:T(8,128)(2,1)S(1)}, u32[]{:S(2)}, u32[]{:S(2)}) collective-permute-start(bf16[64,1024]{1,0:T(8,128)(2,1)S(1)} %get-tuple-element.33), channel_id=1, source_target_pairs={{0,16},{16,0},{32,48},{48,32},{64,80},{80,64},{96,112},{112,96},{1... | collective-permute-start | bytes 393224 | tf_op jit(solution)/shard_map/ppermute | solution.py:249
  33.6 26.8 %collective-permute-start.11 = (bf16[128,1024]{1,0:T(8,128)(2,1)S(1)}, bf16[128,1024]{1,0:T(8,128)(2,1)S(1)}, u32[]{:S(2)}, u32[]{:S(2)}) collective-permute-start(bf16[128,1024]{1,0:T(8,128)(2,1)S(1)} %constant_dynamic-update-slice_fusion.5.refs_4_), channel_id=1, source_target_pairs={{0,64},{16,80},{32,96},{48,112},{64,128},{80,144},{96,160},{112,17... | collective-permute-start | bytes 786440 | tf_op jit(solution)/shard_map/ppermute | solution.py:253
  35.5 24.9 %collective-permute-start.12 = (bf16[128,1024]{1,0:T(8,128)(2,1)S(1)}, bf16[128,1024]{1,0:T(8,128)(2,1)S(1)}, u32[]{:S(2)}, u32[]{:S(2)}) collective-permute-start(bf16[128,1024]{1,0:T(8,128)(2,1)S(1)} %constant_dynamic-update-slice_fusion.5.refs_4_), channel_id=1, source_target_pairs={{0,128},{16,144},{32,160},{48,176},{64,192},{80,208},{96,224},{112... | collective-permute-start | bytes 786440 | tf_op jit(solution)/shard_map/ppermute | solution.py:253
  38.2 22.2 %collective-permute-start.13 = (bf16[128,1024]{1,0:T(8,128)(2,1)S(1)}, bf16[128,1024]{1,0:T(8,128)(2,1)S(1)}, u32[]{:S(2)}, u32[]{:S(2)}) collective-permute-start(bf16[128,1024]{1,0:T(8,128)(2,1)S(1)} %constant_dynamic-update-slice_fusion.5.refs_4_), channel_id=1, source_target_pairs={{0,192},{16,208},{32,224},{48,240},{64,0},{80,16},{96,32},{112,48}... | collective-permute-start | bytes 786440 | tf_op jit(solution)/shard_map/ppermute | solution.py:253
  39.7 4.3 %collective-permute-start.7 = (bf16[256,128]{1,0:T(8,128)(2,1)S(1)}, bf16[256,128]{1,0:T(8,128)(2,1)S(1)}, u32[]{:S(2)}, u32[]{:S(2)}) collective-permute-start(bf16[256,128]{1,0:T(8,128)(2,1)S(1)} %constant_dynamic-update-slice_fusion.2.refs_8_), channel_id=1, source_target_pairs={{0,1},{1,0},{2,3},{3,2},{4,5},{5,4},{6,7},{7,6},{8,9},{9,8},{10,11... | collective-permute-start | bytes 196616 | tf_op jit(solution)/shard_map/ppermute | solution.py:249
  40.9 5.8 %collective-permute-start.8 = (bf16[256,128]{1,0:T(8,128)(2,1)S(1)}, bf16[256,128]{1,0:T(8,128)(2,1)S(1)}, u32[]{:S(2)}, u32[]{:S(2)}) collective-permute-start(bf16[256,128]{1,0:T(8,128)(2,1)S(1)} %constant_dynamic-update-slice_fusion.2.refs_8_), channel_id=1, source_target_pairs={{0,2},{1,3},{2,0},{3,1},{4,6},{5,7},{6,4},{7,5},{8,10},{9,11},{10,... | collective-permute-start | bytes 196616 | tf_op jit(solution)/shard_map/ppermute | solution.py:249
  43.9 4.3 %collective-permute-start.9 = (bf16[256,128]{1,0:T(8,128)(2,1)S(1)}, bf16[256,128]{1,0:T(8,128)(2,1)S(1)}, u32[]{:S(2)}, u32[]{:S(2)}) collective-permute-start(bf16[256,128]{1,0:T(8,128)(2,1)S(1)} %constant_dynamic-update-slice_fusion.2.refs_8_), channel_id=1, source_target_pairs={{0,3},{1,2},{2,1},{3,0},{4,7},{5,6},{6,5},{7,4},{8,11},{9,10},{10,... | collective-permute-start | bytes 196616 | tf_op jit(solution)/shard_map/ppermute | solution.py:249
  61.3 4.4 %collective-permute-start.14 = (f32[64,1024]{1,0:T(8,128)S(1)}, f32[64,1024]{1,0:T(8,128)}, u32[]{:S(2)}, u32[]{:S(2)}) collective-permute-start(f32[64,1024]{1,0:T(8,128)S(1)} %get-tuple-element.35), channel_id=1, source_target_pairs={{0,16},{16,0},{32,48},{48,32},{64,80},{80,64},{96,112},{112,96},{1... | collective-permute-start | bytes 786440 | tf_op jit(solution)/shard_map/ppermute | solution.py:249
  65.7 30.2 %all-to-all-start.1 = ((bf16[16,3,64,128]{3,2,1,0:T(8,128)(2,1)}), bf16[16,3,64,128]{3,2,1,0:T(8,128)(2,1)S(1)}, u32[]{:S(2)}, u32[]{:S(2)}) async-start(bf16[16,3,64,128]{3,2,1,0:T(8,128)(2,1)} %backward.1), calls=%async_computation.1 | async-start | bytes 1572864 | tf_op jit(solution)/shard_map/all_to_all | solution.py:311
  70.4 5.0 %collective-permute-start.15 = (f32[4,4,1024]{2,1,0:T(4,128)S(1)}, f32[4,4,1024]{2,1,0:T(4,128)S(1)}, u32[]{:S(2)}, u32[]{:S(2)}) collective-permute-start(f32[4,4,1024]{2,1,0:T(4,128)S(1)} %get-tuple-element.46), channel_id=1, source_target_pairs={{0,1},{1,0},{2,3},{3,2},{4,5},{5,4},{6,7},{7,6},{8,9},{9,8},{10,11... | collective-permute-start | bytes 196616 | tf_op jit(solution)/shard_map/ppermute | solution.py:249
  71.8 5.8 %collective-permute-start.16 = (f32[4,4,1024]{2,1,0:T(4,128)S(1)}, f32[4,4,1024]{2,1,0:T(4,128)S(1)}, u32[]{:S(2)}, u32[]{:S(2)}) collective-permute-start(f32[4,4,1024]{2,1,0:T(4,128)S(1)} %get-tuple-element.48), channel_id=1, source_target_pairs={{0,2},{1,3},{2,0},{3,1},{4,6},{5,7},{6,4},{7,5},{8,10},{9,11},{10,... | collective-permute-start | bytes 196616 | tf_op jit(solution)/shard_map/ppermute | solution.py:249
  72.4 5.7 %collective-permute-start.17 = (f32[4,4,1024]{2,1,0:T(4,128)S(1)}, f32[4,4,1024]{2,1,0:T(4,128)S(1)}, u32[]{:S(2)}, u32[]{:S(2)}) collective-permute-start(f32[4,4,1024]{2,1,0:T(4,128)S(1)} %get-tuple-element.47), channel_id=1, source_target_pairs={{0,3},{1,2},{2,1},{3,0},{4,7},{5,6},{6,5},{7,4},{8,11},{9,10},{10,... | collective-permute-start | bytes 196616 | tf_op jit(solution)/shard_map/ppermute | solution.py:249
  78.2 9.9 %collective-permute-start.18 = (f32[4,1024]{1,0:T(4,128)S(1)}, f32[4,1024]{1,0:T(4,128)S(1)}, u32[]{:S(2)}, u32[]{:S(2)}) collective-permute-start(f32[4,1024]{1,0:T(4,128)S(1)} %get-tuple-element.49), channel_id=1, source_target_pairs={{0,4},{1,5},{2,6},{3,7},{4,0},{5,1},{6,2},{7,3},{8,12},{9,13},{10,... | collective-permute-start | bytes 49160 | tf_op jit(solution)/shard_map/ppermute | solution.py:249
  79.1 9.0 %collective-permute-start.19 = (f32[4,1024]{1,0:T(4,128)S(1)}, f32[4,1024]{1,0:T(4,128)S(1)}, u32[]{:S(2)}, u32[]{:S(2)}) collective-permute-start(f32[4,1024]{1,0:T(4,128)S(1)} %get-tuple-element.51), channel_id=1, source_target_pairs={{0,8},{1,9},{2,10},{3,11},{4,12},{5,13},{6,14},{7,15},{8,0},{9,1},... | collective-permute-start | bytes 49160 | tf_op jit(solution)/shard_map/ppermute | solution.py:249
  81.6 6.5 %collective-permute-start.20 = (f32[4,1024]{1,0:T(4,128)S(1)}, f32[4,1024]{1,0:T(4,128)S(1)}, u32[]{:S(2)}, u32[]{:S(2)}) collective-permute-start(f32[4,1024]{1,0:T(4,128)S(1)} %get-tuple-element.50), channel_id=1, source_target_pairs={{0,12},{1,13},{2,14},{3,15},{4,8},{5,9},{6,10},{7,11},{8,4},{9,5},... | collective-permute-start | bytes 49160 | tf_op jit(solution)/shard_map/ppermute | solution.py:249

commit v5 on v4

--- a/solution.py
+++ b/solution.py
@@ -290,21 +290,20 @@
     qkv, _ = lax.optimization_barrier((qkv, weight))
     att, lse = forward(qkv)
     keep, send = weight_term(att, places, pieces, norm_factor)
-    lse, _ = lax.optimization_barrier((lse, (keep, send)))
 
     item_grads = backward(qkv, lse, places, pieces, weight)
 
     from_core = swap(send, "tm", 1)
-    item_grads, from_core = lax.optimization_barrier((item_grads, from_core))
-    total = keep + from_core
-    total = total.reshape(4, 4, 4, model_width)
-    for axis, step, place in ((1, 1, track % 4), (0, 4, track // 4)):
-        parts = [lax.dynamic_index_in_dim(total, place ^ j, axis, keepdims=False) for j in range(4)]
+    terms = (keep, from_core)
+    for rest, axis, step, place in (((4, 4, 4), 1, 1, track % 4), ((4, 4), 0, 4, track // 4)):
+        terms = [term.reshape(rest + (model_width,)) for term in terms]
+        parts = [
+            sum(lax.dynamic_index_in_dim(term, place ^ j, axis, keepdims=False) for term in terms) for j in range(4)
+        ]
         total = parts[0]
         for j in (1, 2, 3):
             total = total + swap(parts[j], "track", step * j)
-        if step == 1:
-            after_y = total
+        terms = (total,)
     grad_weight = total
 
 

time: 97.4 us -> 96 us (0.986)
  waiting for transfers between devices: 43.4 us -> 42.2 us
    all_to_all x1, waiting for transfers between devices: 7.2 us -> 2.12 us  [local(): lax.all_to_all(item_grads, 'tm', split_axis=0, concat_axis=0, tiled=True)]
    ppermute x15, waiting for transfers between devices: 22.6 us -> 26.5 us  [swap(): return lax.ppermute(array, axis, [(i, i ^ mask) for i in range(16)])]
  transfers between devices with their start and end apart: 23 -> 23, of which waited for: 14 -> 16; matrix products, arithmetic and copies ran while one was open for 3% -> 2% of each run, Pallas kernels for 9% -> 7%
where the time goes in v5:
time: 96 us; the launch traced here: 95.7 us
  waiting for transfers between devices  42.2 us (44%)
  starting transfers between devices  39.2 us (41%)
  Pallas kernels  11.7 us (12%)
  local copies, waits for them, and re-layouts  1.15 us (1%)
    ppermute x15, waiting for transfers between devices, swap(): return lax.ppermute(array, axis, [(i, i ^ mask) for i in range(16)])  26.5 us
    ppermute x15, starting transfers between devices, swap(): return lax.ppermute(array, axis, [(i, i ^ mask) for i in range(16)])  19.8 us
    ppermute x6, starting transfers between devices, shift(): lax.ppermute(array, 'tm', [(i, (i + 4 * by) % 16) for i in range(16)])  11.7 us
    all_to_all x1, waiting for transfers between devices, local(): qkv = lax.all_to_all(qkv, 'tm', split_axis=0, concat_axis=0, tiled=True)  10 us
    pallas_call x1, Pallas kernels, backward(): pl.pallas_call(functools.partial(backward_kernel, places), out_shape=jax....  4.1 us
    all_to_all x1, starting transfers between devices, local(): qkv = lax.all_to_all(qkv, 'tm', split_axis=0, concat_axis=0, tiled=True)  4.04 us
    all_to_all x1, starting transfers between devices, local(): lax.all_to_all(item_grads, 'tm', split_axis=0, concat_axis=0, tiled=True)  3.61 us
    ppermute x6, waiting for transfers between devices, shift(): lax.ppermute(array, 'tm', [(i, (i + 4 * by) % 16) for i in range(16)])  3.56 us
  transfers between devices with their start and end apart: 23, of which 16 were waited for; matrix products, arithmetic and copies ran while one was open for 2% of the time, Pallas kernels for 7%

profile of v5, /device:TPU:48, one launch (start us, length us, event | category | flops | bytes accessed | tf_op | source)
XLA Modules:
  0.0 95.7 jit_solution(3569778454254108292)
XLA Ops:
  0.6 6.4 %collective-permute-start = (bf16[64,2,1024]{2,1,0:T(2,128)(2,1)}, bf16[64,2,1024]{2,1,0:T(2,128)(2,1)S(1)}, u32[]{:S(2)}, u32[]{:S(2)}) collective-permute-start(bf16[64,2,1024]{2,1,0:T(2,128)(2,1)} %bitcast.68), channel_id=1, source_target_pairs={{0,32},{16,48},{32,0},{48,16},{64,96},{80,112},{96,64},{112,80},{1... | collective-permute-start | bytes 786440 | tf_op jit(solution)/shard_map/ppermute | solution.py:249
  7.0 2.5 %prepare.1 = (bf16[16,3,64,128]{3,2,1,0:T(8,128)(2,1)}, bf16[64,1024]{1,0:T(8,128)(2,1)}, bf16[64,1024]{1,0:T(8,128)(2,1)}) custom-call(bf16[64,2,1024]{2,1,0:T(2,128)(2,1)} %bitcast.65, bf16[64,2,1024]{2,1,0:T(2,128)(2,1)} %bitcast.66, bf16[64,2,1024]{2,1,0:T(2,128)(2,1)} %bitcast.67, bf16[64,2,1024]{2,1,0:T(2,128)(2,1)} %bitcast.69), custom_call_target="tpu_custom_call" | custom-call | tf_op jit(solution)/shard_map/prepare/pallas_call | solution.py:225
  12.2 1.5 %collective-permute-start.4 = (bf16[128,1024]{1,0:T(8,128)(2,1)S(1)}, bf16[128,1024]{1,0:T(8,128)(2,1)S(1)}, u32[]{:S(2)}, u32[]{:S(2)}) collective-permute-start(bf16[128,1024]{1,0:T(8,128)(2,1)S(1)} %constant_dynamic-update-slice_fusion.refs_0_), channel_id=1, source_target_pairs={{0,64},{16,80},{32,96},{48,112},{64,128},{80,144},{96,160},{112,17... | collective-permute-start | bytes 786440 | tf_op jit(solution)/shard_map/ppermute | solution.py:253
  13.7 2.7 %collective-permute-start.5 = (bf16[128,1024]{1,0:T(8,128)(2,1)S(1)}, bf16[128,1024]{1,0:T(8,128)(2,1)S(1)}, u32[]{:S(2)}, u32[]{:S(2)}) collective-permute-start(bf16[128,1024]{1,0:T(8,128)(2,1)S(1)} %constant_dynamic-update-slice_fusion.refs_0_), channel_id=1, source_target_pairs={{0,128},{16,144},{32,160},{48,176},{64,192},{80,208},{96,224},{112... | collective-permute-start | bytes 786440 | tf_op jit(solution)/shard_map/ppermute | solution.py:253
  16.4 1.4 %collective-permute-start.6 = (bf16[128,1024]{1,0:T(8,128)(2,1)S(1)}, bf16[128,1024]{1,0:T(8,128)(2,1)S(1)}, u32[]{:S(2)}, u32[]{:S(2)}) collective-permute-start(bf16[128,1024]{1,0:T(8,128)(2,1)S(1)} %constant_dynamic-update-slice_fusion.refs_0_), channel_id=1, source_target_pairs={{0,192},{16,208},{32,224},{48,240},{64,0},{80,16},{96,32},{112,48}... | collective-permute-start | bytes 786440 | tf_op jit(solution)/shard_map/ppermute | solution.py:253
  17.9 1.6 %collective-permute-done.2 = bf16[64,128]{1,0:T(8,128)(2,1)S(1)} collective-permute-done((bf16[64,128]{1,0:T(8,128)(2,1)S(1)}, bf16[64,128]{1,0:T(8,128)(2,1)S(1)}, u32[]{:S(2)}, u32[]{:S(2)}) %collective-permute-start.2) | collective-permute-done | bytes 16416 | tf_op jit(solution)/shard_map/ppermute | solution.py:249
  19.5 2.0 %collective-permute-start.3 = (bf16[128,128]{1,0:T(8,128)(2,1)S(1)}, bf16[128,128]{1,0:T(8,128)(2,1)S(1)}, u32[]{:S(2)}, u32[]{:S(2)}) collective-permute-start(bf16[128,128]{1,0:T(8,128)(2,1)S(1)} %pad_maximum_fusion), channel_id=1, source_target_pairs={{0,8},{1,9},{2,10},{3,11},{4,12},{5,13},{6,14},{7,15},{8,0},{9,1},... | collective-permute-start | bytes 98312 | tf_op jit(solution)/shard_map/ppermute | solution.py:249
  21.6 2.8 %collective-permute-done.3 = bf16[128,128]{1,0:T(8,128)(2,1)S(1)} collective-permute-done((bf16[128,128]{1,0:T(8,128)(2,1)S(1)}, bf16[128,128]{1,0:T(8,128)(2,1)S(1)}, u32[]{:S(2)}, u32[]{:S(2)}) %collective-permute-start.3) | collective-permute-done | bytes 32800 | tf_op jit(solution)/shard_map/ppermute | solution.py:249
  24.6 3.5 %collective-permute-done.5.refs_2_ = bf16[128,1024]{1,0:T(8,128)(2,1)S(1)} collective-permute-done((bf16[128,1024]{1,0:T(8,128)(2,1)S(1)}, bf16[128,1024]{1,0:T(8,128)(2,1)S(1)}, u32[]{:S(2)}, u32[]{:S(2)}) %collective-permute-start.5) | collective-permute-done | bytes 262176 | tf_op jit(solution)/shard_map/ppermute | solution.py:253
  28.1 4.0 %all-to-all-start = ((bf16[16,3,64,128]{3,2,1,0:T(8,128)(2,1)}), bf16[16,3,64,128]{3,2,1,0:T(8,128)(2,1)S(1)}, u32[]{:S(2)}, u32[]{:S(2)}) async-start(bf16[16,3,64,128]{3,2,1,0:T(8,128)(2,1)} %get-tuple-element.25), calls=%async_computation | async-start | bytes 1572864 | tf_op jit(solution)/shard_map/all_to_all | solution.py:288
  33.6 1.9 %collective-permute-start.11 = (bf16[128,1024]{1,0:T(8,128)(2,1)S(1)}, bf16[128,1024]{1,0:T(8,128)(2,1)S(1)}, u32[]{:S(2)}, u32[]{:S(2)}) collective-permute-start(bf16[128,1024]{1,0:T(8,128)(2,1)S(1)} %constant_dynamic-update-slice_fusion.5.refs_4_), channel_id=1, source_target_pairs={{0,64},{16,80},{32,96},{48,112},{64,128},{80,144},{96,160},{112,17... | collective-permute-start | bytes 786440 | tf_op jit(solution)/shard_map/ppermute | solution.py:253
  35.5 2.7 %collective-permute-start.12 = (bf16[128,1024]{1,0:T(8,128)(2,1)S(1)}, bf16[128,1024]{1,0:T(8,128)(2,1)S(1)}, u32[]{:S(2)}, u32[]{:S(2)}) collective-permute-start(bf16[128,1024]{1,0:T(8,128)(2,1)S(1)} %constant_dynamic-update-slice_fusion.5.refs_4_), channel_id=1, source_target_pairs={{0,128},{16,144},{32,160},{48,176},{64,192},{80,208},{96,224},{112... | collective-permute-start | bytes 786440 | tf_op jit(solution)/shard_map/ppermute | solution.py:253
  38.2 1.5 %collective-permute-start.13 = (bf16[128,1024]{1,0:T(8,128)(2,1)S(1)}, bf16[128,1024]{1,0:T(8,128)(2,1)S(1)}, u32[]{:S(2)}, u32[]{:S(2)}) collective-permute-start(bf16[128,1024]{1,0:T(8,128)(2,1)S(1)} %constant_dynamic-update-slice_fusion.5.refs_4_), channel_id=1, source_target_pairs={{0,192},{16,208},{32,224},{48,240},{64,0},{80,16},{96,32},{112,48}... | collective-permute-start | bytes 786440 | tf_op jit(solution)/shard_map/ppermute | solution.py:253
  39.7 1.3 %collective-permute-start.7 = (bf16[256,128]{1,0:T(8,128)(2,1)S(1)}, bf16[256,128]{1,0:T(8,128)(2,1)S(1)}, u32[]{:S(2)}, u32[]{:S(2)}) collective-permute-start(bf16[256,128]{1,0:T(8,128)(2,1)S(1)} %constant_dynamic-update-slice_fusion.2.refs_8_), channel_id=1, source_target_pairs={{0,1},{1,0},{2,3},{3,2},{4,5},{5,4},{6,7},{7,6},{8,9},{9,8},{10,11... | collective-permute-start | bytes 196616 | tf_op jit(solution)/shard_map/ppermute | solution.py:249
  41.6 2.4 %collective-permute-done.7.refs_9_ = bf16[256,128]{1,0:T(8,128)(2,1)S(1)} collective-permute-done((bf16[256,128]{1,0:T(8,128)(2,1)S(1)}, bf16[256,128]{1,0:T(8,128)(2,1)S(1)}, u32[]{:S(2)}, u32[]{:S(2)}) %collective-permute-start.7) | collective-permute-done | bytes 65568 | tf_op jit(solution)/shard_map/ppermute | solution.py:249
  44.4 2.3 %collective-permute-done.8.refs_10_ = bf16[256,128]{1,0:T(8,128)(2,1)S(1)} collective-permute-done((bf16[256,128]{1,0:T(8,128)(2,1)S(1)}, bf16[256,128]{1,0:T(8,128)(2,1)S(1)}, u32[]{:S(2)}, u32[]{:S(2)}) %collective-permute-start.8) | collective-permute-done | bytes 65568 | tf_op jit(solution)/shard_map/ppermute | solution.py:249
  46.7 1.5 %collective-permute-done.9.refs_11_ = bf16[256,128]{1,0:T(8,128)(2,1)S(1)} collective-permute-done((bf16[256,128]{1,0:T(8,128)(2,1)S(1)}, bf16[256,128]{1,0:T(8,128)(2,1)S(1)}, u32[]{:S(2)}, u32[]{:S(2)}) %collective-permute-start.9) | collective-permute-done | bytes 65568 | tf_op jit(solution)/shard_map/ppermute | solution.py:249
  48.2 10.0 %all-to-all-done.qkv_ref = bf16[16,3,64,128]{3,2,1,0:T(8,128)(2,1)S(1)} async-done(((bf16[16,3,64,128]{3,2,1,0:T(8,128)(2,1)}), bf16[16,3,64,128]{3,2,1,0:T(8,128)(2,1)S(1)}, u32[]{:S(2)}, u32[]{:S(2)}) %all-to-all-start) | async-done | bytes 786464 | tf_op jit(solution)/shard_map/all_to_all | solution.py:288
  58.2 2.2 %forward.1 = (bf16[1024,128]{1,0:T(8,128)(2,1)S(1)}, f32[1024,1]{1,0:T(8,128)S(1)}) custom-call(bf16[16,3,64,128]{3,2,1,0:T(8,128)(2,1)S(1)} %all-to-all-done.qkv_ref), custom_call_target="tpu_custom_call" | custom-call | flops 536870912 | bytes 2097152 | tf_op jit(solution)/shard_map/forward/pallas_call | solution.py:133
  60.5 4.1 %backward.1 = bf16[16,3,64,128]{3,2,1,0:T(8,128)(2,1)} custom-call(bf16[16,3,64,128]{3,2,1,0:T(8,128)(2,1)S(1)} %all-to-all-done.qkv_ref, f32[1024,1]{1,0:T(8,128)S(1)} %get-tuple-element.28.lse_ref, bf16[128,1024]{1,0:T(8,128)(2,1)S(1)} %constant_dynamic-update-slice_fusion.refs_0_, bf16[128,1024]{1,0:T(8,128)(2,1)S(1)} %collective-permute-done.4.refs_1_, ...), custom_call_target="tpu_custom_call" | custom-call | flops 1610612736 | bytes 4194304 | tf_op jit(solution)/shard_map/backward/pallas_call | solution.py:164
  64.6 3.6 %all-to-all-start.1 = ((bf16[16,3,64,128]{3,2,1,0:T(8,128)(2,1)}), bf16[16,3,64,128]{3,2,1,0:T(8,128)(2,1)S(1)}, u32[]{:S(2)}, u32[]{:S(2)}) async-start(bf16[16,3,64,128]{3,2,1,0:T(8,128)(2,1)} %backward.1), calls=%async_computation.1 | async-start | bytes 1572864 | tf_op jit(solution)/shard_map/all_to_all | solution.py:310
  68.2 1.5 %weight_term.1 = (f32[64,1024]{1,0:T(8,128)S(1)}, f32[64,1024]{1,0:T(8,128)}) custom-call(bf16[1024,128]{1,0:T(8,128)(2,1)S(1)} %get-tuple-element.33.att_ref, bf16[128,1024]{1,0:T(8,128)(2,1)S(1)} %constant_dynamic-update-slice_fusion.refs_0_, bf16[128,1024]{1,0:T(8,128)(2,1)S(1)} %collective-permute-done.4.refs_1_, ...), custom_call_target="tpu_custom_call" | custom-call | flops 268435456 | bytes 3145728 | tf_op jit(solution)/shard_map/weight_term/pallas_call | solution.py:150
  70.1 1.4 %collective-permute-done.14 = f32[64,1024]{1,0:T(8,128)S(1)} collective-permute-done((f32[64,1024]{1,0:T(8,128)}, f32[64,1024]{1,0:T(8,128)S(1)}, u32[]{:S(2)}, u32[]{:S(2)}) %collective-permute-start.14) | collective-permute-done | bytes 262176 | tf_op jit(solution)/shard_map/ppermute | solution.py:249
  71.6 1.4 %collective-permute-start.15 = (f32[4,4,1024]{2,1,0:T(4,128)S(1)}, f32[4,4,1024]{2,1,0:T(4,128)S(1)}, u32[]{:S(2)}, u32[]{:S(2)}) collective-permute-start(f32[4,4,1024]{2,1,0:T(4,128)S(1)} %get-tuple-element.40), channel_id=1, source_target_pairs={{0,1},{1,0},{2,3},{3,2},{4,5},{5,4},{6,7},{7,6},{8,9},{9,8},{10,11... | collective-permute-start | bytes 196616 | tf_op jit(solution)/shard_map/ppermute | solution.py:249
  73.6 1.7 %collective-permute-start.17 = (f32[4,4,1024]{2,1,0:T(4,128)S(1)}, f32[4,4,1024]{2,1,0:T(4,128)S(1)}, u32[]{:S(2)}, u32[]{:S(2)}) collective-permute-start(f32[4,4,1024]{2,1,0:T(4,128)S(1)} %add_bitcast_fusion), channel_id=1, source_target_pairs={{0,3},{1,2},{2,1},{3,0},{4,7},{5,6},{6,5},{7,4},{8,11},{9,10},{10,... | collective-permute-start | bytes 196616 | tf_op jit(solution)/shard_map/ppermute | solution.py:249
  75.3 1.3 %collective-permute-done.15 = f32[4,4,1024]{2,1,0:T(4,128)S(1)} collective-permute-done((f32[4,4,1024]{2,1,0:T(4,128)S(1)}, f32[4,4,1024]{2,1,0:T(4,128)S(1)}, u32[]{:S(2)}, u32[]{:S(2)}) %collective-permute-start.15) | collective-permute-done | bytes 65568 | tf_op jit(solution)/shard_map/ppermute | solution.py:249
  76.6 2.2 %collective-permute-done.16 = f32[4,4,1024]{2,1,0:T(4,128)S(1)} collective-permute-done((f32[4,4,1024]{2,1,0:T(4,128)S(1)}, f32[4,4,1024]{2,1,0:T(4,128)S(1)}, u32[]{:S(2)}, u32[]{:S(2)}) %collective-permute-start.16) | collective-permute-done | bytes 65568 | tf_op jit(solution)/shard_map/ppermute | solution.py:249
  80.2 2.5 %collective-permute-start.19 = (f32[4,1024]{1,0:T(4,128)S(1)}, f32[4,1024]{1,0:T(4,128)S(1)}, u32[]{:S(2)}, u32[]{:S(2)}) collective-permute-start(f32[4,1024]{1,0:T(4,128)S(1)} %get-tuple-element.44), channel_id=1, source_target_pairs={{0,8},{1,9},{2,10},{3,11},{4,12},{5,13},{6,14},{7,15},{8,0},{9,1},... | collective-permute-start | bytes 49160 | tf_op jit(solution)/shard_map/ppermute | solution.py:249
  82.8 4.2 %collective-permute-done.18 = f32[4,1024]{1,0:T(4,128)S(1)} collective-permute-done((f32[4,1024]{1,0:T(4,128)S(1)}, f32[4,1024]{1,0:T(4,128)S(1)}, u32[]{:S(2)}, u32[]{:S(2)}) %collective-permute-start.18) | collective-permute-done | bytes 16416 | tf_op jit(solution)/shard_map/ppermute | solution.py:249
  87.0 4.9 %collective-permute-done.20 = f32[4,1024]{1,0:T(4,128)S(1)} collective-permute-done((f32[4,1024]{1,0:T(4,128)S(1)}, f32[4,1024]{1,0:T(4,128)S(1)}, u32[]{:S(2)}, u32[]{:S(2)}) %collective-permute-start.20) | collective-permute-done | bytes 16416 | tf_op jit(solution)/shard_map/ppermute | solution.py:249
  92.5 2.1 %all-to-all-done.1.in_ref = bf16[16,3,64,128]{3,2,1,0:T(8,128)(2,1)S(1)} async-done(((bf16[16,3,64,128]{3,2,1,0:T(8,128)(2,1)}), bf16[16,3,64,128]{3,2,1,0:T(8,128)(2,1)S(1)}, u32[]{:S(2)}, u32[]{:S(2)}) %all-to-all-start.1) | async-done | bytes 786464 | tf_op jit(solution)/shard_map/all_to_all | solution.py:310
  94.6 1.1 %unpack.1 = (bf16[64,2,1024]{2,1,0:T(2,128)(2,1)}, bf16[64,2,1024]{2,1,0:T(2,128)(2,1)}, bf16[64,2,1024]{2,1,0:T(2,128)(2,1)}) custom-call(bf16[16,3,64,128]{3,2,1,0:T(8,128)(2,1)S(1)} %all-to-all-done.1.in_ref), custom_call_target="tpu_custom_call" | custom-call | tf_op jit(solution)/shard_map/unpack/pallas_call | solution.py:243
  (38 shorter events, 8.7 us)
Async XLA Ops:
  0.6 8.9 %copy-start = (bf16[1024,64]{0,1:T(8,128)(2,1)S(1)}, bf16[1024,64]{0,1:T(8,128)(2,1)}, u32[]{:S(2)}) copy-start(bf16[1024,64]{0,1:T(8,128)(2,1)} %param.9) | copy-start | bytes 393220
  0.6 23.7 %collective-permute-start = (bf16[64,2,1024]{2,1,0:T(2,128)(2,1)}, bf16[64,2,1024]{2,1,0:T(2,128)(2,1)S(1)}, u32[]{:S(2)}, u32[]{:S(2)}) collective-permute-start(bf16[64,2,1024]{2,1,0:T(2,128)(2,1)} %bitcast.68), channel_id=1, source_target_pairs={{0,32},{16,48},{32,0},{48,16},{64,96},{80,112},{96,64},{112,80},{1... | collective-permute-start | bytes 786440 | tf_op jit(solution)/shard_map/ppermute | solution.py:249
  9.5 1.6 %collective-permute-start.1 = (bf16[64,1024]{1,0:T(8,128)(2,1)}, bf16[64,1024]{1,0:T(8,128)(2,1)S(1)}, u32[]{:S(2)}, u32[]{:S(2)}) collective-permute-start(bf16[64,1024]{1,0:T(8,128)(2,1)} %get-tuple-element.23), channel_id=1, source_target_pairs={{0,16},{16,0},{32,48},{48,32},{64,80},{80,64},{96,112},{112,96},{1... | collective-permute-start | bytes 393224 | tf_op jit(solution)/shard_map/ppermute | solution.py:249
  11.1 8.4 %collective-permute-start.2 = (bf16[64,128]{1,0:T(8,128)(2,1)S(1)}, bf16[64,128]{1,0:T(8,128)(2,1)S(1)}, u32[]{:S(2)}, u32[]{:S(2)}) collective-permute-start(bf16[64,128]{1,0:T(8,128)(2,1)S(1)} %dynamic-slice_bitcast_fusion.3), channel_id=1, source_target_pairs={{0,4},{1,5},{2,6},{3,7},{4,0},{5,1},{6,2},{7,3},{8,12},{9,13},{10,... | collective-permute-start | bytes 49160 | tf_op jit(solution)/shard_map/ppermute | solution.py:249
  12.2 12.3 %collective-permute-start.4 = (bf16[128,1024]{1,0:T(8,128)(2,1)S(1)}, bf16[128,1024]{1,0:T(8,128)(2,1)S(1)}, u32[]{:S(2)}, u32[]{:S(2)}) collective-permute-start(bf16[128,1024]{1,0:T(8,128)(2,1)S(1)} %constant_dynamic-update-slice_fusion.refs_0_), channel_id=1, source_target_pairs={{0,64},{16,80},{32,96},{48,112},{64,128},{80,144},{96,160},{112,17... | collective-permute-start | bytes 786440 | tf_op jit(solution)/shard_map/ppermute | solution.py:253
  13.7 14.4 %collective-permute-start.5 = (bf16[128,1024]{1,0:T(8,128)(2,1)S(1)}, bf16[128,1024]{1,0:T(8,128)(2,1)S(1)}, u32[]{:S(2)}, u32[]{:S(2)}) collective-permute-start(bf16[128,1024]{1,0:T(8,128)(2,1)S(1)} %constant_dynamic-update-slice_fusion.refs_0_), channel_id=1, source_target_pairs={{0,128},{16,144},{32,160},{48,176},{64,192},{80,208},{96,224},{112... | collective-permute-start | bytes 786440 | tf_op jit(solution)/shard_map/ppermute | solution.py:253
  16.4 11.7 %collective-permute-start.6 = (bf16[128,1024]{1,0:T(8,128)(2,1)S(1)}, bf16[128,1024]{1,0:T(8,128)(2,1)S(1)}, u32[]{:S(2)}, u32[]{:S(2)}) collective-permute-start(bf16[128,1024]{1,0:T(8,128)(2,1)S(1)} %constant_dynamic-update-slice_fusion.refs_0_), channel_id=1, source_target_pairs={{0,192},{16,208},{32,224},{48,240},{64,0},{80,16},{96,32},{112,48}... | collective-permute-start | bytes 786440 | tf_op jit(solution)/shard_map/ppermute | solution.py:253
  19.5 4.8 %collective-permute-start.3 = (bf16[128,128]{1,0:T(8,128)(2,1)S(1)}, bf16[128,128]{1,0:T(8,128)(2,1)S(1)}, u32[]{:S(2)}, u32[]{:S(2)}) collective-permute-start(bf16[128,128]{1,0:T(8,128)(2,1)S(1)} %pad_maximum_fusion), channel_id=1, source_target_pairs={{0,8},{1,9},{2,10},{3,11},{4,12},{5,13},{6,14},{7,15},{8,0},{9,1},... | collective-permute-start | bytes 98312 | tf_op jit(solution)/shard_map/ppermute | solution.py:249
  28.1 30.1 %all-to-all-start = ((bf16[16,3,64,128]{3,2,1,0:T(8,128)(2,1)}), bf16[16,3,64,128]{3,2,1,0:T(8,128)(2,1)S(1)}, u32[]{:S(2)}, u32[]{:S(2)}) async-start(bf16[16,3,64,128]{3,2,1,0:T(8,128)(2,1)} %get-tuple-element.25), calls=%async_computation | async-start | bytes 1572864 | tf_op jit(solution)/shard_map/all_to_all | solution.py:288
  32.2 1.4 %collective-permute-start.10 = (bf16[64,1024]{1,0:T(8,128)(2,1)S(1)}, bf16[64,1024]{1,0:T(8,128)(2,1)S(1)}, u32[]{:S(2)}, u32[]{:S(2)}) collective-permute-start(bf16[64,1024]{1,0:T(8,128)(2,1)S(1)} %get-tuple-element.29), channel_id=1, source_target_pairs={{0,16},{16,0},{32,48},{48,32},{64,80},{80,64},{96,112},{112,96},{1... | collective-permute-start | bytes 393224 | tf_op jit(solution)/shard_map/ppermute | solution.py:249
  33.6 26.8 %collective-permute-start.11 = (bf16[128,1024]{1,0:T(8,128)(2,1)S(1)}, bf16[128,1024]{1,0:T(8,128)(2,1)S(1)}, u32[]{:S(2)}, u32[]{:S(2)}) collective-permute-start(bf16[128,1024]{1,0:T(8,128)(2,1)S(1)} %constant_dynamic-update-slice_fusion.5.refs_4_), channel_id=1, source_target_pairs={{0,64},{16,80},{32,96},{48,112},{64,128},{80,144},{96,160},{112,17... | collective-permute-start | bytes 786440 | tf_op jit(solution)/shard_map/ppermute | solution.py:253
  35.5 24.9 %collective-permute-start.12 = (bf16[128,1024]{1,0:T(8,128)(2,1)S(1)}, bf16[128,1024]{1,0:T(8,128)(2,1)S(1)}, u32[]{:S(2)}, u32[]{:S(2)}) collective-permute-start(bf16[128,1024]{1,0:T(8,128)(2,1)S(1)} %constant_dynamic-update-slice_fusion.5.refs_4_), channel_id=1, source_target_pairs={{0,128},{16,144},{32,160},{48,176},{64,192},{80,208},{96,224},{112... | collective-permute-start | bytes 786440 | tf_op jit(solution)/shard_map/ppermute | solution.py:253
  38.2 22.2 %collective-permute-start.13 = (bf16[128,1024]{1,0:T(8,128)(2,1)S(1)}, bf16[128,1024]{1,0:T(8,128)(2,1)S(1)}, u32[]{:S(2)}, u32[]{:S(2)}) collective-permute-start(bf16[128,1024]{1,0:T(8,128)(2,1)S(1)} %constant_dynamic-update-slice_fusion.5.refs_4_), channel_id=1, source_target_pairs={{0,192},{16,208},{32,224},{48,240},{64,0},{80,16},{96,32},{112,48}... | collective-permute-start | bytes 786440 | tf_op jit(solution)/shard_map/ppermute | solution.py:253
  39.7 4.3 %collective-permute-start.7 = (bf16[256,128]{1,0:T(8,128)(2,1)S(1)}, bf16[256,128]{1,0:T(8,128)(2,1)S(1)}, u32[]{:S(2)}, u32[]{:S(2)}) collective-permute-start(bf16[256,128]{1,0:T(8,128)(2,1)S(1)} %constant_dynamic-update-slice_fusion.2.refs_8_), channel_id=1, source_target_pairs={{0,1},{1,0},{2,3},{3,2},{4,5},{5,4},{6,7},{7,6},{8,9},{9,8},{10,11... | collective-permute-start | bytes 196616 | tf_op jit(solution)/shard_map/ppermute | solution.py:249
  40.9 5.8 %collective-permute-start.8 = (bf16[256,128]{1,0:T(8,128)(2,1)S(1)}, bf16[256,128]{1,0:T(8,128)(2,1)S(1)}, u32[]{:S(2)}, u32[]{:S(2)}) collective-permute-start(bf16[256,128]{1,0:T(8,128)(2,1)S(1)} %constant_dynamic-update-slice_fusion.2.refs_8_), channel_id=1, source_target_pairs={{0,2},{1,3},{2,0},{3,1},{4,6},{5,7},{6,4},{7,5},{8,10},{9,11},{10,... | collective-permute-start | bytes 196616 | tf_op jit(solution)/shard_map/ppermute | solution.py:249
  43.9 4.3 %collective-permute-start.9 = (bf16[256,128]{1,0:T(8,128)(2,1)S(1)}, bf16[256,128]{1,0:T(8,128)(2,1)S(1)}, u32[]{:S(2)}, u32[]{:S(2)}) collective-permute-start(bf16[256,128]{1,0:T(8,128)(2,1)S(1)} %constant_dynamic-update-slice_fusion.2.refs_8_), channel_id=1, source_target_pairs={{0,3},{1,2},{2,1},{3,0},{4,7},{5,6},{6,5},{7,4},{8,11},{9,10},{10,... | collective-permute-start | bytes 196616 | tf_op jit(solution)/shard_map/ppermute | solution.py:249
  64.6 30.1 %all-to-all-start.1 = ((bf16[16,3,64,128]{3,2,1,0:T(8,128)(2,1)}), bf16[16,3,64,128]{3,2,1,0:T(8,128)(2,1)S(1)}, u32[]{:S(2)}, u32[]{:S(2)}) async-start(bf16[16,3,64,128]{3,2,1,0:T(8,128)(2,1)} %backward.1), calls=%async_computation.1 | async-start | bytes 1572864 | tf_op jit(solution)/shard_map/all_to_all | solution.py:310
  69.7 1.7 %collective-permute-start.14 = (f32[64,1024]{1,0:T(8,128)}, f32[64,1024]{1,0:T(8,128)S(1)}, u32[]{:S(2)}, u32[]{:S(2)}) collective-permute-start(f32[64,1024]{1,0:T(8,128)} %get-tuple-element.35), channel_id=1, source_target_pairs={{0,16},{16,0},{32,48},{48,32},{64,80},{80,64},{96,112},{112,96},{1... | collective-permute-start | bytes 786440 | tf_op jit(solution)/shard_map/ppermute | solution.py:249
  71.6 5.0 %collective-permute-start.15 = (f32[4,4,1024]{2,1,0:T(4,128)S(1)}, f32[4,4,1024]{2,1,0:T(4,128)S(1)}, u32[]{:S(2)}, u32[]{:S(2)}) collective-permute-start(f32[4,4,1024]{2,1,0:T(4,128)S(1)} %get-tuple-element.40), channel_id=1, source_target_pairs={{0,1},{1,0},{2,3},{3,2},{4,5},{5,4},{6,7},{7,6},{8,9},{9,8},{10,11... | collective-permute-start | bytes 196616 | tf_op jit(solution)/shard_map/ppermute | solution.py:249
  73.0 5.8 %collective-permute-start.16 = (f32[4,4,1024]{2,1,0:T(4,128)S(1)}, f32[4,4,1024]{2,1,0:T(4,128)S(1)}, u32[]{:S(2)}, u32[]{:S(2)}) collective-permute-start(f32[4,4,1024]{2,1,0:T(4,128)S(1)} %get-tuple-element.41), channel_id=1, source_target_pairs={{0,2},{1,3},{2,0},{3,1},{4,6},{5,7},{6,4},{7,5},{8,10},{9,11},{10,... | collective-permute-start | bytes 196616 | tf_op jit(solution)/shard_map/ppermute | solution.py:249
  73.6 5.6 %collective-permute-start.17 = (f32[4,4,1024]{2,1,0:T(4,128)S(1)}, f32[4,4,1024]{2,1,0:T(4,128)S(1)}, u32[]{:S(2)}, u32[]{:S(2)}) collective-permute-start(f32[4,4,1024]{2,1,0:T(4,128)S(1)} %add_bitcast_fusion), channel_id=1, source_target_pairs={{0,3},{1,2},{2,1},{3,0},{4,7},{5,6},{6,5},{7,4},{8,11},{9,10},{10,... | collective-permute-start | bytes 196616 | tf_op jit(solution)/shard_map/ppermute | solution.py:249
  79.2 7.7 %collective-permute-start.18 = (f32[4,1024]{1,0:T(4,128)S(1)}, f32[4,1024]{1,0:T(4,128)S(1)}, u32[]{:S(2)}, u32[]{:S(2)}) collective-permute-start(f32[4,1024]{1,0:T(4,128)S(1)} %get-tuple-element.42), channel_id=1, source_target_pairs={{0,4},{1,5},{2,6},{3,7},{4,0},{5,1},{6,2},{7,3},{8,12},{9,13},{10,... | collective-permute-start | bytes 49160 | tf_op jit(solution)/shard_map/ppermute | solution.py:249
  80.2 6.8 %collective-permute-start.19 = (f32[4,1024]{1,0:T(4,128)S(1)}, f32[4,1024]{1,0:T(4,128)S(1)}, u32[]{:S(2)}, u32[]{:S(2)}) collective-permute-start(f32[4,1024]{1,0:T(4,128)S(1)} %get-tuple-element.44), channel_id=1, source_target_pairs={{0,8},{1,9},{2,10},{3,11},{4,12},{5,13},{6,14},{7,15},{8,0},{9,1},... | collective-permute-start | bytes 49160 | tf_op jit(solution)/shard_map/ppermute | solution.py:249
  82.7 9.2 %collective-permute-start.20 = (f32[4,1024]{1,0:T(4,128)S(1)}, f32[4,1024]{1,0:T(4,128)S(1)}, u32[]{:S(2)}, u32[]{:S(2)}) collective-permute-start(f32[4,1024]{1,0:T(4,128)S(1)} %get-tuple-element.43), channel_id=1, source_target_pairs={{0,12},{1,13},{2,14},{3,15},{4,8},{5,9},{6,10},{7,11},{8,4},{9,5},... | collective-permute-start | bytes 49160 | tf_op jit(solution)/shard_map/ppermute | solution.py:249

commit v6 on v5

--- a/solution.py
+++ b/solution.py
@@ -11,7 +11,7 @@
 HEADS = 8
 HEAD = 128
 BLOCK = 64
-ROWS = 256
+ROWS = 512
 
 
 def dot(a, b, ca, cb):

time: 96 us -> 95.7 us (level)
  no operation moved by 1% of the time
where the time goes in v6:
time: 95.7 us; the launch traced here: 95.4 us
  waiting for transfers between devices  42.3 us (44%)
  starting transfers between devices  39.2 us (41%)
  Pallas kernels  11.2 us (12%)
  local copies, waits for them, and re-layouts  1.15 us (1%)
    ppermute x15, waiting for transfers between devices, swap(): return lax.ppermute(array, axis, [(i, i ^ mask) for i in range(16)])  26.7 us
    ppermute x15, starting transfers between devices, swap(): return lax.ppermute(array, axis, [(i, i ^ mask) for i in range(16)])  19.8 us
    ppermute x6, starting transfers between devices, shift(): lax.ppermute(array, 'tm', [(i, (i + 4 * by) % 16) for i in range(16)])  11.7 us
    all_to_all x1, waiting for transfers between devices, local(): qkv = lax.all_to_all(qkv, 'tm', split_axis=0, concat_axis=0, tiled=True)  10 us
    all_to_all x1, starting transfers between devices, local(): qkv = lax.all_to_all(qkv, 'tm', split_axis=0, concat_axis=0, tiled=True)  4.04 us
    pallas_call x1, Pallas kernels, backward(): pl.pallas_call(functools.partial(backward_kernel, places), out_shape=jax....  3.79 us
    all_to_all x1, starting transfers between devices, local(): lax.all_to_all(item_grads, 'tm', split_axis=0, concat_axis=0, tiled=True)  3.61 us
    ppermute x6, waiting for transfers between devices, shift(): lax.ppermute(array, 'tm', [(i, (i + 4 * by) % 16) for i in range(16)])  3.56 us
  transfers between devices with their start and end apart: 23, of which 16 were waited for; matrix products, arithmetic and copies ran while one was open for 2% of the time, Pallas kernels for 7%

profile of v6, /device:TPU:48, one launch (start us, length us, event | category | flops | bytes accessed | tf_op | source)
XLA Modules:
  0.0 95.4 jit_solution(13481114241707035332)
XLA Ops:
  0.6 6.4 %collective-permute-start = (bf16[64,2,1024]{2,1,0:T(2,128)(2,1)}, bf16[64,2,1024]{2,1,0:T(2,128)(2,1)S(1)}, u32[]{:S(2)}, u32[]{:S(2)}) collective-permute-start(bf16[64,2,1024]{2,1,0:T(2,128)(2,1)} %bitcast.68), channel_id=1, source_target_pairs={{0,32},{16,48},{32,0},{48,16},{64,96},{80,112},{96,64},{112,80},{1... | collective-permute-start | bytes 786440 | tf_op jit(solution)/shard_map/ppermute | solution.py:249
  7.0 2.5 %prepare.1 = (bf16[16,3,64,128]{3,2,1,0:T(8,128)(2,1)}, bf16[64,1024]{1,0:T(8,128)(2,1)}, bf16[64,1024]{1,0:T(8,128)(2,1)}) custom-call(bf16[64,2,1024]{2,1,0:T(2,128)(2,1)} %bitcast.65, bf16[64,2,1024]{2,1,0:T(2,128)(2,1)} %bitcast.66, bf16[64,2,1024]{2,1,0:T(2,128)(2,1)} %bitcast.67, bf16[64,2,1024]{2,1,0:T(2,128)(2,1)} %bitcast.69), custom_call_target="tpu_custom_call" | custom-call | tf_op jit(solution)/shard_map/prepare/pallas_call | solution.py:225
  12.2 1.5 %collective-permute-start.4 = (bf16[128,1024]{1,0:T(8,128)(2,1)S(1)}, bf16[128,1024]{1,0:T(8,128)(2,1)S(1)}, u32[]{:S(2)}, u32[]{:S(2)}) collective-permute-start(bf16[128,1024]{1,0:T(8,128)(2,1)S(1)} %constant_dynamic-update-slice_fusion.refs_0_), channel_id=1, source_target_pairs={{0,64},{16,80},{32,96},{48,112},{64,128},{80,144},{96,160},{112,17... | collective-permute-start | bytes 786440 | tf_op jit(solution)/shard_map/ppermute | solution.py:253
  13.7 2.7 %collective-permute-start.5 = (bf16[128,1024]{1,0:T(8,128)(2,1)S(1)}, bf16[128,1024]{1,0:T(8,128)(2,1)S(1)}, u32[]{:S(2)}, u32[]{:S(2)}) collective-permute-start(bf16[128,1024]{1,0:T(8,128)(2,1)S(1)} %constant_dynamic-update-slice_fusion.refs_0_), channel_id=1, source_target_pairs={{0,128},{16,144},{32,160},{48,176},{64,192},{80,208},{96,224},{112... | collective-permute-start | bytes 786440 | tf_op jit(solution)/shard_map/ppermute | solution.py:253
  16.4 1.4 %collective-permute-start.6 = (bf16[128,1024]{1,0:T(8,128)(2,1)S(1)}, bf16[128,1024]{1,0:T(8,128)(2,1)S(1)}, u32[]{:S(2)}, u32[]{:S(2)}) collective-permute-start(bf16[128,1024]{1,0:T(8,128)(2,1)S(1)} %constant_dynamic-update-slice_fusion.refs_0_), channel_id=1, source_target_pairs={{0,192},{16,208},{32,224},{48,240},{64,0},{80,16},{96,32},{112,48}... | collective-permute-start | bytes 786440 | tf_op jit(solution)/shard_map/ppermute | solution.py:253
  17.9 1.6 %collective-permute-done.2 = bf16[64,128]{1,0:T(8,128)(2,1)S(1)} collective-permute-done((bf16[64,128]{1,0:T(8,128)(2,1)S(1)}, bf16[64,128]{1,0:T(8,128)(2,1)S(1)}, u32[]{:S(2)}, u32[]{:S(2)}) %collective-permute-start.2) | collective-permute-done | bytes 16416 | tf_op jit(solution)/shard_map/ppermute | solution.py:249
  19.5 2.0 %collective-permute-start.3 = (bf16[128,128]{1,0:T(8,128)(2,1)S(1)}, bf16[128,128]{1,0:T(8,128)(2,1)S(1)}, u32[]{:S(2)}, u32[]{:S(2)}) collective-permute-start(bf16[128,128]{1,0:T(8,128)(2,1)S(1)} %pad_maximum_fusion), channel_id=1, source_target_pairs={{0,8},{1,9},{2,10},{3,11},{4,12},{5,13},{6,14},{7,15},{8,0},{9,1},... | collective-permute-start | bytes 98312 | tf_op jit(solution)/shard_map/ppermute | solution.py:249
  21.6 2.8 %collective-permute-done.3 = bf16[128,128]{1,0:T(8,128)(2,1)S(1)} collective-permute-done((bf16[128,128]{1,0:T(8,128)(2,1)S(1)}, bf16[128,128]{1,0:T(8,128)(2,1)S(1)}, u32[]{:S(2)}, u32[]{:S(2)}) %collective-permute-start.3) | collective-permute-done | bytes 32800 | tf_op jit(solution)/shard_map/ppermute | solution.py:249
  24.6 3.5 %collective-permute-done.5.refs_2_ = bf16[128,1024]{1,0:T(8,128)(2,1)S(1)} collective-permute-done((bf16[128,1024]{1,0:T(8,128)(2,1)S(1)}, bf16[128,1024]{1,0:T(8,128)(2,1)S(1)}, u32[]{:S(2)}, u32[]{:S(2)}) %collective-permute-start.5) | collective-permute-done | bytes 262176 | tf_op jit(solution)/shard_map/ppermute | solution.py:253
  28.1 4.0 %all-to-all-start = ((bf16[16,3,64,128]{3,2,1,0:T(8,128)(2,1)}), bf16[16,3,64,128]{3,2,1,0:T(8,128)(2,1)S(1)}, u32[]{:S(2)}, u32[]{:S(2)}) async-start(bf16[16,3,64,128]{3,2,1,0:T(8,128)(2,1)} %get-tuple-element.25), calls=%async_computation | async-start | bytes 1572864 | tf_op jit(solution)/shard_map/all_to_all | solution.py:288
  33.6 1.9 %collective-permute-start.11 = (bf16[128,1024]{1,0:T(8,128)(2,1)S(1)}, bf16[128,1024]{1,0:T(8,128)(2,1)S(1)}, u32[]{:S(2)}, u32[]{:S(2)}) collective-permute-start(bf16[128,1024]{1,0:T(8,128)(2,1)S(1)} %constant_dynamic-update-slice_fusion.5.refs_4_), channel_id=1, source_target_pairs={{0,64},{16,80},{32,96},{48,112},{64,128},{80,144},{96,160},{112,17... | collective-permute-start | bytes 786440 | tf_op jit(solution)/shard_map/ppermute | solution.py:253
  35.5 2.7 %collective-permute-start.12 = (bf16[128,1024]{1,0:T(8,128)(2,1)S(1)}, bf16[128,1024]{1,0:T(8,128)(2,1)S(1)}, u32[]{:S(2)}, u32[]{:S(2)}) collective-permute-start(bf16[128,1024]{1,0:T(8,128)(2,1)S(1)} %constant_dynamic-update-slice_fusion.5.refs_4_), channel_id=1, source_target_pairs={{0,128},{16,144},{32,160},{48,176},{64,192},{80,208},{96,224},{112... | collective-permute-start | bytes 786440 | tf_op jit(solution)/shard_map/ppermute | solution.py:253
  38.2 1.5 %collective-permute-start.13 = (bf16[128,1024]{1,0:T(8,128)(2,1)S(1)}, bf16[128,1024]{1,0:T(8,128)(2,1)S(1)}, u32[]{:S(2)}, u32[]{:S(2)}) collective-permute-start(bf16[128,1024]{1,0:T(8,128)(2,1)S(1)} %constant_dynamic-update-slice_fusion.5.refs_4_), channel_id=1, source_target_pairs={{0,192},{16,208},{32,224},{48,240},{64,0},{80,16},{96,32},{112,48}... | collective-permute-start | bytes 786440 | tf_op jit(solution)/shard_map/ppermute | solution.py:253
  39.7 1.3 %collective-permute-start.7 = (bf16[256,128]{1,0:T(8,128)(2,1)S(1)}, bf16[256,128]{1,0:T(8,128)(2,1)S(1)}, u32[]{:S(2)}, u32[]{:S(2)}) collective-permute-start(bf16[256,128]{1,0:T(8,128)(2,1)S(1)} %constant_dynamic-update-slice_fusion.2.refs_8_), channel_id=1, source_target_pairs={{0,1},{1,0},{2,3},{3,2},{4,5},{5,4},{6,7},{7,6},{8,9},{9,8},{10,11... | collective-permute-start | bytes 196616 | tf_op jit(solution)/shard_map/ppermute | solution.py:249
  41.6 2.4 %collective-permute-done.7.refs_9_ = bf16[256,128]{1,0:T(8,128)(2,1)S(1)} collective-permute-done((bf16[256,128]{1,0:T(8,128)(2,1)S(1)}, bf16[256,128]{1,0:T(8,128)(2,1)S(1)}, u32[]{:S(2)}, u32[]{:S(2)}) %collective-permute-start.7) | collective-permute-done | bytes 65568 | tf_op jit(solution)/shard_map/ppermute | solution.py:249
  44.4 2.3 %collective-permute-done.8.refs_10_ = bf16[256,128]{1,0:T(8,128)(2,1)S(1)} collective-permute-done((bf16[256,128]{1,0:T(8,128)(2,1)S(1)}, bf16[256,128]{1,0:T(8,128)(2,1)S(1)}, u32[]{:S(2)}, u32[]{:S(2)}) %collective-permute-start.8) | collective-permute-done | bytes 65568 | tf_op jit(solution)/shard_map/ppermute | solution.py:249
  46.7 1.5 %collective-permute-done.9.refs_11_ = bf16[256,128]{1,0:T(8,128)(2,1)S(1)} collective-permute-done((bf16[256,128]{1,0:T(8,128)(2,1)S(1)}, bf16[256,128]{1,0:T(8,128)(2,1)S(1)}, u32[]{:S(2)}, u32[]{:S(2)}) %collective-permute-start.9) | collective-permute-done | bytes 65568 | tf_op jit(solution)/shard_map/ppermute | solution.py:249
  48.2 10.0 %all-to-all-done.qkv_ref = bf16[16,3,64,128]{3,2,1,0:T(8,128)(2,1)S(1)} async-done(((bf16[16,3,64,128]{3,2,1,0:T(8,128)(2,1)}), bf16[16,3,64,128]{3,2,1,0:T(8,128)(2,1)S(1)}, u32[]{:S(2)}, u32[]{:S(2)}) %all-to-all-start) | async-done | bytes 786464 | tf_op jit(solution)/shard_map/all_to_all | solution.py:288
  58.2 2.1 %forward.1 = (bf16[1024,128]{1,0:T(8,128)(2,1)S(1)}, f32[1024,1]{1,0:T(8,128)S(1)}) custom-call(bf16[16,3,64,128]{3,2,1,0:T(8,128)(2,1)S(1)} %all-to-all-done.qkv_ref), custom_call_target="tpu_custom_call" | custom-call | flops 536870912 | bytes 2097152 | tf_op jit(solution)/shard_map/forward/pallas_call | solution.py:133
  60.3 3.8 %backward.1 = bf16[16,3,64,128]{3,2,1,0:T(8,128)(2,1)} custom-call(bf16[16,3,64,128]{3,2,1,0:T(8,128)(2,1)S(1)} %all-to-all-done.qkv_ref, f32[1024,1]{1,0:T(8,128)S(1)} %get-tuple-element.28.lse_ref, bf16[128,1024]{1,0:T(8,128)(2,1)S(1)} %constant_dynamic-update-slice_fusion.refs_0_, bf16[128,1024]{1,0:T(8,128)(2,1)S(1)} %collective-permute-done.4.refs_1_, ...), custom_call_target="tpu_custom_call" | custom-call | flops 1610612736 | bytes 4194304 | tf_op jit(solution)/shard_map/backward/pallas_call | solution.py:164
  64.1 3.6 %all-to-all-start.1 = ((bf16[16,3,64,128]{3,2,1,0:T(8,128)(2,1)}), bf16[16,3,64,128]{3,2,1,0:T(8,128)(2,1)S(1)}, u32[]{:S(2)}, u32[]{:S(2)}) async-start(bf16[16,3,64,128]{3,2,1,0:T(8,128)(2,1)} %backward.1), calls=%async_computation.1 | async-start | bytes 1572864 | tf_op jit(solution)/shard_map/all_to_all | solution.py:310
  67.7 1.5 %weight_term.1 = (f32[64,1024]{1,0:T(8,128)S(1)}, f32[64,1024]{1,0:T(8,128)}) custom-call(bf16[1024,128]{1,0:T(8,128)(2,1)S(1)} %get-tuple-element.33.att_ref, bf16[128,1024]{1,0:T(8,128)(2,1)S(1)} %constant_dynamic-update-slice_fusion.refs_0_, bf16[128,1024]{1,0:T(8,128)(2,1)S(1)} %collective-permute-done.4.refs_1_, ...), custom_call_target="tpu_custom_call" | custom-call | flops 268435456 | bytes 3145728 | tf_op jit(solution)/shard_map/weight_term/pallas_call | solution.py:150
  69.6 1.4 %collective-permute-done.14 = f32[64,1024]{1,0:T(8,128)S(1)} collective-permute-done((f32[64,1024]{1,0:T(8,128)}, f32[64,1024]{1,0:T(8,128)S(1)}, u32[]{:S(2)}, u32[]{:S(2)}) %collective-permute-start.14) | collective-permute-done | bytes 262176 | tf_op jit(solution)/shard_map/ppermute | solution.py:249
  71.1 1.4 %collective-permute-start.15 = (f32[4,4,1024]{2,1,0:T(4,128)S(1)}, f32[4,4,1024]{2,1,0:T(4,128)S(1)}, u32[]{:S(2)}, u32[]{:S(2)}) collective-permute-start(f32[4,4,1024]{2,1,0:T(4,128)S(1)} %get-tuple-element.40), channel_id=1, source_target_pairs={{0,1},{1,0},{2,3},{3,2},{4,5},{5,4},{6,7},{7,6},{8,9},{9,8},{10,11... | collective-permute-start | bytes 196616 | tf_op jit(solution)/shard_map/ppermute | solution.py:249
  73.1 1.7 %collective-permute-start.17 = (f32[4,4,1024]{2,1,0:T(4,128)S(1)}, f32[4,4,1024]{2,1,0:T(4,128)S(1)}, u32[]{:S(2)}, u32[]{:S(2)}) collective-permute-start(f32[4,4,1024]{2,1,0:T(4,128)S(1)} %add_bitcast_fusion), channel_id=1, source_target_pairs={{0,3},{1,2},{2,1},{3,0},{4,7},{5,6},{6,5},{7,4},{8,11},{9,10},{10,... | collective-permute-start | bytes 196616 | tf_op jit(solution)/shard_map/ppermute | solution.py:249
  74.8 1.3 %collective-permute-done.15 = f32[4,4,1024]{2,1,0:T(4,128)S(1)} collective-permute-done((f32[4,4,1024]{2,1,0:T(4,128)S(1)}, f32[4,4,1024]{2,1,0:T(4,128)S(1)}, u32[]{:S(2)}, u32[]{:S(2)}) %collective-permute-start.15) | collective-permute-done | bytes 65568 | tf_op jit(solution)/shard_map/ppermute | solution.py:249
  76.1 2.2 %collective-permute-done.16 = f32[4,4,1024]{2,1,0:T(4,128)S(1)} collective-permute-done((f32[4,4,1024]{2,1,0:T(4,128)S(1)}, f32[4,4,1024]{2,1,0:T(4,128)S(1)}, u32[]{:S(2)}, u32[]{:S(2)}) %collective-permute-start.16) | collective-permute-done | bytes 65568 | tf_op jit(solution)/shard_map/ppermute | solution.py:249
  78.8 1.1 %collective-permute-start.18 = (f32[4,1024]{1,0:T(4,128)S(1)}, f32[4,1024]{1,0:T(4,128)S(1)}, u32[]{:S(2)}, u32[]{:S(2)}) collective-permute-start(f32[4,1024]{1,0:T(4,128)S(1)} %get-tuple-element.42), channel_id=1, source_target_pairs={{0,4},{1,5},{2,6},{3,7},{4,0},{5,1},{6,2},{7,3},{8,12},{9,13},{10,... | collective-permute-start | bytes 49160 | tf_op jit(solution)/shard_map/ppermute | solution.py:249
  79.9 2.3 %collective-permute-start.19 = (f32[4,1024]{1,0:T(4,128)S(1)}, f32[4,1024]{1,0:T(4,128)S(1)}, u32[]{:S(2)}, u32[]{:S(2)}) collective-permute-start(f32[4,1024]{1,0:T(4,128)S(1)} %get-tuple-element.44), channel_id=1, source_target_pairs={{0,8},{1,9},{2,10},{3,11},{4,12},{5,13},{6,14},{7,15},{8,0},{9,1},... | collective-permute-start | bytes 49160 | tf_op jit(solution)/shard_map/ppermute | solution.py:249
  82.4 4.2 %collective-permute-done.18 = f32[4,1024]{1,0:T(4,128)S(1)} collective-permute-done((f32[4,1024]{1,0:T(4,128)S(1)}, f32[4,1024]{1,0:T(4,128)S(1)}, u32[]{:S(2)}, u32[]{:S(2)}) %collective-permute-start.18) | collective-permute-done | bytes 16416 | tf_op jit(solution)/shard_map/ppermute | solution.py:249
  86.5 5.1 %collective-permute-done.20 = f32[4,1024]{1,0:T(4,128)S(1)} collective-permute-done((f32[4,1024]{1,0:T(4,128)S(1)}, f32[4,1024]{1,0:T(4,128)S(1)}, u32[]{:S(2)}, u32[]{:S(2)}) %collective-permute-start.20) | collective-permute-done | bytes 16416 | tf_op jit(solution)/shard_map/ppermute | solution.py:249
  92.3 2.0 %all-to-all-done.1.in_ref = bf16[16,3,64,128]{3,2,1,0:T(8,128)(2,1)S(1)} async-done(((bf16[16,3,64,128]{3,2,1,0:T(8,128)(2,1)}), bf16[16,3,64,128]{3,2,1,0:T(8,128)(2,1)S(1)}, u32[]{:S(2)}, u32[]{:S(2)}) %all-to-all-start.1) | async-done | bytes 786464 | tf_op jit(solution)/shard_map/all_to_all | solution.py:310
  (38 shorter events, 8.9 us)
Async XLA Ops:
  0.6 8.9 %copy-start = (bf16[1024,64]{0,1:T(8,128)(2,1)S(1)}, bf16[1024,64]{0,1:T(8,128)(2,1)}, u32[]{:S(2)}) copy-start(bf16[1024,64]{0,1:T(8,128)(2,1)} %param.9) | copy-start | bytes 393220
  0.6 23.7 %collective-permute-start = (bf16[64,2,1024]{2,1,0:T(2,128)(2,1)}, bf16[64,2,1024]{2,1,0:T(2,128)(2,1)S(1)}, u32[]{:S(2)}, u32[]{:S(2)}) collective-permute-start(bf16[64,2,1024]{2,1,0:T(2,128)(2,1)} %bitcast.68), channel_id=1, source_target_pairs={{0,32},{16,48},{32,0},{48,16},{64,96},{80,112},{96,64},{112,80},{1... | collective-permute-start | bytes 786440 | tf_op jit(solution)/shard_map/ppermute | solution.py:249
  9.5 1.6 %collective-permute-start.1 = (bf16[64,1024]{1,0:T(8,128)(2,1)}, bf16[64,1024]{1,0:T(8,128)(2,1)S(1)}, u32[]{:S(2)}, u32[]{:S(2)}) collective-permute-start(bf16[64,1024]{1,0:T(8,128)(2,1)} %get-tuple-element.23), channel_id=1, source_target_pairs={{0,16},{16,0},{32,48},{48,32},{64,80},{80,64},{96,112},{112,96},{1... | collective-permute-start | bytes 393224 | tf_op jit(solution)/shard_map/ppermute | solution.py:249
  11.1 8.4 %collective-permute-start.2 = (bf16[64,128]{1,0:T(8,128)(2,1)S(1)}, bf16[64,128]{1,0:T(8,128)(2,1)S(1)}, u32[]{:S(2)}, u32[]{:S(2)}) collective-permute-start(bf16[64,128]{1,0:T(8,128)(2,1)S(1)} %dynamic-slice_bitcast_fusion.3), channel_id=1, source_target_pairs={{0,4},{1,5},{2,6},{3,7},{4,0},{5,1},{6,2},{7,3},{8,12},{9,13},{10,... | collective-permute-start | bytes 49160 | tf_op jit(solution)/shard_map/ppermute | solution.py:249
  12.2 12.3 %collective-permute-start.4 = (bf16[128,1024]{1,0:T(8,128)(2,1)S(1)}, bf16[128,1024]{1,0:T(8,128)(2,1)S(1)}, u32[]{:S(2)}, u32[]{:S(2)}) collective-permute-start(bf16[128,1024]{1,0:T(8,128)(2,1)S(1)} %constant_dynamic-update-slice_fusion.refs_0_), channel_id=1, source_target_pairs={{0,64},{16,80},{32,96},{48,112},{64,128},{80,144},{96,160},{112,17... | collective-permute-start | bytes 786440 | tf_op jit(solution)/shard_map/ppermute | solution.py:253
  13.7 14.4 %collective-permute-start.5 = (bf16[128,1024]{1,0:T(8,128)(2,1)S(1)}, bf16[128,1024]{1,0:T(8,128)(2,1)S(1)}, u32[]{:S(2)}, u32[]{:S(2)}) collective-permute-start(bf16[128,1024]{1,0:T(8,128)(2,1)S(1)} %constant_dynamic-update-slice_fusion.refs_0_), channel_id=1, source_target_pairs={{0,128},{16,144},{32,160},{48,176},{64,192},{80,208},{96,224},{112... | collective-permute-start | bytes 786440 | tf_op jit(solution)/shard_map/ppermute | solution.py:253
  16.4 11.7 %collective-permute-start.6 = (bf16[128,1024]{1,0:T(8,128)(2,1)S(1)}, bf16[128,1024]{1,0:T(8,128)(2,1)S(1)}, u32[]{:S(2)}, u32[]{:S(2)}) collective-permute-start(bf16[128,1024]{1,0:T(8,128)(2,1)S(1)} %constant_dynamic-update-slice_fusion.refs_0_), channel_id=1, source_target_pairs={{0,192},{16,208},{32,224},{48,240},{64,0},{80,16},{96,32},{112,48}... | collective-permute-start | bytes 786440 | tf_op jit(solution)/shard_map/ppermute | solution.py:253
  19.5 4.8 %collective-permute-start.3 = (bf16[128,128]{1,0:T(8,128)(2,1)S(1)}, bf16[128,128]{1,0:T(8,128)(2,1)S(1)}, u32[]{:S(2)}, u32[]{:S(2)}) collective-permute-start(bf16[128,128]{1,0:T(8,128)(2,1)S(1)} %pad_maximum_fusion), channel_id=1, source_target_pairs={{0,8},{1,9},{2,10},{3,11},{4,12},{5,13},{6,14},{7,15},{8,0},{9,1},... | collective-permute-start | bytes 98312 | tf_op jit(solution)/shard_map/ppermute | solution.py:249
  28.1 30.1 %all-to-all-start = ((bf16[16,3,64,128]{3,2,1,0:T(8,128)(2,1)}), bf16[16,3,64,128]{3,2,1,0:T(8,128)(2,1)S(1)}, u32[]{:S(2)}, u32[]{:S(2)}) async-start(bf16[16,3,64,128]{3,2,1,0:T(8,128)(2,1)} %get-tuple-element.25), calls=%async_computation | async-start | bytes 1572864 | tf_op jit(solution)/shard_map/all_to_all | solution.py:288
  32.2 1.4 %collective-permute-start.10 = (bf16[64,1024]{1,0:T(8,128)(2,1)S(1)}, bf16[64,1024]{1,0:T(8,128)(2,1)S(1)}, u32[]{:S(2)}, u32[]{:S(2)}) collective-permute-start(bf16[64,1024]{1,0:T(8,128)(2,1)S(1)} %get-tuple-element.29), channel_id=1, source_target_pairs={{0,16},{16,0},{32,48},{48,32},{64,80},{80,64},{96,112},{112,96},{1... | collective-permute-start | bytes 393224 | tf_op jit(solution)/shard_map/ppermute | solution.py:249
  33.6 26.7 %collective-permute-start.11 = (bf16[128,1024]{1,0:T(8,128)(2,1)S(1)}, bf16[128,1024]{1,0:T(8,128)(2,1)S(1)}, u32[]{:S(2)}, u32[]{:S(2)}) collective-permute-start(bf16[128,1024]{1,0:T(8,128)(2,1)S(1)} %constant_dynamic-update-slice_fusion.5.refs_4_), channel_id=1, source_target_pairs={{0,64},{16,80},{32,96},{48,112},{64,128},{80,144},{96,160},{112,17... | collective-permute-start | bytes 786440 | tf_op jit(solution)/shard_map/ppermute | solution.py:253
  35.5 24.8 %collective-permute-start.12 = (bf16[128,1024]{1,0:T(8,128)(2,1)S(1)}, bf16[128,1024]{1,0:T(8,128)(2,1)S(1)}, u32[]{:S(2)}, u32[]{:S(2)}) collective-permute-start(bf16[128,1024]{1,0:T(8,128)(2,1)S(1)} %constant_dynamic-update-slice_fusion.5.refs_4_), channel_id=1, source_target_pairs={{0,128},{16,144},{32,160},{48,176},{64,192},{80,208},{96,224},{112... | collective-permute-start | bytes 786440 | tf_op jit(solution)/shard_map/ppermute | solution.py:253
  38.2 22.1 %collective-permute-start.13 = (bf16[128,1024]{1,0:T(8,128)(2,1)S(1)}, bf16[128,1024]{1,0:T(8,128)(2,1)S(1)}, u32[]{:S(2)}, u32[]{:S(2)}) collective-permute-start(bf16[128,1024]{1,0:T(8,128)(2,1)S(1)} %constant_dynamic-update-slice_fusion.5.refs_4_), channel_id=1, source_target_pairs={{0,192},{16,208},{32,224},{48,240},{64,0},{80,16},{96,32},{112,48}... | collective-permute-start | bytes 786440 | tf_op jit(solution)/shard_map/ppermute | solution.py:253
  39.7 4.3 %collective-permute-start.7 = (bf16[256,128]{1,0:T(8,128)(2,1)S(1)}, bf16[256,128]{1,0:T(8,128)(2,1)S(1)}, u32[]{:S(2)}, u32[]{:S(2)}) collective-permute-start(bf16[256,128]{1,0:T(8,128)(2,1)S(1)} %constant_dynamic-update-slice_fusion.2.refs_8_), channel_id=1, source_target_pairs={{0,1},{1,0},{2,3},{3,2},{4,5},{5,4},{6,7},{7,6},{8,9},{9,8},{10,11... | collective-permute-start | bytes 196616 | tf_op jit(solution)/shard_map/ppermute | solution.py:249
  40.9 5.8 %collective-permute-start.8 = (bf16[256,128]{1,0:T(8,128)(2,1)S(1)}, bf16[256,128]{1,0:T(8,128)(2,1)S(1)}, u32[]{:S(2)}, u32[]{:S(2)}) collective-permute-start(bf16[256,128]{1,0:T(8,128)(2,1)S(1)} %constant_dynamic-update-slice_fusion.2.refs_8_), channel_id=1, source_target_pairs={{0,2},{1,3},{2,0},{3,1},{4,6},{5,7},{6,4},{7,5},{8,10},{9,11},{10,... | collective-permute-start | bytes 196616 | tf_op jit(solution)/shard_map/ppermute | solution.py:249
  43.9 4.3 %collective-permute-start.9 = (bf16[256,128]{1,0:T(8,128)(2,1)S(1)}, bf16[256,128]{1,0:T(8,128)(2,1)S(1)}, u32[]{:S(2)}, u32[]{:S(2)}) collective-permute-start(bf16[256,128]{1,0:T(8,128)(2,1)S(1)} %constant_dynamic-update-slice_fusion.2.refs_8_), channel_id=1, source_target_pairs={{0,3},{1,2},{2,1},{3,0},{4,7},{5,6},{6,5},{7,4},{8,11},{9,10},{10,... | collective-permute-start | bytes 196616 | tf_op jit(solution)/shard_map/ppermute | solution.py:249
  64.1 30.2 %all-to-all-start.1 = ((bf16[16,3,64,128]{3,2,1,0:T(8,128)(2,1)}), bf16[16,3,64,128]{3,2,1,0:T(8,128)(2,1)S(1)}, u32[]{:S(2)}, u32[]{:S(2)}) async-start(bf16[16,3,64,128]{3,2,1,0:T(8,128)(2,1)} %backward.1), calls=%async_computation.1 | async-start | bytes 1572864 | tf_op jit(solution)/shard_map/all_to_all | solution.py:310
  69.2 1.7 %collective-permute-start.14 = (f32[64,1024]{1,0:T(8,128)}, f32[64,1024]{1,0:T(8,128)S(1)}, u32[]{:S(2)}, u32[]{:S(2)}) collective-permute-start(f32[64,1024]{1,0:T(8,128)} %get-tuple-element.35), channel_id=1, source_target_pairs={{0,16},{16,0},{32,48},{48,32},{64,80},{80,64},{96,112},{112,96},{1... | collective-permute-start | bytes 786440 | tf_op jit(solution)/shard_map/ppermute | solution.py:249
  71.1 5.0 %collective-permute-start.15 = (f32[4,4,1024]{2,1,0:T(4,128)S(1)}, f32[4,4,1024]{2,1,0:T(4,128)S(1)}, u32[]{:S(2)}, u32[]{:S(2)}) collective-permute-start(f32[4,4,1024]{2,1,0:T(4,128)S(1)} %get-tuple-element.40), channel_id=1, source_target_pairs={{0,1},{1,0},{2,3},{3,2},{4,5},{5,4},{6,7},{7,6},{8,9},{9,8},{10,11... | collective-permute-start | bytes 196616 | tf_op jit(solution)/shard_map/ppermute | solution.py:249
  72.5 5.8 %collective-permute-start.16 = (f32[4,4,1024]{2,1,0:T(4,128)S(1)}, f32[4,4,1024]{2,1,0:T(4,128)S(1)}, u32[]{:S(2)}, u32[]{:S(2)}) collective-permute-start(f32[4,4,1024]{2,1,0:T(4,128)S(1)} %get-tuple-element.41), channel_id=1, source_target_pairs={{0,2},{1,3},{2,0},{3,1},{4,6},{5,7},{6,4},{7,5},{8,10},{9,11},{10,... | collective-permute-start | bytes 196616 | tf_op jit(solution)/shard_map/ppermute | solution.py:249
  73.1 5.6 %collective-permute-start.17 = (f32[4,4,1024]{2,1,0:T(4,128)S(1)}, f32[4,4,1024]{2,1,0:T(4,128)S(1)}, u32[]{:S(2)}, u32[]{:S(2)}) collective-permute-start(f32[4,4,1024]{2,1,0:T(4,128)S(1)} %add_bitcast_fusion), channel_id=1, source_target_pairs={{0,3},{1,2},{2,1},{3,0},{4,7},{5,6},{6,5},{7,4},{8,11},{9,10},{10,... | collective-permute-start | bytes 196616 | tf_op jit(solution)/shard_map/ppermute | solution.py:249
  78.8 7.7 %collective-permute-start.18 = (f32[4,1024]{1,0:T(4,128)S(1)}, f32[4,1024]{1,0:T(4,128)S(1)}, u32[]{:S(2)}, u32[]{:S(2)}) collective-permute-start(f32[4,1024]{1,0:T(4,128)S(1)} %get-tuple-element.42), channel_id=1, source_target_pairs={{0,4},{1,5},{2,6},{3,7},{4,0},{5,1},{6,2},{7,3},{8,12},{9,13},{10,... | collective-permute-start | bytes 49160 | tf_op jit(solution)/shard_map/ppermute | solution.py:249
  79.9 6.6 %collective-permute-start.19 = (f32[4,1024]{1,0:T(4,128)S(1)}, f32[4,1024]{1,0:T(4,128)S(1)}, u32[]{:S(2)}, u32[]{:S(2)}) collective-permute-start(f32[4,1024]{1,0:T(4,128)S(1)} %get-tuple-element.44), channel_id=1, source_target_pairs={{0,8},{1,9},{2,10},{3,11},{4,12},{5,13},{6,14},{7,15},{8,0},{9,1},... | collective-permute-start | bytes 49160 | tf_op jit(solution)/shard_map/ppermute | solution.py:249
  82.2 9.4 %collective-permute-start.20 = (f32[4,1024]{1,0:T(4,128)S(1)}, f32[4,1024]{1,0:T(4,128)S(1)}, u32[]{:S(2)}, u32[]{:S(2)}) collective-permute-start(f32[4,1024]{1,0:T(4,128)S(1)} %get-tuple-element.43), channel_id=1, source_target_pairs={{0,12},{1,13},{2,14},{3,15},{4,8},{5,9},{6,10},{7,11},{8,4},{9,5},... | collective-permute-start | bytes 49160 | tf_op jit(solution)/shard_map/ppermute | solution.py:249
